TPU v7x, 128 devices: a whole 4x4x4 slice. The times are simulated.
128 devices in a mesh: band: 8 (over x, core), fft: 16 (over y, z).
Axes of the slice: x: 4, y: 4, z: 4, core: 2. Of those that a mesh axis runs over, the one named last changes fastest.
Arguments:
- orbitals: bfloat16 [16, 30720, 480], P('band', 'fft'), may hold values from -24 to 24
- potential: float32 [240, 57600], P('fft'), may hold values from -8 to 8
- stick_column: int32 [30720], replicated, may hold values from -1 to 57599, as said below
- column_slot: int32 [57600], replicated, may hold values from -1 to 30719, as said below
Outputs:
- applied_orbitals: bfloat16 [16, 30720, 480], P('band', 'fft')
- intersection: float32 [2, 16, 16], replicated
- hamiltonian: float32 [2, 16, 16], replicated
Inputs may be any that keep to these rules, and one draw needn't show every extreme that they name: `stick_column`: the live entries are the 24576 flat indices x 240 + y of a disk of columns around zero wrapped frequency, each once; the slots p * 1920 to (p + 1) * 1920 - 1 of fft index p hold its sticks first, then -1; counts differ between indices and some index has all 1920 slots live. column_slot[stick_column[g]] = g for every live slot g, and -1 at every other flat index.
All inputs are finite; a program needn't handle non-finite values.
Results may differ from a plain program's by a relative error of at most 0.011.
Values may be sent and summed in bfloat16 or wider, within the bound.
No kernel may reach another device: no remote copies, remote signals or barrier semaphores. Data moves between devices by JAX's collectives and lax.ppermute only.
A program may use at most 192 MiB of HBM per device.

v0:
```python
import math

import jax
import jax.numpy as jnp
from jax import lax
from jax.sharding import PartitionSpec as P

STICKS = 24576


def fourier_tables(length, direction):
    counter = jnp.arange(length, dtype=jnp.int32)
    phases = counter[:, None] * counter[None, :] % length
    angles = phases.astype(jnp.float32) * (2.0 * math.pi / length)
    factor = 1.0 / math.sqrt(length)
    cosine = jnp.cos(angles) * factor
    sine = jnp.sin(angles) * (factor * direction)
    upper_half = jnp.stack([cosine, sine], axis=1)
    lower_half = jnp.stack([-sine, cosine], axis=1)
    return jnp.stack([upper_half, lower_half], axis=0).astype(jnp.bfloat16)


def rotated(values):
    middle = values.shape[-1] // 2
    return jnp.concatenate([values[..., middle:], -values[..., :middle]], axis=-1)


def matrix_rows(left, right):
    return jnp.dot(left, right.T, preferred_element_type=jnp.float32)


def local(orbitals, potential, stick_column, column_slot):
    band_count, slots, doubled = orbitals.shape
    length = doubled // 2
    groups = lax.axis_size("fft")
    planes = potential.shape[0]
    forward = fourier_tables(length, 1.0)
    backward = fourier_tables(length, -1.0)
    z_forward = forward.reshape(doubled, doubled)
    z_backward = backward.reshape(doubled, doubled)
    live_all = (stick_column >= 0).astype(jnp.bfloat16)
    own_live = lax.dynamic_slice_in_dim(live_all, lax.axis_index("fft") * slots, slots)
    column_pick = jnp.maximum(stick_column, 0)
    slot_pick = jnp.maximum(column_slot, 0)
    filled = (column_slot >= 0)[:, None]
    field_xy = potential.reshape(planes, length, length).transpose(1, 2, 0)[:, :, None, None, :]
    masked = orbitals * own_live[None, :, None]
    zvalues = jnp.einsum(
        "bsk,kz->sbz", masked, z_forward, preferred_element_type=jnp.float32
    ).astype(jnp.bfloat16)
    outgoing = zvalues.reshape(slots, band_count, 2, groups, planes)
    incoming = lax.all_to_all(outgoing, "fft", split_axis=3, concat_axis=0, tiled=True)
    items = incoming.shape[1]
    rows_all = incoming.reshape(groups * slots, items * 2 * planes)
    placed = jnp.where(filled, jnp.take(rows_all, slot_pick, axis=0), jnp.zeros((), jnp.bfloat16))
    placed = placed.reshape(length, length, items, 2, planes)
    sectioned = jnp.einsum(
        "xkbcp,ckdy->xybdp", placed, forward, preferred_element_type=jnp.float32
    ).astype(jnp.bfloat16)
    spatial = jnp.einsum(
        "kybcp,ckdx->xybdp", sectioned, forward, preferred_element_type=jnp.float32
    )
    sectioned = (spatial * field_xy).astype(jnp.bfloat16)
    sectioned = jnp.einsum(
        "kybcp,ckdx->xybdp", sectioned, backward, preferred_element_type=jnp.float32
    ).astype(jnp.bfloat16)
    sectioned = jnp.einsum(
        "xkbcp,ckdy->xybdp", sectioned, backward, preferred_element_type=jnp.float32
    ).astype(jnp.bfloat16)
    flat_rows = sectioned.reshape(length * length, items * 2 * planes)
    picked = jnp.take(flat_rows, column_pick, axis=0) * live_all[:, None]
    returning = lax.all_to_all(
        picked.reshape(groups, slots, items, 2, planes),
        "fft",
        split_axis=0,
        concat_axis=4,
        tiled=True,
    )
    stick_values = returning.reshape(slots, band_count, doubled)
    applied = jnp.einsum(
        "sbk,kz->bsz", stick_values, z_backward, preferred_element_type=jnp.float32
    )
    applied = (applied * own_live.astype(jnp.float32)[None, :, None]).astype(jnp.bfloat16)
    scale = 1.0 / (2.0 * STICKS * length)
    full_bands, full_applied = (
        lax.all_to_all(masked, "band", split_axis=1, concat_axis=0, tiled=True),
        lax.all_to_all(applied, "band", split_axis=1, concat_axis=0, tiled=True),
    )
    every = full_bands.shape[0]
    left = full_bands.reshape(every, -1)
    products = jnp.stack(
        [
            matrix_rows(left, left),
            matrix_rows(left, rotated(full_bands).reshape(every, -1)),
            matrix_rows(left, full_applied.reshape(every, -1)),
            matrix_rows(left, rotated(full_applied).reshape(every, -1)),
        ]
    )
    totals = lax.psum(products, ("band", "fft"))
    intersection = totals[0:2] * scale
    hamiltonian = totals[2:4] * scale
    return (applied, intersection, hamiltonian)


def solution(mesh):
    return jax.shard_map(
        local,
        mesh=mesh,
        in_specs=(P("band", "fft", None), P("fft", None), P(), P()),
        out_specs=(P("band", "fft", None), P(), P()),
        check_vma=False,
    )
```

profile of v0, /device:TPU:0, one launch (start us, length us, event | category | flops | bytes accessed | tf_op | source)
XLA Modules:
  0.0 693.4 jit_solution(16220530700768839833)
XLA Ops:
  0.6 1.1 cosine_multiply_fusion
  1.7 1.0 fusion.46
  2.7 0.9 maximum_compare_fusion
  3.8 0.4 copy.134
  4.5 0.7 fusion.49
  5.2 2.4 broadcast_multiply_fusion
  7.6 1.9 copy-done.2
  9.4 2.1 convert_bitcast_fusion
  11.6 2.8 copy.135
  14.4 4.4 copy.136
  18.8 8.8 %all-to-all-start = ((bf16[1920,2,2,16,15]{0,1,4,2,3:T(2,128)(2,1)}), bf16[1920,2,2,16,15]{0,1,4,2,3:T(2,128)(2,1)}, u32[]{:S(2)}, u32[]{:S(2)}) async-start(bf16[1920,2,2,16,15]{0,1,4,2,3:T(2,128)(2,1)} %copy.136), calls=%async_computation | async-start | bytes 7372800 | tf_op jit(solution)/shard_map/all_to_all | solution.py:52
  27.6 1.0 negate_convert_fusion
  28.6 1.0 fusion.47
  29.5 0.7 mul.237
  30.8 6.3 reshape.174
  37.2 0.7 broadcast_in_dim.51
  38.0 0.9 fusion.48
  38.9 39.1 %all-to-all-done = bf16[1920,2,2,16,15]{0,1,4,2,3:T(2,128)(2,1)} async-done(((bf16[1920,2,2,16,15]{0,1,4,2,3:T(2,128)(2,1)}), bf16[1920,2,2,16,15]{0,1,4,2,3:T(2,128)(2,1)}, u32[]{:S(2)}, u32[]{:S(2)}) %all-to-all-start) | async-done | bytes 3686432 | tf_op jit(solution)/shard_map/all_to_all | solution.py:52
  78.1 2.5 copy.137
  80.8 2.8 copy.185
  83.6 8.4 %copy.138 = bf16[30720,60]{1,0:T(8,128)(2,1)} copy(bf16[30720,60]{0,1:T(8,128)(2,1)} %bitcast.168) | data formatting | bytes 7372800 | tf_op jit(solution)/shard_map/reshape | solution.py:54
  92.1 110.6 %gather_fusion = bf16[57600,60]{1,0:T(8,128)(2,1)} fusion(bf16[30720,60]{1,0:T(8,128)(2,1)} %copy.138, s32[58368]{0:T(1024)S(1)} %pad_clamp_fusion), kind=kCustom, calls=%fused_computation | custom fusion | bytes 14054400 | tf_op jit(solution)/shard_map/jit(_take)/gather | solution.py:55
  202.7 15.4 %copy.139 = bf16[57600,60]{0,1:T(8,128)(2,1)} copy(bf16[57600,60]{1,0:T(8,128)(2,1)} %gather_fusion) | data formatting | bytes 13824000 | tf_op jit(solution)/shard_map/jit(_take)/gather | solution.py:55
  218.0 18.9 %gather.13 = bf16[240,240,2,2,15]{1,0,4,3,2:T(8,128)(2,1)} reshape(bf16[57600,60]{0,1:T(8,128)(2,1)} %copy.139) | data formatting | bytes 13824000 | tf_op jit(solution)/shard_map/jit(_take)/gather | solution.py:55
  236.9 13.2 %fusion.5 = bf16[240,240,2,2,15,1]{1,0,4,2,3,5:T(8,128)(2,1)} fusion(f32[240,240,15]{1,0,2:T(8,128)} %bitcast.174, bf16[1,240,2,240]{1,3,0,2:T(8,128)(2,1)S(1)} %get-tuple-element.20, bf16[1,240,2,240]{1,3,0,2:T(8,128)(2,1)S(1)} %get-tuple-element.19, bf16[240,240,2,2,15]{1,0,4,3,2:T(8,128)(2,1)} %gather.13, pred[240,240]{1,0:T(8,128)(4,1)S(1)} %broadcast_in_dim.55, ...), kind=kOutput, calls=%fused_computation.10 | convolution fusion | flops 6654643200 | bytes 17856000 | tf_op jit(solution)/shard_map/kybcp,ckdx->xybdp/dot_general | solution.py:60
  250.1 12.0 %fusion.4 = bf16[240,240,2,2,15]{0,1,4,2,3:T(8,128)(2,1)} fusion(bf16[2,240,2,240,1,1]{1,3,2,0,5,4:T(8,128)(2,1)S(1)} %get-tuple-element.13, bf16[240,240,2,2,15,1]{1,0,4,2,3,5:T(8,128)(2,1)} %fusion.5), kind=kOutput, calls=%fused_computation.9 | convolution fusion | flops 6642432000 | bytes 14284800 | tf_op jit(solution)/shard_map/xkbcp,ckdy->xybdp/dot_general | solution.py:67
  262.0 10.3 %copy.145 = bf16[240,240,2,2,15]{1,0,4,3,2:T(8,128)(2,1)} copy(bf16[240,240,2,2,15]{0,1,4,2,3:T(8,128)(2,1)} %fusion.4) | data formatting | bytes 13824000 | tf_op jit(solution)/shard_map/convert_element_type | solution.py:69
  272.3 15.9 %reshape.175 = bf16[57600,60]{0,1:T(8,128)(2,1)} reshape(bf16[240,240,2,2,15]{1,0,4,3,2:T(8,128)(2,1)} %copy.145) | data formatting | bytes 13824000 | tf_op jit(solution)/shard_map/reshape | solution.py:70
  288.1 14.8 %copy.146 = bf16[57600,60]{1,0:T(8,128)(2,1)} copy(bf16[57600,60]{0,1:T(8,128)(2,1)} %reshape.175) | data formatting | bytes 13824000 | tf_op jit(solution)/shard_map/reshape | solution.py:70
  302.9 110.4 %gather_fusion.1 = bf16[30720,60]{1,0:T(8,128)(2,1)} fusion(bf16[57600,60]{1,0:T(8,128)(2,1)} %copy.146, s32[30720]{0:T(1024)S(1)} %maximum_clamp_fusion), kind=kCustom, calls=%fused_computation.1 | custom fusion | bytes 7495680 | tf_op jit(solution)/shard_map/jit(_take)/gather | solution.py:71
  413.3 8.6 %copy.147 = bf16[30720,60]{0,1:T(8,128)(2,1)} copy(bf16[30720,60]{1,0:T(8,128)(2,1)} %gather_fusion.1) | data formatting | bytes 7372800 | tf_op jit(solution)/shard_map/jit(_take)/gather | solution.py:71
  421.9 2.6 copy.186
  424.9 0.5 copy-done.7
  425.4 0.5 select_multiply_fusion
  425.9 4.7 copy.148
  430.5 11.8 %all-to-all-start.1 = ((bf16[16,1920,2,2,15]{1,3,4,2,0:T(2,128)(2,1)}), bf16[16,1920,2,2,15]{1,3,4,2,0:T(2,128)(2,1)}, u32[]{:S(2)}, u32[]{:S(2)}) async-start(bf16[16,1920,2,2,15]{1,3,4,2,0:T(2,128)(2,1)} %copy.148), calls=%async_computation.1 | async-start | bytes 7372800 | tf_op jit(solution)/shard_map/all_to_all | solution.py:72
  442.4 10.6 %copy.152 = bf16[2,1920,480]{2,0,1:T(2,128)(2,1)} copy(bf16[2,1920,480]{1,2,0:T(8,128)(2,1)} %copy-done.2) | data formatting | bytes 7372800 | tf_op jit(solution)/shard_map/mul | solution.py:47
  453.0 37.7 %all-to-all-done.1 = bf16[16,1920,2,2,15]{1,3,4,2,0:T(2,128)(2,1)} async-done(((bf16[16,1920,2,2,15]{1,3,4,2,0:T(2,128)(2,1)}), bf16[16,1920,2,2,15]{1,3,4,2,0:T(2,128)(2,1)}, u32[]{:S(2)}, u32[]{:S(2)}) %all-to-all-start.1) | async-done | bytes 3686432 | tf_op jit(solution)/shard_map/all_to_all | solution.py:72
  490.7 4.8 all-to-all-start.2
  495.5 0.4 copy.132
  496.3 4.9 copy.149
  501.2 4.0 fusion.26
  505.1 10.6 %copy.156 = bf16[2,1920,480]{2,0,1:T(2,128)(2,1)} copy(bf16[2,1920,480]{1,2,0:T(8,128)(2,1)} %fusion.26) | data formatting | bytes 7372800 | tf_op jit(solution)/shard_map/convert_element_type | solution.py:83
  515.7 26.6 %all-to-all-done.2 = bf16[2,1920,480]{2,0,1:T(2,128)(2,1)} async-done(((bf16[2,1920,480]{2,0,1:T(2,128)(2,1)}), bf16[2,1920,480]{2,0,1:T(2,128)(2,1)}, u32[]{:S(2)}, u32[]{:S(2)}) %all-to-all-start.2) | async-done | bytes 3686432 | tf_op jit(solution)/shard_map/all_to_all | solution.py:86
  542.4 5.0 all-to-all-start.3
  547.4 4.8 copy.216
  552.2 9.0 %reshape.177 = bf16[16,115200]{1,0:T(8,128)(2,1)} reshape(bf16[8,2,240,480]{3,2,1,0:T(8,128)(2,1)} %bitcast.165) | data formatting | bytes 7372800 | tf_op jit(solution)/shard_map/reshape | solution.py:90
  561.1 3.1 fusion.50
  564.3 3.5 pad_maximum_fusion
  567.8 9.1 %reshape.178 = bf16[16,115200]{1,0:T(8,128)(2,1)} reshape(bf16[16,240,480]{2,1,0:T(8,128)(2,1)} %pad_maximum_fusion) | data formatting | bytes 7372800 | tf_op jit(solution)/shard_map/reshape | solution.py:94
  576.9 4.8 convolution_bitcast_fusion.3
  581.7 0.5 copy-done.3
  582.2 1.5 convolution_bitcast_fusion.2
  583.7 10.5 %all-to-all-done.3 = bf16[2,1920,480]{2,0,1:T(2,128)(2,1)} async-done(((bf16[2,1920,480]{2,0,1:T(2,128)(2,1)}), bf16[2,1920,480]{2,0,1:T(2,128)(2,1)}, u32[]{:S(2)}, u32[]{:S(2)}) %all-to-all-start.3) | async-done | bytes 3686432 | tf_op jit(solution)/shard_map/all_to_all | solution.py:87
  594.2 2.9 copy.215
  597.1 0.7 fusion.52
  597.8 1.2 copy-done.1
  599.0 3.5 pad_maximum_fusion.1
  602.5 8.9 %reshape.180 = bf16[16,115200]{1,0:T(8,128)(2,1)} reshape(bf16[16,240,480]{2,1,0:T(8,128)(2,1)} %pad_maximum_fusion.1) | data formatting | bytes 7372800 | tf_op jit(solution)/shard_map/reshape | solution.py:96
  611.4 4.7 convolution_bitcast_fusion
  616.1 9.0 %reshape.179 = bf16[16,115200]{1,0:T(8,128)(2,1)} reshape(bf16[8,2,240,480]{3,2,1,0:T(8,128)(2,1)} %bitcast.164) | data formatting | bytes 7372800 | tf_op jit(solution)/shard_map/reshape | solution.py:95
  625.1 4.7 convolution_bitcast_fusion.1
  629.8 62.8 %psum.7 = f32[4,16,16]{2,1,0:T(8,128)S(1)} all-reduce(f32[4,16,16]{2,1,0:T(8,128)S(1)} %pad_maximum_fusion.3), channel_id=1, replica_groups=mesh['band'=8,'fft'=16] {'band','fft'}, use_global_device_ids=true, to_apply=%region_0.1 | all-reduce | flops 1024 | bytes 8192 | tf_op jit(solution)/shard_map/psum | solution.py:99
  692.6 0.6 slice_multiply_fusion
  (30 shorter events, 2.1 us)
Async XLA Ops:
  7.6 1.9 copy-start.2
  18.8 11.4 %copy-start.5 = (s32[57600]{0:T(1024)S(1)}, s32[57600]{0:T(1024)}, u32[]{:S(2)}) copy-start(s32[57600]{0:T(1024)} %param.7) | copy-start | bytes 691204
  18.8 59.3 %all-to-all-start = ((bf16[1920,2,2,16,15]{0,1,4,2,3:T(2,128)(2,1)}), bf16[1920,2,2,16,15]{0,1,4,2,3:T(2,128)(2,1)}, u32[]{:S(2)}, u32[]{:S(2)}) async-start(bf16[1920,2,2,16,15]{0,1,4,2,3:T(2,128)(2,1)} %copy.136), calls=%async_computation | async-start | bytes 7372800 | tf_op jit(solution)/shard_map/all_to_all | solution.py:52
  30.8 8.0 %copy-start.6 = (s32[30720]{0:T(1024)S(1)}, s32[30720]{0:T(1024)}, u32[]{:S(2)}) copy-start(s32[30720]{0:T(1024)} %param.6) | copy-start | bytes 368644
  424.6 0.8 copy-start.7
  424.6 0.8 copy-start.8
  430.5 60.1 %all-to-all-start.1 = ((bf16[16,1920,2,2,15]{1,3,4,2,0:T(2,128)(2,1)}), bf16[16,1920,2,2,15]{1,3,4,2,0:T(2,128)(2,1)}, u32[]{:S(2)}, u32[]{:S(2)}) async-start(bf16[16,1920,2,2,15]{1,3,4,2,0:T(2,128)(2,1)} %copy.148), calls=%async_computation.1 | async-start | bytes 7372800 | tf_op jit(solution)/shard_map/all_to_all | solution.py:72
  453.0 42.5 %copy-start.4 = (bf16[2,240,2,240]{1,3,2,0:T(8,128)(2,1)S(1)}, bf16[2,240,2,240]{1,3,2,0:T(8,128)(2,1)}, u32[]{:S(2)}) copy-start(bf16[2,240,2,240]{1,3,2,0:T(8,128)(2,1)} %get-tuple-element.14) | copy-start | bytes 1382404
  490.7 51.7 %all-to-all-start.2 = ((bf16[2,1920,480]{2,0,1:T(2,128)(2,1)}), bf16[2,1920,480]{2,0,1:T(2,128)(2,1)}, u32[]{:S(2)}, u32[]{:S(2)}) async-start(bf16[2,1920,480]{2,0,1:T(2,128)(2,1)} %copy.152), calls=%async_computation.2 | async-start | bytes 7864320 | tf_op jit(solution)/shard_map/all_to_all | solution.py:86
  496.3 4.9 copy-start.9
  542.4 51.9 %all-to-all-start.3 = ((bf16[2,1920,480]{2,0,1:T(2,128)(2,1)}), bf16[2,1920,480]{2,0,1:T(2,128)(2,1)}, u32[]{:S(2)}, u32[]{:S(2)}) async-start(bf16[2,1920,480]{2,0,1:T(2,128)(2,1)} %copy.156), calls=%async_computation.3 | async-start | bytes 7864320 | tf_op jit(solution)/shard_map/all_to_all | solution.py:87
  576.9 4.8 copy-start
  576.9 5.3 copy-start.3
  597.1 1.9 copy-start.1
where the time goes:
time: 704 us; the launch traced here: 693 us
  local copies, waits for them, and re-layouts  417 us (59%)
  waiting for transfers between devices  114 us (16%)
  blocking collectives  62.8 us (9%)
  matrix products  46.9 us (7%)
  starting transfers between devices  30.4 us (4%)
  other arithmetic  21.3 us (3%)
    gather x3, local copies, waits for them, and re-layouts, local(): jnp.take(rows_all, slot_pick, axis=0)  145 us
    gather x2, local copies, waits for them, and re-layouts, local(): picked = jnp.take(flat_rows, column_pick, axis=0) * live_all[:, None]  119 us
    psum x1, blocking collectives, local(): totals = lax.psum(products, ('band', 'fft'))  62.8 us
    all_to_all x1, waiting for transfers between devices, local(): lax.all_to_all(outgoing, 'fft', split_axis=3, concat_axis=0, tiled=True)  39.1 us
    all_to_all x1, waiting for transfers between devices, local(): lax.all_to_all(picked.reshape(groups, slots, items, 2, planes), 'fft', sp...  37.7 us
    reshape x2, local copies, waits for them, and re-layouts, local(): flat_rows = sectioned.reshape(length * length, items * 2 * planes)  30.7 us
    all_to_all x1, waiting for transfers between devices, local(): lax.all_to_all(masked, 'band', split_axis=1, concat_axis=0, tiled=True)  26.6 us
    dot_general x4, matrix products, matrix_rows(): return jnp.dot(left, right.T, preferred_element_type=jnp.float32)  15.7 us
  transfers between devices with their start and end apart: 4, of which 4 were waited for; matrix products, arithmetic and copies ran while one was open for 11% of the time, Pallas kernels for 0%

commit v1 on v0

v1 whole, which is shorter than its diff:
```python
import functools
import math

import jax
import jax.numpy as jnp
import ml_dtypes
import numpy as np
from jax import lax
from jax.experimental import pallas as pl
from jax.experimental.pallas import tpu as pltpu
from jax.sharding import PartitionSpec as P

STICKS = 24576
GRID = 240
SLOTS = 1920
GROUPS = 16
PLANES = 15
ZPAD = 16
BOX = 192
HALF = BOX // 2
PAIRS = GRID // 2
ROWS = BOX * BOX
BLOCK = 384
MIB = 1 << 20


def trig():
    counter = np.arange(GRID, dtype=np.int32)
    phases = counter[:, None] * counter[None, :] % GRID
    angles = phases.astype(np.float32) * np.float32(2.0 * math.pi / GRID)
    factor = np.float32(1.0 / math.sqrt(GRID))
    cosine = (np.cos(angles) * factor).astype(ml_dtypes.bfloat16)
    sine = (np.sin(angles) * factor).astype(ml_dtypes.bfloat16)
    return cosine, sine


def tables():
    cosine, sine = trig()
    box = np.arange(BOX) - HALF
    box = np.where(box < 0, box + GRID, box)
    z_forward = np.zeros((GROUPS, 2, ZPAD, 2, GRID), ml_dtypes.bfloat16)
    cos_z = cosine.reshape(GROUPS, PLANES, GRID)
    sin_z = sine.reshape(GROUPS, PLANES, GRID)
    z_forward[:, 0, :PLANES, 0] = cos_z
    z_forward[:, 0, :PLANES, 1] = -sin_z
    z_forward[:, 1, :PLANES, 0] = sin_z
    z_forward[:, 1, :PLANES, 1] = cos_z
    z_forward = z_forward.reshape(GROUPS * 2 * ZPAD, 2 * GRID)
    z_backward = np.ascontiguousarray(z_forward.T)
    cos_box, sin_box = cosine[:, box], sine[:, box]
    forward = np.concatenate([cos_box, sin_box], axis=1)
    backward = np.concatenate([cos_box.T, -sin_box.T], axis=1)
    return z_forward, z_backward, forward, backward


def z_forward_kernel(orbit_ref, live_ref, table_ref, wire_ref, share_ref):
    masked = (orbit_ref[0].astype(jnp.float32) * live_ref[...]).astype(jnp.bfloat16)
    values = jnp.dot(table_ref[...], masked, preferred_element_type=jnp.float32).astype(jnp.bfloat16)
    lanes = values.shape[-1]
    wire_ref[...] = values.reshape(GROUPS, 2, 1, ZPAD, lanes)
    for c in range(2):
        for q in range(15):
            share_ref[q // 2, q % 2, c, 0] = masked[c * GRID + q * 16 : c * GRID + q * 16 + 16]
        share_ref[7, 1, c, 0] = jnp.zeros((16, lanes), jnp.bfloat16)


def z_forward_call(orbits, live, table):
    lanes = BLOCK
    return pl.pallas_call(
        z_forward_kernel,
        grid=(2, SLOTS // lanes),
        in_specs=[
            pl.BlockSpec((1, 2 * GRID, lanes), lambda b, t: (b, 0, t)),
            pl.BlockSpec((1, lanes), lambda b, t: (0, t)),
            pl.BlockSpec((512, 2 * GRID), lambda b, t: (0, 0)),
        ],
        out_specs=[
            pl.BlockSpec((GROUPS, 2, 1, ZPAD, lanes), lambda b, t: (0, 0, b, 0, t)),
            pl.BlockSpec((8, 2, 2, 1, 16, lanes), lambda b, t: (0, 0, 0, b, 0, t)),
        ],
        out_shape=[
            jax.ShapeDtypeStruct((GROUPS, 2, 2, ZPAD, SLOTS), jnp.bfloat16),
            jax.ShapeDtypeStruct((8, 2, 2, 2, 16, SLOTS), jnp.bfloat16),
        ],
        compiler_params=pltpu.CompilerParams(vmem_limit_bytes=40 * MIB),
        cost_estimate=pl.CostEstimate(flops=1_800_000_000, bytes_accessed=12_000_000, transcendentals=0),
        name="z_forward",
    )(orbits, live, table)


def z_backward_kernel(wire_ref, live_ref, table_ref, out_ref):
    lanes = wire_ref.shape[-1]
    values = wire_ref[...].reshape(512, lanes)
    applied = jnp.dot(table_ref[...], values, preferred_element_type=jnp.float32)
    out_ref[0] = (applied * live_ref[...]).astype(jnp.bfloat16)


def z_backward_call(wire, live, table):
    lanes = BLOCK
    return pl.pallas_call(
        z_backward_kernel,
        grid=(2, SLOTS // lanes),
        in_specs=[
            pl.BlockSpec((GROUPS, 2, 1, ZPAD, lanes), lambda b, t: (0, 0, b, 0, t)),
            pl.BlockSpec((1, lanes), lambda b, t: (0, t)),
            pl.BlockSpec((2 * GRID, 512), lambda b, t: (0, 0)),
        ],
        out_specs=pl.BlockSpec((1, 2 * GRID, lanes), lambda b, t: (b, 0, t)),
        out_shape=jax.ShapeDtypeStruct((2, 2 * GRID, SLOTS), jnp.bfloat16),
        compiler_params=pltpu.CompilerParams(vmem_limit_bytes=40 * MIB),
        cost_estimate=pl.CostEstimate(flops=1_800_000_000, bytes_accessed=8_000_000, transcendentals=0),
        name="z_backward",
    )(wire, live, table)


def gram_kernel(left_ref, right_ref, out_ref, total):
    step = pl.program_id(0) * pl.num_programs(1) + pl.program_id(1)
    lanes = left_ref.shape[-1]
    left = left_ref[...].reshape(512, lanes)
    right = right_ref[...].reshape(512, lanes)
    product = lax.dot_general(left, right, (((1,), (1,)), ((), ())), preferred_element_type=jnp.float32)

    @pl.when(step == 0)
    def _():
        total[...] = product

    @pl.when(step > 0)
    def _():
        total[...] += product

    @pl.when(step == pl.num_programs(0) * pl.num_programs(1) - 1)
    def _():
        row = lax.broadcasted_iota(jnp.int32, (512, 512), 0)
        column = lax.broadcasted_iota(jnp.int32, (512, 512), 1)
        diagonal = jnp.where(row % 16 == column % 16, total[...], 0.0)
        pick_row = lax.broadcasted_iota(jnp.int32, (32, 512), 0)
        pick_column = lax.broadcasted_iota(jnp.int32, (32, 512), 1)
        pick = jnp.where(pick_column // 16 == pick_row, 1.0, 0.0)
        by_row = jnp.dot(pick, diagonal, preferred_element_type=jnp.float32, precision=lax.Precision.HIGHEST)
        out_ref[...] = lax.dot_general(
            by_row,
            pick,
            (((1,), (1,)), ((), ())),
            preferred_element_type=jnp.float32,
            precision=lax.Precision.HIGHEST,
        )


def gram_call(left, right, name):
    lanes = 640
    spec = pl.BlockSpec((8, 1, 2, 2, 16, lanes), lambda g, t: (0, g, 0, 0, 0, t))
    return pl.pallas_call(
        gram_kernel,
        grid=(2, SLOTS // lanes),
        in_specs=[spec, spec],
        out_specs=pl.BlockSpec((32, 32), lambda g, t: (0, 0)),
        out_shape=jax.ShapeDtypeStruct((32, 32), jnp.float32),
        scratch_shapes=[pltpu.VMEM((512, 512), jnp.float32)],
        compiler_params=pltpu.CompilerParams(vmem_limit_bytes=40 * MIB),
        cost_estimate=pl.CostEstimate(flops=2_000_000_000, bytes_accessed=8_000_000, transcendentals=0),
        name=name,
    )(left, right)


def matrices(product):
    parts = product.reshape(8, 2, 2, 8, 2, 2)
    first = parts[:, 0, :, :, 0, :] + parts[:, 1, :, :, 1, :]
    second = parts[:, 0, :, :, 1, :] - parts[:, 1, :, :, 0, :]
    return jnp.stack([first.reshape(16, 16), second.reshape(16, 16)])


def plane_kernel(
    place_ref, count_ref, wire_ref, field_ref, forward_ref, backward_ref, out_ref, grid_ref, mid_ref, stage_a, stage_b
):
    step = pl.program_id(0)
    lane = lax.broadcasted_iota(jnp.int32, (1, 128), 1)
    low = lane % 64 < 32
    sign = jnp.where(lane < 64, -1.0, 1.0)

    def turned(values):
        return pltpu.roll(values, 64, 1) * sign

    def doubled(values):
        return jnp.concatenate([values, turned(values)], axis=0).astype(jnp.bfloat16)

    def exchange(first, second):
        return (
            jnp.where(low, first, pltpu.roll(second, 32, 1)),
            jnp.where(low, pltpu.roll(first, 96, 1), second),
        )

    @pl.when(step == 0)
    def _():
        def clear(i, carry):
            grid_ref[pl.ds(pl.multiple_of(i * 512, 512), 512), :] = jnp.zeros((512, 128), jnp.float32)
            return carry

        lax.fori_loop(0, ROWS // 512, clear, 0)
        eye_row = lax.broadcasted_iota(jnp.int32, (128, 128), 0)
        eye_column = lax.broadcasted_iota(jnp.int32, (128, 128), 1)
        eye = jnp.where(eye_row == eye_column, 1.0, 0.0).astype(jnp.bfloat16)

        def group(p, carry):
            def scatter(t, inner):
                base = pl.multiple_of(t * 128, 128)
                block = wire_ref[p, :, pl.ds(base, 128)]
                twice = jnp.concatenate([block[0:32], block[0:32], block[32:64], block[32:64]], axis=0)
                stage_a[...] = lax.dot_general(
                    eye, twice, (((1,), (1,)), ((), ())), preferred_element_type=jnp.float32
                )
                first = p * SLOTS + base
                for u in range(128):
                    grid_ref[pl.ds(place_ref[first + u], 1), :] = stage_a[u : u + 1, :]
                return inner

            return lax.fori_loop(0, count_ref[p], scatter, carry)

        lax.fori_loop(0, GROUPS, group, 0)

        def x_forward(i, carry):
            parts = []
            for j in range(4):
                k = i * 4 + j
                first = grid_ref[pl.ds(pl.multiple_of(k * BOX, BOX), BOX), :]
                second = grid_ref[pl.ds(pl.multiple_of((k + HALF) * BOX, BOX), BOX), :]
                parts.append(doubled(jnp.where(low, first, second)))
            result = jnp.dot(forward_ref[...], jnp.concatenate(parts, axis=1), preferred_element_type=jnp.float32)
            for j in range(4):
                k = i * 4 + j
                part = result[:, j * 128 : (j + 1) * 128]
                mid_ref[pl.ds(k, PAIRS, stride=BOX), :] = part[:PAIRS]
                mid_ref[pl.ds(k + HALF, PAIRS, stride=BOX), :] = part[PAIRS:]
            return carry

        lax.fori_loop(0, HALF // 4, x_forward, 0)

    def y_steps(i, carry):
        parts = []
        for j in range(4):
            pair = step * 8 + i * 4 + j
            base = pl.multiple_of(pair * BOX, BOX)
            first = mid_ref[pl.ds(base, HALF), :]
            second = mid_ref[pl.ds(base + HALF, HALF), :]
            even, odd = exchange(first, second)
            parts.append(doubled(jnp.concatenate([even, odd], axis=0)))
        spatial = jnp.dot(forward_ref[...], jnp.concatenate(parts, axis=1), preferred_element_type=jnp.float32)
        parts = []
        for j in range(4):
            parts.append(doubled(spatial[:, j * 128 : (j + 1) * 128] * field_ref[i * 4 + j]))
        result = jnp.dot(backward_ref[...], jnp.concatenate(parts, axis=1), preferred_element_type=jnp.float32)
        for j in range(4):
            pair = step * 8 + i * 4 + j
            mid_ref[pl.ds(pl.multiple_of(pair * BOX, BOX), BOX), :] = result[:, j * 128 : (j + 1) * 128]
        return carry

    lax.fori_loop(0, 2, y_steps, 0)

    @pl.when(step == pl.num_programs(0) - 1)
    def _():
        def x_backward(i, carry):
            parts = []
            for j in range(4):
                k = i * 4 + j
                first = mid_ref[pl.ds(k, PAIRS, stride=BOX), :]
                second = mid_ref[pl.ds(k + HALF, PAIRS, stride=BOX), :]
                even, odd = exchange(first, second)
                parts.append(doubled(jnp.concatenate([even, odd], axis=0)))
            result = jnp.dot(backward_ref[...], jnp.concatenate(parts, axis=1), preferred_element_type=jnp.float32)
            for j in range(4):
                k = i * 4 + j
                part = result[:, j * 128 : (j + 1) * 128]
                grid_ref[pl.ds(pl.multiple_of(k * BOX, BOX), BOX), :] = jnp.where(low, part, pltpu.roll(part, 32, 1))
                grid_ref[pl.ds(pl.multiple_of((k + HALF) * BOX, BOX), BOX), :] = jnp.where(
                    low, pltpu.roll(part, 96, 1), part
                )
            return carry

        lax.fori_loop(0, HALF // 4, x_backward, 0)
        select_row = lax.broadcasted_iota(jnp.int32, (64, 128), 0)
        select_column = lax.broadcasted_iota(jnp.int32, (64, 128), 1)
        select = jnp.where(select_column == select_row // 32 * 64 + select_row % 32, 1.0, 0.0).astype(jnp.bfloat16)

        def group(p, carry):
            def pick(t, inner):
                base = pl.multiple_of(t * 128, 128)
                first = p * SLOTS + base
                for u in range(128):
                    stage_b[u : u + 1, :] = grid_ref[pl.ds(place_ref[first + u], 1), :]
                out_ref[p, :, pl.ds(base, 128)] = lax.dot_general(
                    select,
                    stage_b[...].astype(jnp.bfloat16),
                    (((1,), (1,)), ((), ())),
                    preferred_element_type=jnp.float32,
                ).astype(jnp.bfloat16)
                return inner

            lax.fori_loop(0, count_ref[p], pick, carry)

            def blank(t, inner):
                out_ref[p, :, pl.ds(pl.multiple_of(t * 128, 128), 128)] = jnp.zeros((64, 128), jnp.bfloat16)
                return inner

            return lax.fori_loop(count_ref[p], SLOTS // 128, blank, carry)

        lax.fori_loop(0, GROUPS, group, 0)


def plane_call(place, count, wire, field, forward, backward):
    whole = lambda shape: pl.BlockSpec(shape, lambda i: (0,) * len(shape), pipeline_mode=pl.Buffered(1))
    return pl.pallas_call(
        plane_kernel,
        grid=(PAIRS // 8,),
        in_specs=[
            pl.BlockSpec(memory_space=pltpu.SMEM),
            pl.BlockSpec(memory_space=pltpu.SMEM),
            whole((GROUPS, 64, SLOTS)),
            pl.BlockSpec((8, GRID, 128), lambda i: (i, 0, 0)),
            whole((GRID, 2 * BOX)),
            whole((BOX, 2 * GRID)),
        ],
        out_specs=whole((GROUPS, 64, SLOTS)),
        out_shape=jax.ShapeDtypeStruct((GROUPS, 64, SLOTS), jnp.bfloat16),
        scratch_shapes=[
            pltpu.VMEM((ROWS + 8, 128), jnp.float32),
            pltpu.VMEM((PAIRS * BOX, 128), jnp.float32),
            pltpu.VMEM((128, 128), jnp.float32),
            pltpu.VMEM((128, 128), jnp.float32),
        ],
        compiler_params=pltpu.CompilerParams(vmem_limit_bytes=56 * MIB),
        cost_estimate=pl.CostEstimate(flops=13_000_000_000, bytes_accessed=24_000_000, transcendentals=0),
        name="planes",
    )(place, count, wire, field, forward, backward)


def local(orbitals, potential, stick_column, column_slot):
    z_forward, z_backward, forward, backward = (jnp.asarray(table) for table in tables())
    live_all = stick_column >= 0
    own = lax.dynamic_slice_in_dim(stick_column, lax.axis_index("fft") * SLOTS, SLOTS)
    live = (own >= 0).astype(jnp.float32)[None, :]
    column_x, column_y = stick_column // GRID, stick_column % GRID
    box_x = jnp.where(column_x < GRID // 2, column_x + HALF, column_x - (GRID - HALF))
    box_y = jnp.where(column_y < GRID // 2, column_y + HALF, column_y - (GRID - HALF))
    place = jnp.where(live_all, box_y * BOX + box_x, ROWS)
    count = (jnp.sum(live_all.reshape(GROUPS, SLOTS).astype(jnp.int32), axis=1) + 127) // 128
    field = jnp.pad(potential.reshape(PLANES, 2, PAIRS, GRID), ((0, 1), (0, 0), (0, 0), (0, 0)))
    field = field.transpose(2, 3, 1, 0)[:, :, None, :, None, :]
    field = jnp.broadcast_to(field, (PAIRS, GRID, 2, 2, 2, ZPAD)).reshape(PAIRS, GRID, 128)

    wire, share = z_forward_call(orbitals.transpose(0, 2, 1), live, z_forward)
    wire = wire.reshape(GROUPS, 64, SLOTS)
    share = share.reshape(8, 128, SLOTS)
    incoming = lax.all_to_all(wire, "fft", split_axis=0, concat_axis=0, tiled=True)
    share = lax.all_to_all(share, "band", split_axis=0, concat_axis=0, tiled=True)
    share = share.reshape(8, 2, 2, 2, 16, SLOTS)
    product_s = gram_call(share, share, "gram_s")
    outgoing = plane_call(place, count, incoming, field, forward, backward)
    left = lax.all_to_all(incoming.reshape(8, 128, SLOTS), "band", split_axis=0, concat_axis=0, tiled=True)
    right = lax.all_to_all(outgoing.reshape(8, 128, SLOTS), "band", split_axis=0, concat_axis=0, tiled=True)
    returned = lax.all_to_all(outgoing, "fft", split_axis=0, concat_axis=0, tiled=True)
    product_h = gram_call(
        left.reshape(8, 2, 2, 2, 16, SLOTS), right.reshape(8, 2, 2, 2, 16, SLOTS), "gram_h"
    )
    applied = z_backward_call(returned.reshape(GROUPS, 2, 2, ZPAD, SLOTS), live, z_backward)
    products = lax.psum(jnp.concatenate([matrices(product_s), matrices(product_h)]), ("band", "fft"))
    products = products * (1.0 / (2.0 * STICKS * GRID))
    return (applied.transpose(0, 2, 1), products[0:2], products[2:4])


def solution(mesh):
    return jax.shard_map(
        local,
        mesh=mesh,
        in_specs=(P("band", "fft", None), P("fft", None), P(), P()),
        out_specs=(P("band", "fft", None), P(), P()),
        check_vma=False,
    )
```

time: 704 us -> 523 us (0.74); the launches traced: 693 us -> 521 us
  local copies, waits for them, and re-layouts: 417 us -> 47.2 us
  Pallas kernels: 0 us -> 198 us
  blocking collectives: 62.8 us -> 198 us
  waiting for transfers between devices: 114 us -> 51 us
  matrix products: 46.9 us -> 0 us
  other arithmetic: 21.3 us -> 3.16 us
  starting transfers between devices: 30.4 us -> 23.3 us
    gather x5 -> x0, local copies, waits for them, and re-layouts: 264 us -> none  [the longest x3 145 us: local(): jnp.take(rows_all, slot_pick, axis=0)]
    pallas_call x0 -> x5, Pallas kernels: none -> 198 us  [the longest x1 169 us: plane_call(): pl.pallas_call(plane_kernel, grid=(PAIRS // 8,), in_specs=[pl.BlockSpec(m...]
    all_to_all x0 -> x2, blocking collectives: none -> 104 us  [the longest x1 52.3 us: local(): lax.all_to_all(outgoing.reshape(8, 128, SLOTS), 'band', split_axis=0, con...]
    reshape x9 -> x4, local copies, waits for them, and re-layouts: 85.7 us -> 22.6 us  [the longest x1 15.4 us: local(): jnp.broadcast_to(field, (PAIRS, GRID, 2, 2, 2, ZPAD))]
    all_to_all x4 -> x3, waiting for transfers between devices: 114 us -> 51 us  [the longest x1 51 us: local(): lax.all_to_all(wire, 'fft', split_axis=0, concat_axis=0, tiled=True)]
    dot_general x8 -> x0, matrix products: 46.9 us -> none  [the longest x4 15.7 us: matrix_rows(): return jnp.dot(left, right.T, preferred_element_type=jnp.float32)]
    psum x1, blocking collectives: 62.8 us -> 93.4 us  [local(): lax.psum(jnp.concatenate([matrices(product_s), matrices(product_h)]), ('b...]
    convert_element_type x6 -> x1, local copies, waits for them, and re-layouts: 24.6 us -> 0.02 us  [local(): live_all.reshape(GROUPS, SLOTS).astype(jnp.int32)]
  transfers between devices with their start and end apart: 4 -> 3, of which waited for: 4 -> 1; matrix products, arithmetic and copies ran while one was open for 11% -> 7% of each run, Pallas kernels for 0% -> 35%
where the time goes in v1:
time: 523 us; the launch traced here: 521 us
  Pallas kernels  198 us (38%)
  blocking collectives  198 us (38%)
  waiting for transfers between devices  51 us (10%)
  local copies, waits for them, and re-layouts  47.2 us (9%)
  starting transfers between devices  23.3 us (4%)
    pallas_call x1, Pallas kernels, plane_call(): pl.pallas_call(plane_kernel, grid=(PAIRS // 8,), in_specs=[pl.BlockSpec(m...  169 us
    psum x1, blocking collectives, local(): lax.psum(jnp.concatenate([matrices(product_s), matrices(product_h)]), ('b...  93.4 us
    all_to_all x1, blocking collectives, local(): lax.all_to_all(outgoing.reshape(8, 128, SLOTS), 'band', split_axis=0, con...  52.3 us
    all_to_all x1, blocking collectives, local(): lax.all_to_all(incoming.reshape(8, 128, SLOTS), 'band', split_axis=0, con...  51.9 us
    all_to_all x1, waiting for transfers between devices, local(): lax.all_to_all(wire, 'fft', split_axis=0, concat_axis=0, tiled=True)  51 us
    reshape x1, local copies, waits for them, and re-layouts, local(): jnp.broadcast_to(field, (PAIRS, GRID, 2, 2, 2, ZPAD))  15.4 us
    pallas_call x2, Pallas kernels, gram_call(): pl.pallas_call(gram_kernel, grid=(2, SLOTS // lanes), in_specs=[spec, spe...  13.7 us
    unnamed x16, local copies, waits for them, and re-layouts  11.2 us
  transfers between devices with their start and end apart: 3, of which 1 were waited for; matrix products, arithmetic and copies ran while one was open for 7% of the time, Pallas kernels for 35%

profile of v1, /device:TPU:0, one launch (start us, length us, event | category | flops | bytes accessed | tf_op | source)
XLA Modules:
  0.0 520.9 jit_solution(11352591134787091418)
XLA Ops:
  0.6 0.8 fusion.6
  1.4 0.0 copy-start.5
  1.4 2.0 copy-done.5
  3.5 0.0 copy-start.6
  3.5 1.0 copy-done.6
  4.5 5.7 %z_forward.1 = (bf16[16,2,2,16,1920]{4,3,2,1,0:T(8,128)(2,1)S(1)}, bf16[8,2,2,2,16,1920]{5,4,3,2,1,0:T(8,128)(2,1)S(1)}) custom-call(bf16[2,480,1920]{2,1,0:T(8,128)(2,1)S(1)} %bitcast.25, f32[1,1920]{1,0:T(1,128)S(1)} %reshape.131.live_ref, bf16[512,480]{1,0:T(8,128)(2,1)S(1)} %copy-done.6), custom_call_target="tpu_custom_call" | custom-call | flops 1800000000 | bytes 12000000 | tf_op jit(solution)/shard_map/z_forward/pallas_call | solution.py:69
  10.2 0.0 copy-start.2
  10.3 1.9 copy-done.2
  12.2 0.0 copy-start.3
  12.2 2.0 copy-done.3
  14.1 8.2 %all-to-all-start = ((bf16[16,64,1920]{2,1,0:T(8,128)(2,1)}), bf16[16,64,1920]{2,1,0:T(8,128)(2,1)}, u32[]{:S(2)}, u32[]{:S(2)}) async-start(bf16[16,64,1920]{2,1,0:T(8,128)(2,1)} %bitcast.24), calls=%async_computation | async-start | bytes 7864320 | tf_op jit(solution)/shard_map/all_to_all | solution.py:352
  22.3 6.3 %reshape.119 = f32[15,2,120,240]{3,2,1,0:T(8,128)} reshape(f32[15,57600]{1,0:T(8,128)} %param.9) | data formatting | bytes 6912000 | tf_op jit(solution)/shard_map/reshape | solution.py:345
  28.6 51.0 %all-to-all-done.wire_ref = bf16[16,64,1920]{2,1,0:T(8,128)(2,1)} async-done(((bf16[16,64,1920]{2,1,0:T(8,128)(2,1)}), bf16[16,64,1920]{2,1,0:T(8,128)(2,1)}, u32[]{:S(2)}, u32[]{:S(2)}) %all-to-all-start) | async-done | bytes 3932192 | tf_op jit(solution)/shard_map/all_to_all | solution.py:352
  79.6 4.5 all-to-all-start.2
  84.1 2.5 pad_bitcast_fusion
  86.6 2.3 copy.13
  88.9 7.7 %broadcast_in_dim.18 = f32[120,240,2,2,2,16]{1,5,4,3,2,0:T(8,128)} broadcast(f32[120,240,2,16]{1,3,2,0:T(8,128)S(1)} %copy.13), dimensions={0,1,3,5} | broadcast | bytes 18432000 | tf_op jit(solution)/shard_map/broadcast_in_dim | solution.py:347
  96.6 0.0 copy-start.7
  96.6 15.4 %copy.14.field_ref = f32[120,240,128]{2,1,0:T(8,128)} copy(f32[120,240,128]{1,2,0:T(8,128)} %bitcast.26) | data formatting | bytes 29491200 | tf_op jit(solution)/shard_map/reshape | solution.py:347
  112.0 0.0 copy-done.7
  112.0 0.1 reduce_sum.9
  112.2 0.5 and_select_fusion.count_ref
  112.7 0.8 add_select_fusion.2.place_ref
  113.5 169.4 %planes.1 = bf16[16,64,1920]{2,1,0:T(8,128)(2,1)} custom-call(s32[30720]{0:T(1024)} %add_select_fusion.2.place_ref, s32[16]{0:T(128)} %and_select_fusion.count_ref, bf16[16,64,1920]{2,1,0:T(8,128)(2,1)} %all-to-all-done.wire_ref, f32[120,240,128]{2,1,0:T(8,128)} %copy.14.field_ref, bf16[240,384]{1,0:T(8,128)(2,1)} %constant.71.clone.forward_ref, ...), custom_call_target="tpu_custom_call" | custom-call | flops 12999999488 | bytes 24000000 | tf_op jit(solution)/shard_map/planes/pallas_call | solution.py:310
  282.8 0.0 all-to-all-done.2
  282.9 52.3 %all_to_all.25 = bf16[8,128,1920]{2,1,0:T(8,128)(2,1)} all-to-all(bf16[8,128,1920]{2,1,0:T(8,128)(2,1)} %bitcast.27), channel_id=1, replica_groups=mesh['band'=8,'fft'=16] {'band'}, dimensions={0} | all-to-all | bytes 7864320 | tf_op jit(solution)/shard_map/all_to_all | solution.py:358
  335.2 51.9 %all_to_all.26 = bf16[8,128,1920]{2,1,0:T(8,128)(2,1)} all-to-all(bf16[8,128,1920]{2,1,0:T(8,128)(2,1)} %bitcast.8), channel_id=1, replica_groups=mesh['band'=8,'fft'=16] {'band'}, dimensions={0} | all-to-all | bytes 7864320 | tf_op jit(solution)/shard_map/all_to_all | solution.py:357
  387.1 10.6 %all-to-all-start.1 = ((bf16[16,64,1920]{2,1,0:T(8,128)(2,1)}), bf16[16,64,1920]{2,1,0:T(8,128)(2,1)}, u32[]{:S(2)}, u32[]{:S(2)}) async-start(bf16[16,64,1920]{2,1,0:T(8,128)(2,1)} %planes.1), calls=%async_computation.1 | async-start | bytes 7864320 | tf_op jit(solution)/shard_map/all_to_all | solution.py:359
  397.7 7.8 %gram_s.1 = f32[32,32]{1,0:T(8,128)S(1)} custom-call(bf16[8,2,2,2,16,1920]{5,4,3,2,1,0:T(8,128)(2,1)} %bitcast.7.left_ref.right_ref, bf16[8,2,2,2,16,1920]{5,4,3,2,1,0:T(8,128)(2,1)} %bitcast.7.left_ref.right_ref), custom_call_target="tpu_custom_call" | custom-call | flops 2000000000 | bytes 8000000 | tf_op jit(solution)/shard_map/gram_s/pallas_call | solution.py:152
  405.5 0.4 reshape.124
  406.0 0.0 copy-start
  406.0 2.1 copy-done
  408.1 0.0 copy-start.1
  408.1 2.1 copy-done.1
  410.2 0.0 copy-start.4
  410.2 5.8 %gram_h.1 = f32[32,32]{1,0:T(8,128)S(1)} custom-call(bf16[8,2,2,2,16,1920]{5,4,3,2,1,0:T(8,128)(2,1)S(1)} %bitcast.22, bf16[8,2,2,2,16,1920]{5,4,3,2,1,0:T(8,128)(2,1)S(1)} %bitcast.21), custom_call_target="tpu_custom_call" | custom-call | flops 2000000000 | bytes 8000000 | tf_op jit(solution)/shard_map/gram_h/pallas_call | solution.py:152
  416.1 0.4 reshape.129
  416.5 0.9 fusion.2
  417.4 0.1 add.62
  417.5 0.1 add.64
  417.6 0.1 sub.47
  417.6 0.1 sub.49
  417.7 93.4 %psum.7 = f32[4,16,16]{2,1,0:T(8,128)S(1)} all-reduce(f32[4,16,16]{2,1,0:T(8,128)S(1)} %pad_maximum_fusion), channel_id=1, replica_groups=mesh['band'=8,'fft'=16] {'band','fft'}, use_global_device_ids=true, to_apply=%region_1.2 | all-reduce | flops 1024 | bytes 8192 | tf_op jit(solution)/shard_map/psum | solution.py:364
  511.1 0.6 fusion.7
  511.8 0.0 all-to-all-done.1
  511.8 0.0 copy-done.4
  511.8 9.2 %z_backward.1 = bf16[2,480,1920]{2,1,0:T(8,128)(2,1)} custom-call(bf16[16,2,2,16,1920]{4,3,2,1,0:T(8,128)(2,1)} %bitcast.4.wire_ref, f32[1,1920]{1,0:T(1,128)S(1)} %reshape.131.live_ref, bf16[480,512]{1,0:T(8,128)(2,1)S(1)} %copy-done.4), custom_call_target="tpu_custom_call" | custom-call | flops 1800000000 | bytes 8000000 | tf_op jit(solution)/shard_map/z_backward/pallas_call | solution.py:100
  (5 shorter events, 0.1 us)
Async XLA Ops:
  1.4 2.0 copy-start.5
  3.5 1.0 copy-start.6
  10.2 1.9 copy-start.2
  12.2 2.0 copy-start.3
  14.1 65.5 %all-to-all-start = ((bf16[16,64,1920]{2,1,0:T(8,128)(2,1)}), bf16[16,64,1920]{2,1,0:T(8,128)(2,1)}, u32[]{:S(2)}, u32[]{:S(2)}) async-start(bf16[16,64,1920]{2,1,0:T(8,128)(2,1)} %bitcast.24), calls=%async_computation | async-start | bytes 7864320 | tf_op jit(solution)/shard_map/all_to_all | solution.py:352
  79.6 203.3 %all-to-all-start.2 = ((bf16[8,128,1920]{2,1,0:T(8,128)(2,1)}), bf16[8,128,1920]{2,1,0:T(8,128)(2,1)}, u32[]{:S(2)}, u32[]{:S(2)}) async-start(bf16[8,128,1920]{2,1,0:T(8,128)(2,1)} %bitcast.23), calls=%async_computation.2 | async-start | bytes 7864320 | tf_op jit(solution)/shard_map/all_to_all | solution.py:353
  96.6 15.4 %copy-start.7 = (s32[30720]{0:T(1024)S(1)}, s32[30720]{0:T(1024)}, u32[]{:S(2)}) copy-start(s32[30720]{0:T(1024)} %param.10) | copy-start | bytes 368644
  387.1 124.6 %all-to-all-start.1 = ((bf16[16,64,1920]{2,1,0:T(8,128)(2,1)}), bf16[16,64,1920]{2,1,0:T(8,128)(2,1)}, u32[]{:S(2)}, u32[]{:S(2)}) async-start(bf16[16,64,1920]{2,1,0:T(8,128)(2,1)} %planes.1), calls=%async_computation.1 | async-start | bytes 7864320 | tf_op jit(solution)/shard_map/all_to_all | solution.py:359
  406.0 2.1 copy-start
  408.1 2.1 copy-start.1
  410.2 101.5 %copy-start.4 = (bf16[480,512]{1,0:T(8,128)(2,1)S(1)}, bf16[480,512]{1,0:T(8,128)(2,1)}, u32[]{:S(2)}) copy-start(bf16[480,512]{1,0:T(8,128)(2,1)} %constant.70.clone.table_ref) | copy-start | bytes 1474564

commit v2 on v1

v2 whole, which is shorter than its diff:
```python
import functools
import math

import jax
import jax.numpy as jnp
import ml_dtypes
import numpy as np
from jax import lax
from jax.experimental import pallas as pl
from jax.experimental.pallas import tpu as pltpu
from jax.sharding import PartitionSpec as P

STICKS = 24576
GRID = 240
SLOTS = 1920
GROUPS = 16
PLANES = 15
ZPAD = 16
BOX = 192
HALF = BOX // 2
PAIRS = GRID // 2
ROWS = BOX * BOX
BLOCK = 384
PITCH = 200
PITCHB = 120
N1 = 8
N2 = 8
N4 = 8
MIB = 1 << 20


def trig():
    counter = np.arange(GRID, dtype=np.int32)
    phases = counter[:, None] * counter[None, :] % GRID
    angles = phases.astype(np.float32) * np.float32(2.0 * math.pi / GRID)
    factor = np.float32(1.0 / math.sqrt(GRID))
    cosine = (np.cos(angles) * factor).astype(ml_dtypes.bfloat16)
    sine = (np.sin(angles) * factor).astype(ml_dtypes.bfloat16)
    return cosine, sine


def tables():
    cosine, sine = trig()
    box = np.arange(BOX) - HALF
    box = np.where(box < 0, box + GRID, box)
    z_forward = np.zeros((GROUPS, 2, ZPAD, 2, GRID), ml_dtypes.bfloat16)
    cos_z = cosine.reshape(GROUPS, PLANES, GRID)
    sin_z = sine.reshape(GROUPS, PLANES, GRID)
    z_forward[:, 0, :PLANES, 0] = cos_z
    z_forward[:, 0, :PLANES, 1] = -sin_z
    z_forward[:, 1, :PLANES, 0] = sin_z
    z_forward[:, 1, :PLANES, 1] = cos_z
    z_forward = z_forward.reshape(GROUPS * 2 * ZPAD, 2 * GRID)
    z_backward = np.ascontiguousarray(z_forward.T)
    cos_box, sin_box = cosine[:, box], sine[:, box]
    forward = np.concatenate([cos_box, sin_box], axis=1)
    backward = np.concatenate([cos_box.T, -sin_box.T], axis=1)
    return z_forward, z_backward, forward, backward


def z_forward_kernel(orbit_ref, live_ref, table_ref, wire_ref, share_ref):
    masked = (orbit_ref[0].astype(jnp.float32) * live_ref[...]).astype(jnp.bfloat16)
    values = jnp.dot(table_ref[...], masked, preferred_element_type=jnp.float32).astype(jnp.bfloat16)
    lanes = values.shape[-1]
    wire_ref[...] = values.reshape(GROUPS, 2, 1, ZPAD, lanes)
    for c in range(2):
        for q in range(15):
            share_ref[q // 2, q % 2, c, 0] = masked[c * GRID + q * 16 : c * GRID + q * 16 + 16]
        share_ref[7, 1, c, 0] = jnp.zeros((16, lanes), jnp.bfloat16)


def z_forward_call(orbits, live, table):
    lanes = BLOCK
    return pl.pallas_call(
        z_forward_kernel,
        grid=(2, SLOTS // lanes),
        in_specs=[
            pl.BlockSpec((1, 2 * GRID, lanes), lambda b, t: (b, 0, t)),
            pl.BlockSpec((1, lanes), lambda b, t: (0, t)),
            pl.BlockSpec((512, 2 * GRID), lambda b, t: (0, 0)),
        ],
        out_specs=[
            pl.BlockSpec((GROUPS, 2, 1, ZPAD, lanes), lambda b, t: (0, 0, b, 0, t)),
            pl.BlockSpec((8, 2, 2, 1, 16, lanes), lambda b, t: (0, 0, 0, b, 0, t)),
        ],
        out_shape=[
            jax.ShapeDtypeStruct((GROUPS, 2, 2, ZPAD, SLOTS), jnp.bfloat16),
            jax.ShapeDtypeStruct((8, 4, 2, 2, 16, SLOTS), jnp.bfloat16),
        ],
        compiler_params=pltpu.CompilerParams(vmem_limit_bytes=60 * MIB),
        cost_estimate=pl.CostEstimate(flops=1_800_000_000, bytes_accessed=12_000_000, transcendentals=0),
        name="z_forward",
    )(orbits, live, table)


def z_backward_kernel(wire_ref, live_ref, table_ref, out_ref):
    lanes = wire_ref.shape[-1]
    values = wire_ref[...].reshape(512, lanes)
    applied = jnp.dot(table_ref[...], values, preferred_element_type=jnp.float32)
    out_ref[0] = (applied * live_ref[...]).astype(jnp.bfloat16)


def z_backward_call(wire, live, table):
    lanes = BLOCK
    return pl.pallas_call(
        z_backward_kernel,
        grid=(2, SLOTS // lanes),
        in_specs=[
            pl.BlockSpec((GROUPS, 2, 1, ZPAD, lanes), lambda b, t: (0, 0, b, 0, t)),
            pl.BlockSpec((1, lanes), lambda b, t: (0, t)),
            pl.BlockSpec((2 * GRID, 512), lambda b, t: (0, 0)),
        ],
        out_specs=pl.BlockSpec((1, 2 * GRID, lanes), lambda b, t: (b, 0, t)),
        out_shape=jax.ShapeDtypeStruct((2, 2 * GRID, SLOTS), jnp.bfloat16),
        compiler_params=pltpu.CompilerParams(vmem_limit_bytes=60 * MIB),
        cost_estimate=pl.CostEstimate(flops=1_800_000_000, bytes_accessed=8_000_000, transcendentals=0),
        name="z_backward",
    )(wire, live, table)


def gram_kernel(left_ref, *refs):
    *right_refs, out_ref, total = refs
    step = pl.program_id(0) * pl.num_programs(1) + pl.program_id(1)
    lanes = left_ref.shape[-1]
    left = left_ref[...].reshape(512, lanes)
    right = jnp.concatenate([ref[...].reshape(512 // len(right_refs), lanes) for ref in right_refs], axis=0)
    product = lax.dot_general(left, right, (((1,), (1,)), ((), ())), preferred_element_type=jnp.float32)

    @pl.when(step == 0)
    def _():
        total[...] = product

    @pl.when(step > 0)
    def _():
        total[...] += product

    @pl.when(step == pl.num_programs(0) * pl.num_programs(1) - 1)
    def _():
        row = lax.broadcasted_iota(jnp.int32, (512, 512), 0)
        column = lax.broadcasted_iota(jnp.int32, (512, 512), 1)
        diagonal = jnp.where(row % 16 == column % 16, total[...], 0.0)
        pick_row = lax.broadcasted_iota(jnp.int32, (32, 512), 0)
        pick_column = lax.broadcasted_iota(jnp.int32, (32, 512), 1)
        pick = jnp.where(pick_column // 16 == pick_row, 1.0, 0.0)
        by_row = jnp.dot(pick, diagonal, preferred_element_type=jnp.float32, precision=lax.Precision.HIGHEST)
        out_ref[...] = lax.dot_general(
            by_row,
            pick,
            (((1,), (1,)), ((), ())),
            preferred_element_type=jnp.float32,
            precision=lax.Precision.HIGHEST,
        )


def gram_call(left, rights, name):
    lanes = 640
    spec = pl.BlockSpec((8, 1, 2, 2, 16, lanes), lambda g, t: (0, g, 0, 0, 0, t))
    if len(rights) == 1:
        right_spec = spec
    else:
        right_spec = pl.BlockSpec((1, 2, 2, 16, lanes), lambda g, t: (g, 0, 0, 0, t))
    return pl.pallas_call(
        gram_kernel,
        grid=(2, SLOTS // lanes),
        in_specs=[spec] + [right_spec] * len(rights),
        out_specs=pl.BlockSpec((32, 32), lambda g, t: (0, 0)),
        out_shape=jax.ShapeDtypeStruct((32, 32), jnp.float32),
        scratch_shapes=[pltpu.VMEM((512, 512), jnp.float32)],
        compiler_params=pltpu.CompilerParams(vmem_limit_bytes=60 * MIB),
        cost_estimate=pl.CostEstimate(flops=2_000_000_000, bytes_accessed=8_000_000, transcendentals=0),
        name=name,
    )(left, *rights)


def matrices(product, order=None):
    parts = product.reshape(8, 2, 2, 8, 2, 2)
    if order is not None:
        parts = jnp.take(parts, order, axis=3)
    first = parts[:, 0, :, :, 0, :] + parts[:, 1, :, :, 1, :]
    second = parts[:, 0, :, :, 1, :] - parts[:, 1, :, :, 0, :]
    return jnp.stack([first.reshape(16, 16), second.reshape(16, 16)])


def summed(values, axis):
    size = lax.axis_size(axis)
    copies = jnp.broadcast_to(values[None], (size,) + values.shape)
    return jnp.sum(lax.all_to_all(copies, axis, split_axis=0, concat_axis=0, tiled=True), axis=0)


def spread_blocks(blocks, axis):
    size = lax.axis_size(axis)
    me = lax.axis_index(axis)
    result = []
    for shift in range(size):
        block = lax.dynamic_index_in_dim(blocks, (me + shift) % size, 0, keepdims=False)
        if shift:
            block = lax.ppermute(block, axis, [(i, (i + shift) % size) for i in range(size)])
        result.append(block)
    return result, (me - jnp.arange(size)) % size


def plane_kernel(
    place_ref, pick_ref, count_ref, upper_ref, wire_ref, field_ref, forward_ref, backward_ref, out_ref,
    grid_ref, mid_ref, stage_a, stage_b, list_ref
):
    step = pl.program_id(0)
    lane = lax.broadcasted_iota(jnp.int32, (1, 128), 1)
    low = lane % 64 < 32
    sign = jnp.where(lane < 64, -1.0, 1.0)

    def turned(values):
        return pltpu.roll(values, 64, 1) * sign

    def doubled(values):
        return jnp.concatenate([values, turned(values)], axis=0).astype(jnp.bfloat16)

    def exchange(first, second):
        return (
            jnp.where(low, first, pltpu.roll(second, 32, 1)),
            jnp.where(low, pltpu.roll(first, 96, 1), second),
        )

    @pl.when(step == 0)
    def _():
        def clear(i, carry):
            grid_ref[pl.ds(pl.multiple_of(i * 512, 512), 512), :] = jnp.zeros((512, 128), jnp.float32)
            return carry

        lax.fori_loop(0, ROWS // 512, clear, 0)

        def group(p, total):
            def note(t, inner):
                list_ref[inner] = p * 15 + t
                return inner + 1

            return lax.fori_loop(0, count_ref[p], note, total)

        total = lax.fori_loop(0, GROUPS, group, 0)
        list_ref[total] = list_ref[total - 1]
        list_ref[total + 1] = list_ref[total - 1]
        list_ref[total + 2] = list_ref[total - 1]
        list_ref[255] = (total + 1) // 2
        eye_row = lax.broadcasted_iota(jnp.int32, (128, 128), 0)
        eye_column = lax.broadcasted_iota(jnp.int32, (128, 128), 1)
        eye = jnp.where(eye_row == eye_column, 1.0, 0.0).astype(jnp.bfloat16)

        def rows_of(entry):
            p = entry // 15
            block = wire_ref[p, :, pl.ds(pl.multiple_of((entry - p * 15) * 128, 128), 128)]
            twice = jnp.concatenate([block[0:32], block[0:32], block[32:64], block[32:64]], axis=0)
            return lax.dot_general(eye, twice, (((1,), (1,)), ((), ())), preferred_element_type=jnp.float32)

        def spread(entry, stage):
            for u in range(128):
                grid_ref[pl.ds(place_ref[entry * 128 + u], 1), :] = stage[u : u + 1, :]

        def scatter(i, carry):
            entry = list_ref[2 * i]
            entry_b = list_ref[2 * i + 1]
            entry_c = list_ref[2 * i + 2]
            stage_b[...] = rows_of(entry_b)
            spread(entry, stage_a)
            stage_a[...] = rows_of(entry_c)
            spread(entry_b, stage_b)
            return carry

        stage_a[...] = rows_of(list_ref[0])
        lax.fori_loop(0, list_ref[255], scatter, 0)

        def x_forward(i, carry):
            parts = []
            for j in range(N1):
                k = i * N1 + j
                first = grid_ref[pl.ds(pl.multiple_of(k * BOX, BOX), BOX), :]
                second = grid_ref[pl.ds(pl.multiple_of((k + HALF) * BOX, BOX), BOX), :]
                parts.append(doubled(jnp.where(low, first, second)))
            result = jnp.dot(forward_ref[...], jnp.concatenate(parts, axis=1), preferred_element_type=jnp.float32)
            for j in range(N1):
                k = i * N1 + j
                part = result[:, j * 128 : (j + 1) * 128]
                mid_ref[pl.ds(k, PAIRS, stride=PITCH), :] = part[:PAIRS]
                mid_ref[pl.ds(k + HALF, PAIRS, stride=PITCH), :] = part[PAIRS:]
            return carry

        lax.fori_loop(0, HALF // N1, x_forward, 0)

    def y_steps(i, carry):
        parts = []
        for j in range(N2):
            pair = step * 8 + i * N2 + j
            base = pl.multiple_of(pair * PITCH, 8)
            first = mid_ref[pl.ds(base, HALF), :]
            second = mid_ref[pl.ds(base + HALF, HALF), :]
            even, odd = exchange(first, second)
            parts.append(doubled(jnp.concatenate([even, odd], axis=0)))
        spatial = jnp.dot(forward_ref[...], jnp.concatenate(parts, axis=1), preferred_element_type=jnp.float32)
        parts = []
        for j in range(N2):
            parts.append(doubled(spatial[:, j * 128 : (j + 1) * 128] * field_ref[i * N2 + j]))
        result = jnp.dot(backward_ref[...], jnp.concatenate(parts, axis=1), preferred_element_type=jnp.float32)
        for j in range(N2):
            pair = step * 8 + i * N2 + j
            grid_ref[pl.ds(pair, BOX, stride=PITCHB), :] = result[:, j * 128 : (j + 1) * 128]
        return carry

    lax.fori_loop(0, 8 // N2, y_steps, 0)

    @pl.when(step == pl.num_programs(0) - 1)
    def _():
        def x_backward(i, carry):
            parts = []
            for j in range(N4):
                k = i * N4 + j
                first = grid_ref[pl.ds(pl.multiple_of(k * PITCHB, 8), PAIRS), :]
                second = grid_ref[pl.ds(pl.multiple_of((k + HALF) * PITCHB, 8), PAIRS), :]
                even, odd = exchange(first, second)
                parts.append(doubled(jnp.concatenate([even, odd], axis=0)))
            result = jnp.dot(backward_ref[...], jnp.concatenate(parts, axis=1), preferred_element_type=jnp.float32)
            for j in range(N4):
                k = i * N4 + j
                mid_ref[pl.ds(pl.multiple_of(k * BOX, BOX), BOX), :] = result[:, j * 128 : (j + 1) * 128]
            return carry

        lax.fori_loop(0, HALF // N4, x_backward, 0)
        select_row = lax.broadcasted_iota(jnp.int32, (128, 128), 0)
        select_column = lax.broadcasted_iota(jnp.int32, (128, 128), 1)
        source = select_row % 64 // 32 * 64 + select_row // 64 * 32 + select_row % 32
        select = jnp.where(select_column == source, 1.0, 0.0).astype(jnp.bfloat16)
        origin = pl.multiple_of((step - (pl.num_programs(0) - 1)) * 8, 8)

        def gather(entry, stage):
            for u in range(128):
                stage[pl.ds(origin + u, 1), :] = mid_ref[pl.ds(pick_ref[entry * 128 + u], 1), :]

        def write(entry, stage):
            p = entry // 15
            base = pl.multiple_of((entry - p * 15) * 128, 128)
            both = lax.dot_general(
                select, stage[...].astype(jnp.bfloat16), (((1,), (1,)), ((), ())), preferred_element_type=jnp.float32
            )
            upper = upper_ref[pl.ds(entry, 1), :] > 0.0
            out_ref[p, :, pl.ds(base, 128)] = jnp.where(upper, both[64:], both[:64]).astype(jnp.bfloat16)

        def pick(i, carry):
            entry = list_ref[2 * i]
            entry_b = list_ref[2 * i + 1]
            entry_c = list_ref[2 * i + 2]
            gather(entry_b, stage_b)
            write(entry, stage_a)
            gather(entry_c, stage_a)
            write(entry_b, stage_b)
            return carry

        def group(p, carry):
            def blank(t, inner):
                out_ref[p, :, pl.ds(pl.multiple_of(t * 128, 128), 128)] = jnp.zeros((64, 128), jnp.bfloat16)
                return inner

            return lax.fori_loop(count_ref[p], SLOTS // 128, blank, carry)

        lax.fori_loop(0, GROUPS, group, 0)
        gather(list_ref[0], stage_a)
        lax.fori_loop(0, list_ref[255], pick, 0)


def plane_call(place, pick, count, upper, wire, field, forward, backward):
    whole = lambda shape: pl.BlockSpec(shape, lambda i: (0,) * len(shape), pipeline_mode=pl.Buffered(1))
    return pl.pallas_call(
        plane_kernel,
        grid=(PAIRS // 8,),
        in_specs=[
            pl.BlockSpec(memory_space=pltpu.SMEM),
            pl.BlockSpec(memory_space=pltpu.SMEM),
            pl.BlockSpec(memory_space=pltpu.SMEM),
            whole((GROUPS * SLOTS // 128, 128)),
            whole((GROUPS, 64, SLOTS)),
            pl.BlockSpec((8, GRID, 128), lambda i: (i, 0, 0)),
            whole((GRID, 2 * BOX)),
            whole((BOX, 2 * GRID)),
        ],
        out_specs=whole((GROUPS, 64, SLOTS)),
        out_shape=jax.ShapeDtypeStruct((GROUPS, 64, SLOTS), jnp.bfloat16),
        scratch_shapes=[
            pltpu.VMEM((ROWS + 8, 128), jnp.float32),
            pltpu.VMEM((PAIRS * PITCH, 128), jnp.float32),
            pltpu.VMEM((128, 128), jnp.float32),
            pltpu.VMEM((128, 128), jnp.float32),
            pltpu.SMEM((256,), jnp.int32),
        ],
        compiler_params=pltpu.CompilerParams(vmem_limit_bytes=56 * MIB),
        cost_estimate=pl.CostEstimate(flops=13_000_000_000, bytes_accessed=24_000_000, transcendentals=0),
        name="planes",
    )(place, pick, count, upper, wire, field, forward, backward)


def field_kernel(lower_ref, upper_ref, out_ref):
    blank = jnp.zeros((1, lower_ref.shape[-1]), jnp.float32)
    lower = jnp.concatenate([lower_ref[...], blank], axis=0)
    upper = jnp.concatenate([upper_ref[...], blank], axis=0)
    once = jnp.concatenate([lower, lower, upper, upper], axis=0)
    out_ref[...] = jnp.concatenate([once, once], axis=0).T.reshape(8, GRID, 128)


def field_call(potential):
    lanes = 8 * GRID
    return pl.pallas_call(
        field_kernel,
        grid=(PAIRS // 8,),
        in_specs=[
            pl.BlockSpec((PLANES, lanes), lambda i: (0, i)),
            pl.BlockSpec((PLANES, lanes), lambda i: (0, i + PAIRS // 8)),
        ],
        out_specs=pl.BlockSpec((8, GRID, 128), lambda i: (i, 0, 0)),
        out_shape=jax.ShapeDtypeStruct((PAIRS, GRID, 128), jnp.float32),
        compiler_params=pltpu.CompilerParams(vmem_limit_bytes=60 * MIB),
        cost_estimate=pl.CostEstimate(flops=0, bytes_accessed=18_000_000, transcendentals=0),
        name="field",
    )(potential, potential)


def local(orbitals, potential, stick_column, column_slot):
    z_forward, z_backward, forward, backward = (jnp.asarray(table) for table in tables())
    live_all = stick_column >= 0
    own = lax.dynamic_slice_in_dim(stick_column, lax.axis_index("fft") * SLOTS, SLOTS)
    live = (own >= 0).astype(jnp.float32)[None, :]
    column_x, column_y = stick_column // GRID, stick_column % GRID
    box_x = jnp.where(column_x < GRID // 2, column_x + HALF, column_x - (GRID - HALF))
    box_y = jnp.where(column_y < GRID // 2, column_y + HALF, column_y - (GRID - HALF))
    place = jnp.where(live_all, box_y * BOX + box_x, ROWS)
    count = (jnp.sum(live_all.reshape(GROUPS, SLOTS).astype(jnp.int32), axis=1) + 127) // 128
    upper = live_all & (box_y >= HALF)
    choose = jnp.where(live_all, jnp.where(upper, box_y - HALF, box_y) * BOX + box_x, 0)
    upper = upper.astype(jnp.float32).reshape(GROUPS * SLOTS // 128, 128)
    field = field_call(potential)

    wire, share = z_forward_call(orbitals.transpose(0, 2, 1), live, z_forward)
    share = share.reshape(8, 256, SLOTS)
    incoming = lax.all_to_all(wire.reshape(GROUPS, 64, SLOTS), "fft", split_axis=0, concat_axis=0, tiled=True)
    share, field, place, choose, count, upper = lax.optimization_barrier(
        (share, field, place, choose, count, upper)
    )
    shared = share.at[:, 128:].set(incoming.reshape(8, 128, SLOTS))
    shared = lax.all_to_all(shared, "band", split_axis=0, concat_axis=0, tiled=True)
    outgoing = plane_call(place, choose, count, upper, incoming, field, forward, backward)
    returned = lax.all_to_all(outgoing, "fft", split_axis=0, concat_axis=0, tiled=True)
    rights, order = spread_blocks(outgoing.reshape(8, 2, 2, 2, 16, SLOTS), "band")
    share = shared[:, :128].reshape(8, 2, 2, 2, 16, SLOTS)
    left = shared[:, 128:].reshape(8, 2, 2, 2, 16, SLOTS)
    product_s = gram_call(share, [share], "gram_s")
    product_h = gram_call(left, rights, "gram_h")
    product_s, product_h, returned = lax.optimization_barrier((product_s, product_h, returned))
    applied = z_backward_call(returned.reshape(GROUPS, 2, 2, ZPAD, SLOTS), live, z_backward)
    products = jnp.concatenate([matrices(product_s), matrices(product_h, order)])
    products = summed(summed(products, "fft"), "band") * (1.0 / (2.0 * STICKS * GRID))
    return (applied.transpose(0, 2, 1), products[0:2], products[2:4])


def solution(mesh):
    return jax.shard_map(
        local,
        mesh=mesh,
        in_specs=(P("band", "fft", None), P("fft", None), P(), P()),
        out_specs=(P("band", "fft", None), P(), P()),
        check_vma=False,
    )
```

time: 523 us -> 301 us (0.58)
  blocking collectives: 198 us -> 16.3 us
  Pallas kernels: 198 us -> 152 us
  local copies, waits for them, and re-layouts: 47.2 us -> 19.3 us
  starting transfers between devices: 23.3 us -> 50.8 us
    psum x1 -> x0, blocking collectives: 93.4 us -> none  [local(): lax.psum(jnp.concatenate([matrices(product_s), matrices(product_h)]), ('b...]
    all_to_all x2 -> x1, blocking collectives: 104 us -> 16.3 us  [summed(): lax.all_to_all(copies, axis, split_axis=0, concat_axis=0, tiled=True)]
    pallas_call x1, Pallas kernels: 169 us -> 101 us  [plane_call(): pl.pallas_call(plane_kernel, grid=(PAIRS // 8,), in_specs=[pl.BlockSpec(m...]
    reshape x2 -> x0, local copies, waits for them, and re-layouts: 21.7 us -> none  [the longest x1 15.4 us: local(): jnp.broadcast_to(field, (PAIRS, GRID, 2, 2, 2, ZPAD))]
    ppermute x0 -> x7, starting transfers between devices: none -> 19.9 us  [spread_blocks(): lax.ppermute(block, axis, [(i, (i + shift) % size) for i in range(size)])]
    pallas_call x2 -> x3, Pallas kernels: 13.7 us -> 30.5 us  [the longest x2 16.8 us: gram_call(): pl.pallas_call(gram_kernel, grid=(2, SLOTS // lanes), in_specs=[spec] + [...]
    ppermute x0 -> x7, waiting for transfers between devices: none -> 12.3 us  [spread_blocks(): lax.ppermute(block, axis, [(i, (i + shift) % size) for i in range(size)])]
    unnamed x16 -> x14, local copies, waits for them, and re-layouts: 11.2 us -> 1.32 us
  transfers between devices with their start and end apart: 3 -> 11, of which waited for: 1 -> 4; matrix products, arithmetic and copies ran while one was open for 7% -> 4% of each run, Pallas kernels for 35% -> 47%
where the time goes in v2:
time: 301 us; the launch traced here: 298 us
  Pallas kernels  152 us (50%)
  waiting for transfers between devices  53.7 us (18%)
  starting transfers between devices  50.8 us (17%)
  local copies, waits for them, and re-layouts  19.3 us (6%)
  blocking collectives  16.3 us (5%)
  other arithmetic  5.49 us (2%)
    pallas_call x1, Pallas kernels, plane_call(): pl.pallas_call(plane_kernel, grid=(PAIRS // 8,), in_specs=[pl.BlockSpec(m...  101 us
    all_to_all x1, waiting for transfers between devices, local(): lax.all_to_all(wire.reshape(GROUPS, 64, SLOTS), 'fft', split_axis=0, conc...  41.3 us
    ppermute x7, starting transfers between devices, spread_blocks(): lax.ppermute(block, axis, [(i, (i + shift) % size) for i in range(size)])  19.9 us
    pallas_call x2, Pallas kernels, gram_call(): pl.pallas_call(gram_kernel, grid=(2, SLOTS // lanes), in_specs=[spec] + [...  16.8 us
    all_to_all x1, blocking collectives, summed(): lax.all_to_all(copies, axis, split_axis=0, concat_axis=0, tiled=True)  16.3 us
    pallas_call x1, Pallas kernels, field_call(): pl.pallas_call(field_kernel, grid=(PAIRS // 8,), in_specs=[pl.BlockSpec((...  13.7 us
    ppermute x7, waiting for transfers between devices, spread_blocks(): lax.ppermute(block, axis, [(i, (i + shift) % size) for i in range(size)])  12.3 us
    all_to_all x1, starting transfers between devices, local(): lax.all_to_all(outgoing, 'fft', split_axis=0, concat_axis=0, tiled=True)  10.5 us
  transfers between devices with their start and end apart: 11, of which 4 were waited for; matrix products, arithmetic and copies ran while one was open for 4% of the time, Pallas kernels for 47%

profile of v2, /device:TPU:0, one launch (start us, length us, event | category | flops | bytes accessed | tf_op | source)
XLA Modules:
  0.0 298.0 jit_solution(1555653850294441920)
XLA Ops:
  0.6 0.8 fusion.6
  1.4 0.6 reshape.212.live_ref
  2.0 10.3 %z_forward.1 = (bf16[16,2,2,16,1920]{4,3,2,1,0:T(8,128)(2,1)}, bf16[8,4,2,2,16,1920]{5,4,3,2,1,0:T(8,128)(2,1)}) custom-call(bf16[2,480,1920]{2,1,0:T(8,128)(2,1)} %bitcast.52, f32[1,1920]{1,0:T(1,128)} %reshape.212.live_ref, bf16[512,480]{1,0:T(8,128)(2,1)} %constant.196.clone.table_ref), custom_call_target="tpu_custom_call" | custom-call | flops 1800000000 | bytes 12000000 | tf_op jit(solution)/shard_map/z_forward/pallas_call | solution.py:74
  12.3 0.0 copy-start
  12.3 8.3 %all-to-all-start = ((bf16[16,64,1920]{2,1,0:T(8,128)(2,1)}), bf16[16,64,1920]{2,1,0:T(8,128)(2,1)}, u32[]{:S(2)}, u32[]{:S(2)}) async-start(bf16[16,64,1920]{2,1,0:T(8,128)(2,1)} %bitcast.50), calls=%async_computation | async-start | bytes 7864320 | tf_op jit(solution)/shard_map/all_to_all | solution.py:438
  20.6 0.0 copy-done
  20.6 0.8 convert_bitcast_fusion
  21.5 0.1 reduce_sum.27
  21.6 13.7 %field.1.field_ref = f32[120,240,128]{2,1,0:T(8,128)} custom-call(f32[15,57600]{1,0:T(8,128)} %upper_ref.1, f32[15,57600]{1,0:T(8,128)} %upper_ref.1), custom_call_target="tpu_custom_call" | custom-call | bytes 18000000 | tf_op jit(solution)/shard_map/field/pallas_call | solution.py:406
  35.3 0.5 and_select_fusion.2.count_ref
  35.8 0.9 fusion.2
  36.7 41.3 %all-to-all-done.wire_ref = bf16[16,64,1920]{2,1,0:T(8,128)(2,1)} async-done(((bf16[16,64,1920]{2,1,0:T(8,128)(2,1)}), bf16[16,64,1920]{2,1,0:T(8,128)(2,1)}, u32[]{:S(2)}, u32[]{:S(2)}) %all-to-all-start) | async-done | bytes 3932192 | tf_op jit(solution)/shard_map/all_to_all | solution.py:438
  78.1 4.4 %bitcast_dynamic-update-slice_fusion = bf16[8,256,1920]{2,1,0:T(8,128)(2,1)} fusion(bf16[8,256,1920]{2,1,0:T(8,128)(2,1)} %bitcast.49, bf16[8,128,1920]{2,1,0:T(8,128)(2,1)} %bitcast.44), kind=kLoop, calls=%fused_computation.1 | loop fusion | bytes 7864320 | tf_op jit(solution)/shard_map/scatter | solution.py:442
  82.5 4.9 %all-to-all-start.1 = ((bf16[8,256,1920]{2,1,0:T(8,128)(2,1)}), bf16[8,256,1920]{2,1,0:T(8,128)(2,1)}, u32[]{:S(2)}, u32[]{:S(2)}) async-start(bf16[8,256,1920]{2,1,0:T(8,128)(2,1)} %bitcast_dynamic-update-slice_fusion), calls=%async_computation.1 | async-start | bytes 15728640 | tf_op jit(solution)/shard_map/all_to_all | solution.py:443
  87.4 101.4 %planes.1 = bf16[16,64,1920]{2,1,0:T(8,128)(2,1)} custom-call(s32[30720]{0:T(1024)} %get-tuple-element.29.place_ref, s32[30720]{0:T(1024)} %get-tuple-element.30.pick_ref, s32[16]{0:T(128)} %and_select_fusion.2.count_ref, f32[240,128]{1,0:T(8,128)} %get-tuple-element.32.upper_ref, bf16[16,64,1920]{2,1,0:T(8,128)(2,1)} %all-to-all-done.wire_ref, ...), custom_call_target="tpu_custom_call" | custom-call | flops 12999999488 | bytes 24000000 | tf_op jit(solution)/shard_map/planes/pallas_call | solution.py:368
  188.8 0.0 all-to-all-done.1
  188.8 10.5 %all-to-all-start.2 = ((bf16[16,64,1920]{2,1,0:T(8,128)(2,1)}), bf16[16,64,1920]{2,1,0:T(8,128)(2,1)}, u32[]{:S(2)}, u32[]{:S(2)}) async-start(bf16[16,64,1920]{2,1,0:T(8,128)(2,1)} %planes.1), calls=%async_computation.2 | async-start | bytes 7864320 | tf_op jit(solution)/shard_map/all_to_all | solution.py:445
  199.4 3.2 %dynamic-slice_bitcast_fusion = (bf16[2,2,2,16,1920]{4,3,2,1,0:T(8,128)(2,1)S(1)}, bf16[2,2,2,16,1920]{4,3,2,1,0:T(8,128)(2,1)S(1)}, bf16[2,2,2,16,1920]{4,3,2,1...) fusion(bf16[8,2,2,2,16,1920]{5,4,3,2,1,0:T(8,128)(2,1)} %bitcas, ...), kind=kLoop, calls=%fused_computation.2 | loop fusion | bytes 7864352 | tf_op jit(solution)/shard_map/jit(dynamic_index_in_dim)/squeeze | solution.py:195
  202.6 0.1 collective-permute-start
  202.7 1.8 collective-permute-start.1
  204.6 2.1 collective-permute-start.2
  206.7 2.0 collective-permute-start.3
  208.7 1.6 collective-permute-start.4
  210.3 6.5 %collective-permute-done.refs_1_ = bf16[2,2,2,16,1920]{4,3,2,1,0:T(8,128)(2,1)S(1)} collective-permute-done((bf16[2,2,2,16,1920]{4,3,2,1,0:T(8,128)(2,1)S(1)}, bf16[2,2,2,16,1920]{4,3,2,1,0:T(8,128)(2,1)S(1)}, u32[]{:S(2)}, u32[]{:S(2)}) %collective-permute-start) | collective-permute-done | bytes 491552 | tf_op jit(solution)/shard_map/ppermute | solution.py:197
  216.8 0.0 copy-start.1
  216.8 1.9 collective-permute-start.5
  218.7 0.0 collective-permute-done.1.refs_2_
  218.7 0.0 copy-start.2
  218.7 10.4 %collective-permute-start.6 = (bf16[2,2,2,16,1920]{4,3,2,1,0:T(8,128)(2,1)S(1)}, bf16[2,2,2,16,1920]{4,3,2,1,0:T(8,128)(2,1)}, u32[]{:S(2)}, u32[]{:S(2)}) collective-permute-start(bf16[2,2,2,16,1920]{4,3,2,1,0:T(8,128)(2,1)S(1)} %get-tuple-element.43), channel_id=1, source_target_pairs={{0,112},{16,0},{32,16},{48,32},{64,48},{80,64},{96,80},{112,96},{1... | collective-permute-start | bytes 1474568 | tf_op jit(solution)/shard_map/ppermute | solution.py:197
  229.0 5.7 %fusion.10 = (bf16[8,128,1920]{2,1,0:T(8,128)(2,1)}, bf16[8,128,1920]{2,1,0:T(8,128)(2,1)}) fusion(bf16[8,256,1920]{2,1,0:T(8,128)(2,1)} %all-to-all-done.1), kind=kLoop, calls=%fused_computation.53 | loop fusion | bytes 15728640 | tf_op jit(solution)/shard_map/slice | solution.py:448
  234.8 0.0 copy-done.1
  234.8 0.0 copy-done.2
  234.8 8.4 %gram_s.1 = f32[32,32]{1,0:T(8,128)} custom-call(bf16[8,2,2,2,16,1920]{5,4,3,2,1,0:T(8,128)(2,1)} %bitcast.45, bf16[8,2,2,2,16,1920]{5,4,3,2,1,0:T(8,128)(2,1)} %bitcast.46), custom_call_target="tpu_custom_call" | custom-call | flops 2000000000 | bytes 8000000 | tf_op jit(solution)/shard_map/gram_s/pallas_call | solution.py:162
  243.2 0.0 collective-permute-done.2.refs_3_
  243.2 0.0 collective-permute-done.3.refs_4_
  243.2 3.9 %collective-permute-done.4.refs_5_ = bf16[2,2,2,16,1920]{4,3,2,1,0:T(8,128)(2,1)} collective-permute-done((bf16[2,2,2,16,1920]{4,3,2,1,0:T(8,128)(2,1)S(1)}, bf16[2,2,2,16,1920]{4,3,2,1,0:T(8,128)(2,1)}, u32[]{:S(2)}, u32[]{:S(2)}) %collective-permute-start.4) | collective-permute-done | bytes 491552 | tf_op jit(solution)/shard_map/ppermute | solution.py:197
  247.1 0.0 collective-permute-done.5.refs_6_
  247.1 1.9 collective-permute-done.6.refs_7_
  249.1 0.0 copy-done.3
  249.1 8.3 %gram_h.1 = f32[32,32]{1,0:T(8,128)} custom-call(bf16[8,2,2,2,16,1920]{5,4,3,2,1,0:T(8,128)(2,1)} %bitcast.48, bf16[2,2,2,16,1920]{4,3,2,1,0:T(8,128)(2,1)} %get-tuple-element.50.refs_0_, bf16[2,2,2,16,1920]{4,3,2,1,0:T(8,128)(2,1)} %copy-done.1, bf16[2,2,2,16,1920]{4,3,2,1,0:T(8,128)(2,1)} %copy-done.2, bf16[2,2,2,16,1920]{4,3,2,1,0:T(8,128)(2,1)} %copy-done.3, ...), custom_call_target="tpu_custom_call" | custom-call | flops 2000000000 | bytes 8000000 | tf_op jit(solution)/shard_map/gram_h/pallas_call | solution.py:162
  257.4 0.0 all-to-all-done.2
  257.4 1.1 reshape.211
  258.6 0.9 gather_fusion
  259.5 0.2 select_bitcast_fusion
  259.6 0.1 slice_add_fusion
  259.8 0.1 add.197
  259.9 0.1 sub.76
  260.0 0.0 copy-done.4
  260.0 0.4 reshape.210
  260.4 0.4 fusion.5
  260.9 0.1 add.191
  261.0 0.1 sub.70
  261.1 0.2 reshape.237
  261.3 16.3 %all_to_all.25 = f32[16,1,1024]{2,1,0:T(1,128)S(1)} all-to-all(f32[16,1,1024]{2,1,0:T(1,128)S(1)} %reshape.237), channel_id=1, replica_groups=mesh['band'=8,'fft'=16] {'fft'}, dimensions={0} | all-to-all | bytes 131072 | tf_op jit(solution)/shard_map/all_to_all | solution.py:187
  277.6 0.5 broadcast.235
  278.1 0.8 reduce.10
  278.9 0.2 reshape.238
  279.2 0.7 reshape.239
  280.0 7.2 %all-to-all-start.4 = ((f32[8,1,1024]{2,1,0:T(1,128)}), f32[8,1,1024]{2,1,0:T(1,128)S(1)}, u32[]{:S(2)}, u32[]{:S(2)}) async-start(f32[8,1,1024]{2,1,0:T(1,128)} %reshape.239), calls=%async_computation.4 | async-start | bytes 65536 | tf_op jit(solution)/shard_map/all_to_all | solution.py:187
  287.1 9.4 %z_backward.1 = bf16[2,480,1920]{2,1,0:T(8,128)(2,1)} custom-call(bf16[16,2,2,16,1920]{4,3,2,1,0:T(8,128)(2,1)} %bitcast.16.wire_ref, f32[1,1920]{1,0:T(1,128)} %reshape.212.live_ref, bf16[480,512]{1,0:T(8,128)(2,1)} %constant.197.clone.table_ref), custom_call_target="tpu_custom_call" | custom-call | flops 1800000000 | bytes 8000000 | tf_op jit(solution)/shard_map/z_backward/pallas_call | solution.py:105
  296.5 0.0 all-to-all-done.4
  296.5 0.7 reduce.11
  297.2 0.1 reshape.240
  297.4 0.6 fusion.11
  (15 shorter events, 0.3 us)
Async XLA Ops:
  12.3 8.3 %copy-start = (s32[30720]{0:T(1024)S(1)}, s32[30720]{0:T(1024)}, u32[]{:S(2)}) copy-start(s32[30720]{0:T(1024)} %param.12) | copy-start | bytes 368644
  12.3 65.8 %all-to-all-start = ((bf16[16,64,1920]{2,1,0:T(8,128)(2,1)}), bf16[16,64,1920]{2,1,0:T(8,128)(2,1)}, u32[]{:S(2)}, u32[]{:S(2)}) async-start(bf16[16,64,1920]{2,1,0:T(8,128)(2,1)} %bitcast.50), calls=%async_computation | async-start | bytes 7864320 | tf_op jit(solution)/shard_map/all_to_all | solution.py:438
  82.5 106.3 %all-to-all-start.1 = ((bf16[8,256,1920]{2,1,0:T(8,128)(2,1)}), bf16[8,256,1920]{2,1,0:T(8,128)(2,1)}, u32[]{:S(2)}, u32[]{:S(2)}) async-start(bf16[8,256,1920]{2,1,0:T(8,128)(2,1)} %bitcast_dynamic-update-slice_fusion), calls=%async_computation.1 | async-start | bytes 15728640 | tf_op jit(solution)/shard_map/all_to_all | solution.py:443
  188.8 68.6 %all-to-all-start.2 = ((bf16[16,64,1920]{2,1,0:T(8,128)(2,1)}), bf16[16,64,1920]{2,1,0:T(8,128)(2,1)}, u32[]{:S(2)}, u32[]{:S(2)}) async-start(bf16[16,64,1920]{2,1,0:T(8,128)(2,1)} %planes.1), calls=%async_computation.2 | async-start | bytes 7864320 | tf_op jit(solution)/shard_map/all_to_all | solution.py:445
  202.6 14.1 %collective-permute-start = (bf16[2,2,2,16,1920]{4,3,2,1,0:T(8,128)(2,1)S(1)}, bf16[2,2,2,16,1920]{4,3,2,1,0:T(8,128)(2,1)S(1)}, u32[]{:S(2)}, u32[]{:S(2)}) collective-permute-start(bf16[2,2,2,16,1920]{4,3,2,1,0:T(8,128)(2,1)S(1)} %get-tuple-element.49), channel_id=1, source_target_pairs={{0,16},{16,32},{32,48},{48,64},{64,80},{80,96},{96,112},{112,0},{1... | collective-permute-start | bytes 1474568 | tf_op jit(solution)/shard_map/ppermute | solution.py:197
  202.7 16.0 %collective-permute-start.1 = (bf16[2,2,2,16,1920]{4,3,2,1,0:T(8,128)(2,1)S(1)}, bf16[2,2,2,16,1920]{4,3,2,1,0:T(8,128)(2,1)S(1)}, u32[]{:S(2)}, u32[]{:S(2)}) collective-permute-start(bf16[2,2,2,16,1920]{4,3,2,1,0:T(8,128)(2,1)S(1)} %get-tuple-element.48), channel_id=1, source_target_pairs={{0,32},{16,48},{32,64},{48,80},{64,96},{80,112},{96,0},{112,16},{1... | collective-permute-start | bytes 1474568 | tf_op jit(solution)/shard_map/ppermute | solution.py:197
  204.6 38.6 %collective-permute-start.2 = (bf16[2,2,2,16,1920]{4,3,2,1,0:T(8,128)(2,1)S(1)}, bf16[2,2,2,16,1920]{4,3,2,1,0:T(8,128)(2,1)S(1)}, u32[]{:S(2)}, u32[]{:S(2)}) collective-permute-start(bf16[2,2,2,16,1920]{4,3,2,1,0:T(8,128)(2,1)S(1)} %get-tuple-element.47), channel_id=1, source_target_pairs={{0,48},{16,64},{32,80},{48,96},{64,112},{80,0},{96,16},{112,32},{1... | collective-permute-start | bytes 1474568 | tf_op jit(solution)/shard_map/ppermute | solution.py:197
  206.7 36.5 %collective-permute-start.3 = (bf16[2,2,2,16,1920]{4,3,2,1,0:T(8,128)(2,1)S(1)}, bf16[2,2,2,16,1920]{4,3,2,1,0:T(8,128)(2,1)}, u32[]{:S(2)}, u32[]{:S(2)}) collective-permute-start(bf16[2,2,2,16,1920]{4,3,2,1,0:T(8,128)(2,1)S(1)} %get-tuple-element.46), channel_id=1, source_target_pairs={{0,64},{16,80},{32,96},{48,112},{64,0},{80,16},{96,32},{112,48},{1... | collective-permute-start | bytes 1474568 | tf_op jit(solution)/shard_map/ppermute | solution.py:197
  208.7 38.4 %collective-permute-start.4 = (bf16[2,2,2,16,1920]{4,3,2,1,0:T(8,128)(2,1)S(1)}, bf16[2,2,2,16,1920]{4,3,2,1,0:T(8,128)(2,1)}, u32[]{:S(2)}, u32[]{:S(2)}) collective-permute-start(bf16[2,2,2,16,1920]{4,3,2,1,0:T(8,128)(2,1)S(1)} %get-tuple-element.45), channel_id=1, source_target_pairs={{0,80},{16,96},{32,112},{48,0},{64,16},{80,32},{96,48},{112,64},{1... | collective-permute-start | bytes 1474568 | tf_op jit(solution)/shard_map/ppermute | solution.py:197
  216.8 18.0 %copy-start.1 = (bf16[2,2,2,16,1920]{4,3,2,1,0:T(8,128)(2,1)}, bf16[2,2,2,16,1920]{4,3,2,1,0:T(8,128)(2,1)S(1)}, u32[]{:S(2)}) copy-start(bf16[2,2,2,16,1920]{4,3,2,1,0:T(8,128)(2,1)S(1)} %collective-permute-done.refs_1_) | copy-start | bytes 1474564
  216.8 30.4 %collective-permute-start.5 = (bf16[2,2,2,16,1920]{4,3,2,1,0:T(8,128)(2,1)S(1)}, bf16[2,2,2,16,1920]{4,3,2,1,0:T(8,128)(2,1)}, u32[]{:S(2)}, u32[]{:S(2)}) collective-permute-start(bf16[2,2,2,16,1920]{4,3,2,1,0:T(8,128)(2,1)S(1)} %get-tuple-element.44), channel_id=1, source_target_pairs={{0,96},{16,112},{32,0},{48,16},{64,32},{80,48},{96,64},{112,80},{1... | collective-permute-start | bytes 1474568 | tf_op jit(solution)/shard_map/ppermute | solution.py:197
  218.7 16.1 %copy-start.2 = (bf16[2,2,2,16,1920]{4,3,2,1,0:T(8,128)(2,1)}, bf16[2,2,2,16,1920]{4,3,2,1,0:T(8,128)(2,1)S(1)}, u32[]{:S(2)}) copy-start(bf16[2,2,2,16,1920]{4,3,2,1,0:T(8,128)(2,1)S(1)} %collective-permute-done.1.refs_2_) | copy-start | bytes 1474564
  218.7 30.4 %collective-permute-start.6 = (bf16[2,2,2,16,1920]{4,3,2,1,0:T(8,128)(2,1)S(1)}, bf16[2,2,2,16,1920]{4,3,2,1,0:T(8,128)(2,1)}, u32[]{:S(2)}, u32[]{:S(2)}) collective-permute-start(bf16[2,2,2,16,1920]{4,3,2,1,0:T(8,128)(2,1)S(1)} %get-tuple-element.43), channel_id=1, source_target_pairs={{0,112},{16,0},{32,16},{48,32},{64,48},{80,64},{96,80},{112,96},{1... | collective-permute-start | bytes 1474568 | tf_op jit(solution)/shard_map/ppermute | solution.py:197
  243.2 5.9 %copy-start.3 = (bf16[2,2,2,16,1920]{4,3,2,1,0:T(8,128)(2,1)}, bf16[2,2,2,16,1920]{4,3,2,1,0:T(8,128)(2,1)S(1)}, u32[]{:S(2)}) copy-start(bf16[2,2,2,16,1920]{4,3,2,1,0:T(8,128)(2,1)S(1)} %collective-permute-done.2.refs_3_) | copy-start | bytes 1474564
  249.1 11.0 %copy-start.4 = (f32[32,32]{1,0:T(8,128)S(1)}, f32[32,32]{1,0:T(8,128)}, u32[]{:S(2)}) copy-start(f32[32,32]{1,0:T(8,128)} %gram_s.1) | copy-start | bytes 12292
  280.0 16.5 %all-to-all-start.4 = ((f32[8,1,1024]{2,1,0:T(1,128)}), f32[8,1,1024]{2,1,0:T(1,128)S(1)}, u32[]{:S(2)}, u32[]{:S(2)}) async-start(f32[8,1,1024]{2,1,0:T(1,128)} %reshape.239), calls=%async_computation.4 | async-start | bytes 65536 | tf_op jit(solution)/shard_map/all_to_all | solution.py:187

commit v3 on v2

--- a/solution.py
+++ b/solution.py
@@ -20,11 +20,11 @@
 HALF = BOX // 2
 PAIRS = GRID // 2
 ROWS = BOX * BOX
-BLOCK = 384
 PITCH = 200
 PITCHB = 120
+PB = 24
 N1 = 8
-N2 = 8
+N2 = 12
 N4 = 8
 MIB = 1 << 20
 
@@ -58,35 +58,35 @@
     return z_forward, z_backward, forward, backward
 
 
-def z_forward_kernel(orbit_ref, live_ref, table_ref, wire_ref, share_ref):
-    masked = (orbit_ref[0].astype(jnp.float32) * live_ref[...]).astype(jnp.bfloat16)
-    values = jnp.dot(table_ref[...], masked, preferred_element_type=jnp.float32).astype(jnp.bfloat16)
-    lanes = values.shape[-1]
-    wire_ref[...] = values.reshape(GROUPS, 2, 1, ZPAD, lanes)
+def z_forward_kernel(orbit_ref, live_ref, table_ref, wire_ref, share_ref, masked_ref):
+    masked_ref[...] = (orbit_ref[0].astype(jnp.float32) * live_ref[...]).astype(jnp.bfloat16)
     for c in range(2):
         for q in range(15):
-            share_ref[q // 2, q % 2, c, 0] = masked[c * GRID + q * 16 : c * GRID + q * 16 + 16]
-        share_ref[7, 1, c, 0] = jnp.zeros((16, lanes), jnp.bfloat16)
+            start = c * GRID + q * 16
+            share_ref[q // 2, q % 2, c, 0] = masked_ref[start : start + 16]
+        share_ref[7, 1, c, 0] = jnp.zeros((16, SLOTS), jnp.bfloat16)
+    values = jnp.dot(table_ref[...], masked_ref[...], preferred_element_type=jnp.float32).astype(jnp.bfloat16)
+    wire_ref[...] = values.reshape(GROUPS, 2, 1, ZPAD, SLOTS)
 
 
 def z_forward_call(orbits, live, table):
-    lanes = BLOCK
     return pl.pallas_call(
         z_forward_kernel,
-        grid=(2, SLOTS // lanes),
+        grid=(2,),
         in_specs=[
-            pl.BlockSpec((1, 2 * GRID, lanes), lambda b, t: (b, 0, t)),
-            pl.BlockSpec((1, lanes), lambda b, t: (0, t)),
-            pl.BlockSpec((512, 2 * GRID), lambda b, t: (0, 0)),
+            pl.BlockSpec((1, 2 * GRID, SLOTS), lambda b: (b, 0, 0)),
+            pl.BlockSpec((1, SLOTS), lambda b: (0, 0)),
+            pl.BlockSpec((512, 2 * GRID), lambda b: (0, 0)),
         ],
         out_specs=[
-            pl.BlockSpec((GROUPS, 2, 1, ZPAD, lanes), lambda b, t: (0, 0, b, 0, t)),
-            pl.BlockSpec((8, 2, 2, 1, 16, lanes), lambda b, t: (0, 0, 0, b, 0, t)),
+            pl.BlockSpec((GROUPS, 2, 1, ZPAD, SLOTS), lambda b: (0, 0, b, 0, 0)),
+            pl.BlockSpec((8, 2, 2, 1, 16, SLOTS), lambda b: (0, 0, 0, b, 0, 0)),
         ],
         out_shape=[
             jax.ShapeDtypeStruct((GROUPS, 2, 2, ZPAD, SLOTS), jnp.bfloat16),
-            jax.ShapeDtypeStruct((8, 4, 2, 2, 16, SLOTS), jnp.bfloat16),
-        ],
+            jax.ShapeDtypeStruct((8, 2, 2, 2, 16, SLOTS), jnp.bfloat16),
+        ],
+        scratch_shapes=[pltpu.VMEM((2 * GRID, SLOTS), jnp.bfloat16)],
         compiler_params=pltpu.CompilerParams(vmem_limit_bytes=60 * MIB),
         cost_estimate=pl.CostEstimate(flops=1_800_000_000, bytes_accessed=12_000_000, transcendentals=0),
         name="z_forward",
@@ -94,23 +94,21 @@
 
 
 def z_backward_kernel(wire_ref, live_ref, table_ref, out_ref):
-    lanes = wire_ref.shape[-1]
-    values = wire_ref[...].reshape(512, lanes)
+    values = wire_ref[...].reshape(512, SLOTS)
     applied = jnp.dot(table_ref[...], values, preferred_element_type=jnp.float32)
     out_ref[0] = (applied * live_ref[...]).astype(jnp.bfloat16)
 
 
 def z_backward_call(wire, live, table):
-    lanes = BLOCK
     return pl.pallas_call(
         z_backward_kernel,
-        grid=(2, SLOTS // lanes),
+        grid=(2,),
         in_specs=[
-            pl.BlockSpec((GROUPS, 2, 1, ZPAD, lanes), lambda b, t: (0, 0, b, 0, t)),
-            pl.BlockSpec((1, lanes), lambda b, t: (0, t)),
-            pl.BlockSpec((2 * GRID, 512), lambda b, t: (0, 0)),
-        ],
-        out_specs=pl.BlockSpec((1, 2 * GRID, lanes), lambda b, t: (b, 0, t)),
+            pl.BlockSpec((GROUPS, 2, 1, ZPAD, SLOTS), lambda b: (0, 0, b, 0, 0)),
+            pl.BlockSpec((1, SLOTS), lambda b: (0, 0)),
+            pl.BlockSpec((2 * GRID, 512), lambda b: (0, 0)),
+        ],
+        out_specs=pl.BlockSpec((1, 2 * GRID, SLOTS), lambda b: (b, 0, 0)),
         out_shape=jax.ShapeDtypeStruct((2, 2 * GRID, SLOTS), jnp.bfloat16),
         compiler_params=pltpu.CompilerParams(vmem_limit_bytes=60 * MIB),
         cost_estimate=pl.CostEstimate(flops=1_800_000_000, bytes_accessed=8_000_000, transcendentals=0),
@@ -118,67 +116,71 @@
     )(wire, live, table)
 
 
-def gram_kernel(left_ref, *refs):
-    *right_refs, out_ref, total = refs
-    step = pl.program_id(0) * pl.num_programs(1) + pl.program_id(1)
-    lanes = left_ref.shape[-1]
-    left = left_ref[...].reshape(512, lanes)
-    right = jnp.concatenate([ref[...].reshape(512 // len(right_refs), lanes) for ref in right_refs], axis=0)
+def gram_kernel(me_ref, *refs, left_blocks, right_blocks, first_lane):
+    left_refs, right_refs = refs[:left_blocks], refs[left_blocks : left_blocks + right_blocks]
+    out_ref, total = refs[left_blocks + right_blocks :]
+    step = pl.program_id(0)
+    left = jnp.concatenate([ref[...].reshape(-1, SLOTS) for ref in left_refs], axis=0)
+    if right_blocks:
+        right = jnp.concatenate([ref[...].reshape(-1, SLOTS) for ref in right_refs], axis=0)
+    else:
+        right = left
     product = lax.dot_general(left, right, (((1,), (1,)), ((), ())), preferred_element_type=jnp.float32)
 
     @pl.when(step == 0)
     def _():
         total[...] = product
 
-    @pl.when(step > 0)
-    def _():
-        total[...] += product
-
-    @pl.when(step == pl.num_programs(0) * pl.num_programs(1) - 1)
+    def band_of(index, rotated):
+        source = index // 64
+        if rotated:
+            chip, core = me_ref[0] // 2, me_ref[0] % 2
+            source = (chip + 4 - source // 2) % 4 * 2 + (core + source) % 2
+        return source * 2 + index // 16 % 2
+
+    @pl.when(step == 1)
     def _():
         row = lax.broadcasted_iota(jnp.int32, (512, 512), 0)
         column = lax.broadcasted_iota(jnp.int32, (512, 512), 1)
-        diagonal = jnp.where(row % 16 == column % 16, total[...], 0.0)
-        pick_row = lax.broadcasted_iota(jnp.int32, (32, 512), 0)
-        pick_column = lax.broadcasted_iota(jnp.int32, (32, 512), 1)
-        pick = jnp.where(pick_column // 16 == pick_row, 1.0, 0.0)
-        by_row = jnp.dot(pick, diagonal, preferred_element_type=jnp.float32, precision=lax.Precision.HIGHEST)
+        diagonal = jnp.where(row % 16 == column % 16, total[...] + product, 0.0)
+        band = lax.broadcasted_iota(jnp.int32, (32, 512), 0)
+        index = lax.broadcasted_iota(jnp.int32, (32, 512), 1)
+        pick = (band % 16 == band_of(index, left_blocks > 1)) & (band // 16 == index // 32 % 2)
+        by_band = jnp.dot(
+            jnp.where(pick, 1.0, 0.0), diagonal, preferred_element_type=jnp.float32, precision=lax.Precision.HIGHEST
+        )
+        lane = lax.broadcasted_iota(jnp.int32, (128, 512), 0) - first_lane
+        index = lax.broadcasted_iota(jnp.int32, (128, 512), 1)
+        match = (lane >= 0) & (lane < 32) & (lane % 16 == band_of(index, right_blocks != 1))
+        part = index // 32 % 2
+        second = lane // 16 == 1
+        with_real = jnp.where(match & (part == jnp.where(second, 1, 0)), 1.0, 0.0)
+        with_imag = jnp.where(match & (part == jnp.where(second, 0, 1)), jnp.where(second, -1.0, 1.0), 0.0)
+        dims = (((1,), (1,)), ((), ()))
         out_ref[...] = lax.dot_general(
-            by_row,
-            pick,
-            (((1,), (1,)), ((), ())),
-            preferred_element_type=jnp.float32,
-            precision=lax.Precision.HIGHEST,
+            by_band[:16], with_real, dims, preferred_element_type=jnp.float32, precision=lax.Precision.HIGHEST
+        ) + lax.dot_general(
+            by_band[16:], with_imag, dims, preferred_element_type=jnp.float32, precision=lax.Precision.HIGHEST
         )
 
 
-def gram_call(left, rights, name):
-    lanes = 640
-    spec = pl.BlockSpec((8, 1, 2, 2, 16, lanes), lambda g, t: (0, g, 0, 0, 0, t))
-    if len(rights) == 1:
-        right_spec = spec
-    else:
-        right_spec = pl.BlockSpec((1, 2, 2, 16, lanes), lambda g, t: (g, 0, 0, 0, t))
+def gram_call(me, lefts, rights, first_lane, name):
+    whole = pl.BlockSpec((8, 1, 2, 2, 16, SLOTS), lambda g: (0, g, 0, 0, 0, 0))
+    piece = pl.BlockSpec((2, 1, 2, 2, 16, SLOTS), lambda g: (0, g, 0, 0, 0, 0))
+    specs = [whole if len(lefts) == 1 else piece] * len(lefts) + [whole if len(rights) == 1 else piece] * len(rights)
     return pl.pallas_call(
-        gram_kernel,
-        grid=(2, SLOTS // lanes),
-        in_specs=[spec] + [right_spec] * len(rights),
-        out_specs=pl.BlockSpec((32, 32), lambda g, t: (0, 0)),
-        out_shape=jax.ShapeDtypeStruct((32, 32), jnp.float32),
+        functools.partial(
+            gram_kernel, left_blocks=len(lefts), right_blocks=len(rights), first_lane=first_lane
+        ),
+        grid=(2,),
+        in_specs=[pl.BlockSpec(memory_space=pltpu.SMEM)] + specs,
+        out_specs=pl.BlockSpec((16, 128), lambda g: (0, 0)),
+        out_shape=jax.ShapeDtypeStruct((16, 128), jnp.float32),
         scratch_shapes=[pltpu.VMEM((512, 512), jnp.float32)],
         compiler_params=pltpu.CompilerParams(vmem_limit_bytes=60 * MIB),
         cost_estimate=pl.CostEstimate(flops=2_000_000_000, bytes_accessed=8_000_000, transcendentals=0),
         name=name,
-    )(left, *rights)
-
-
-def matrices(product, order=None):
-    parts = product.reshape(8, 2, 2, 8, 2, 2)
-    if order is not None:
-        parts = jnp.take(parts, order, axis=3)
-    first = parts[:, 0, :, :, 0, :] + parts[:, 1, :, :, 1, :]
-    second = parts[:, 0, :, :, 1, :] - parts[:, 1, :, :, 0, :]
-    return jnp.stack([first.reshape(16, 16), second.reshape(16, 16)])
+    )(me, *lefts, *rights)
 
 
 def summed(values, axis):
@@ -188,31 +190,36 @@
 
 
 def spread_blocks(blocks, axis):
-    size = lax.axis_size(axis)
     me = lax.axis_index(axis)
+    chip, core = me // 2, me % 2
+    halves = blocks.reshape((4, 2) + blocks.shape[1:])
+    kept = lax.dynamic_index_in_dim(halves, core, 1, keepdims=False)
+    given = lax.dynamic_index_in_dim(halves, 1 - core, 1, keepdims=False)
+    got = lax.ppermute(given, axis, [(i, i ^ 1) for i in range(8)])
     result = []
-    for shift in range(size):
-        block = lax.dynamic_index_in_dim(blocks, (me + shift) % size, 0, keepdims=False)
+    for shift in range(4):
+        target = (chip + shift) % 4
+        pair = jnp.concatenate(
+            [lax.dynamic_slice_in_dim(kept, target, 1, 0), lax.dynamic_slice_in_dim(got, target, 1, 0)], axis=0
+        )
         if shift:
-            block = lax.ppermute(block, axis, [(i, (i + shift) % size) for i in range(size)])
-        result.append(block)
-    return result, (me - jnp.arange(size)) % size
+            pair = lax.ppermute(pair, axis, [(i, (i // 2 + shift) % 4 * 2 + i % 2) for i in range(8)])
+        result.append(pair)
+    return result
 
 
 def plane_kernel(
-    place_ref, pick_ref, count_ref, upper_ref, wire_ref, field_ref, forward_ref, backward_ref, out_ref,
-    grid_ref, mid_ref, stage_a, stage_b, list_ref
+    place_ref, count_ref, upper_ref, wire_ref, field_ref, forward_ref, backward_ref, out_ref,
+    grid_ref, mid_ref, back_ref, stage_a, stage_b, list_ref
 ):
     step = pl.program_id(0)
     lane = lax.broadcasted_iota(jnp.int32, (1, 128), 1)
     low = lane % 64 < 32
-    sign = jnp.where(lane < 64, -1.0, 1.0)
-
-    def turned(values):
-        return pltpu.roll(values, 64, 1) * sign
+    sign = jnp.where(lane < 64, -1.0, 1.0).astype(jnp.bfloat16)
 
     def doubled(values):
-        return jnp.concatenate([values, turned(values)], axis=0).astype(jnp.bfloat16)
+        values = values.astype(jnp.bfloat16)
+        return jnp.concatenate([values, pltpu.roll(values, 64, 1) * sign], axis=0)
 
     def exchange(first, second):
         return (
@@ -227,6 +234,7 @@
             return carry
 
         lax.fori_loop(0, ROWS // 512, clear, 0)
+        grid_ref[pl.ds(ROWS, 8), :] = jnp.zeros((8, 128), jnp.float32)
 
         def group(p, total):
             def note(t, inner):
@@ -287,7 +295,7 @@
     def y_steps(i, carry):
         parts = []
         for j in range(N2):
-            pair = step * 8 + i * N2 + j
+            pair = step * PB + i * N2 + j
             base = pl.multiple_of(pair * PITCH, 8)
             first = mid_ref[pl.ds(base, HALF), :]
             second = mid_ref[pl.ds(base + HALF, HALF), :]
@@ -299,11 +307,11 @@
             parts.append(doubled(spatial[:, j * 128 : (j + 1) * 128] * field_ref[i * N2 + j]))
         result = jnp.dot(backward_ref[...], jnp.concatenate(parts, axis=1), preferred_element_type=jnp.float32)
         for j in range(N2):
-            pair = step * 8 + i * N2 + j
-            grid_ref[pl.ds(pair, BOX, stride=PITCHB), :] = result[:, j * 128 : (j + 1) * 128]
+            pair = step * PB + i * N2 + j
+            back_ref[pl.ds(pair, BOX, stride=PITCHB), :] = result[:, j * 128 : (j + 1) * 128]
         return carry
 
-    lax.fori_loop(0, 8 // N2, y_steps, 0)
+    lax.fori_loop(0, PB // N2, y_steps, 0)
 
     @pl.when(step == pl.num_programs(0) - 1)
     def _():
@@ -311,14 +319,16 @@
             parts = []
             for j in range(N4):
                 k = i * N4 + j
-                first = grid_ref[pl.ds(pl.multiple_of(k * PITCHB, 8), PAIRS), :]
-                second = grid_ref[pl.ds(pl.multiple_of((k + HALF) * PITCHB, 8), PAIRS), :]
+                first = back_ref[pl.ds(pl.multiple_of(k * PITCHB, 8), PAIRS), :]
+                second = back_ref[pl.ds(pl.multiple_of((k + HALF) * PITCHB, 8), PAIRS), :]
                 even, odd = exchange(first, second)
                 parts.append(doubled(jnp.concatenate([even, odd], axis=0)))
             result = jnp.dot(backward_ref[...], jnp.concatenate(parts, axis=1), preferred_element_type=jnp.float32)
             for j in range(N4):
                 k = i * N4 + j
-                mid_ref[pl.ds(pl.multiple_of(k * BOX, BOX), BOX), :] = result[:, j * 128 : (j + 1) * 128]
+                part = result[:, j * 128 : (j + 1) * 128]
+                grid_ref[pl.ds(pl.multiple_of(k * BOX, BOX), BOX), :] = part
+                grid_ref[pl.ds(pl.multiple_of((k + HALF) * BOX, BOX), BOX), :] = part
             return carry
 
         lax.fori_loop(0, HALF // N4, x_backward, 0)
@@ -330,7 +340,7 @@
 
         def gather(entry, stage):
             for u in range(128):
-                stage[pl.ds(origin + u, 1), :] = mid_ref[pl.ds(pick_ref[entry * 128 + u], 1), :]
+                stage[pl.ds(origin + u, 1), :] = grid_ref[pl.ds(place_ref[entry * 128 + u], 1), :]
 
         def write(entry, stage):
             p = entry // 15
@@ -363,18 +373,17 @@
         lax.fori_loop(0, list_ref[255], pick, 0)
 
 
-def plane_call(place, pick, count, upper, wire, field, forward, backward):
+def plane_call(place, count, upper, wire, field, forward, backward):
     whole = lambda shape: pl.BlockSpec(shape, lambda i: (0,) * len(shape), pipeline_mode=pl.Buffered(1))
     return pl.pallas_call(
         plane_kernel,
-        grid=(PAIRS // 8,),
+        grid=(PAIRS // PB,),
         in_specs=[
-            pl.BlockSpec(memory_space=pltpu.SMEM),
             pl.BlockSpec(memory_space=pltpu.SMEM),
             pl.BlockSpec(memory_space=pltpu.SMEM),
             whole((GROUPS * SLOTS // 128, 128)),
             whole((GROUPS, 64, SLOTS)),
-            pl.BlockSpec((8, GRID, 128), lambda i: (i, 0, 0)),
+            pl.BlockSpec((PB, GRID, 128), lambda i: (i, 0, 0)),
             whole((GRID, 2 * BOX)),
             whole((BOX, 2 * GRID)),
         ],
@@ -383,14 +392,15 @@
         scratch_shapes=[
             pltpu.VMEM((ROWS + 8, 128), jnp.float32),
             pltpu.VMEM((PAIRS * PITCH, 128), jnp.float32),
+            pltpu.VMEM((BOX * PITCHB, 128), jnp.float32),
             pltpu.VMEM((128, 128), jnp.float32),
             pltpu.VMEM((128, 128), jnp.float32),
             pltpu.SMEM((256,), jnp.int32),
         ],
-        compiler_params=pltpu.CompilerParams(vmem_limit_bytes=56 * MIB),
+        compiler_params=pltpu.CompilerParams(vmem_limit_bytes=62 * MIB),
         cost_estimate=pl.CostEstimate(flops=13_000_000_000, bytes_accessed=24_000_000, transcendentals=0),
         name="planes",
-    )(place, pick, count, upper, wire, field, forward, backward)
+    )(place, count, upper, wire, field, forward, backward)
 
 
 def field_kernel(lower_ref, upper_ref, out_ref):
@@ -428,30 +438,27 @@
     box_y = jnp.where(column_y < GRID // 2, column_y + HALF, column_y - (GRID - HALF))
     place = jnp.where(live_all, box_y * BOX + box_x, ROWS)
     count = (jnp.sum(live_all.reshape(GROUPS, SLOTS).astype(jnp.int32), axis=1) + 127) // 128
-    upper = live_all & (box_y >= HALF)
-    choose = jnp.where(live_all, jnp.where(upper, box_y - HALF, box_y) * BOX + box_x, 0)
-    upper = upper.astype(jnp.float32).reshape(GROUPS * SLOTS // 128, 128)
+    upper = (live_all & (box_y >= HALF)).astype(jnp.float32).reshape(GROUPS * SLOTS // 128, 128)
+    me = lax.axis_index("band").astype(jnp.int32)[None]
     field = field_call(potential)
 
     wire, share = z_forward_call(orbitals.transpose(0, 2, 1), live, z_forward)
-    share = share.reshape(8, 256, SLOTS)
     incoming = lax.all_to_all(wire.reshape(GROUPS, 64, SLOTS), "fft", split_axis=0, concat_axis=0, tiled=True)
-    share, field, place, choose, count, upper = lax.optimization_barrier(
-        (share, field, place, choose, count, upper)
+    shares = spread_blocks(share, "band")
+    incoming, field, place, count, upper, *shares = lax.optimization_barrier(
+        (incoming, field, place, count, upper, *shares)
     )
-    shared = share.at[:, 128:].set(incoming.reshape(8, 128, SLOTS))
-    shared = lax.all_to_all(shared, "band", split_axis=0, concat_axis=0, tiled=True)
-    outgoing = plane_call(place, choose, count, upper, incoming, field, forward, backward)
+    left = lax.all_to_all(incoming.reshape(8, 128, SLOTS), "band", split_axis=0, concat_axis=0, tiled=True)
+    outgoing = plane_call(place, count, upper, incoming, field, forward, backward)
     returned = lax.all_to_all(outgoing, "fft", split_axis=0, concat_axis=0, tiled=True)
-    rights, order = spread_blocks(outgoing.reshape(8, 2, 2, 2, 16, SLOTS), "band")
-    share = shared[:, :128].reshape(8, 2, 2, 2, 16, SLOTS)
-    left = shared[:, 128:].reshape(8, 2, 2, 2, 16, SLOTS)
-    product_s = gram_call(share, [share], "gram_s")
-    product_h = gram_call(left, rights, "gram_h")
-    product_s, product_h, returned = lax.optimization_barrier((product_s, product_h, returned))
+    rights = spread_blocks(outgoing.reshape(8, 2, 2, 2, 16, SLOTS), "band")
+    product_h = gram_call(me, [left.reshape(8, 2, 2, 2, 16, SLOTS)], rights, 32, "gram_h")
+    product_s = gram_call(me, shares, [], 0, "gram_s")
+    product_h, product_s, returned = lax.optimization_barrier((product_h, product_s, returned))
+    products = product_s + product_h
     applied = z_backward_call(returned.reshape(GROUPS, 2, 2, ZPAD, SLOTS), live, z_backward)
-    products = jnp.concatenate([matrices(product_s), matrices(product_h, order)])
-    products = summed(summed(products, "fft"), "band") * (1.0 / (2.0 * STICKS * GRID))
+    products = summed(summed(products, "band"), "fft") * (1.0 / (2.0 * STICKS * GRID))
+    products = products[:, :64].reshape(16, 4, 16).transpose(1, 0, 2)
     return (applied.transpose(0, 2, 1), products[0:2], products[2:4])
 
 

time: 301 us -> 277 us (0.920)
  Pallas kernels: 152 us -> 125 us
  waiting for transfers between devices: 53.7 us -> 79.9 us
  starting transfers between devices: 50.8 us -> 39.8 us
  blocking collectives: 16.3 us -> 7.98 us
  local copies, waits for them, and re-layouts: 19.3 us -> 14.1 us
    ppermute x7 -> x8, waiting for transfers between devices: 12.3 us -> 77.3 us  [the longest x6 77.3 us: spread_blocks(): lax.ppermute(pair, axis, [(i, (i // 2 + shift) % 4 * 2 + i % 2) for i in...]
    all_to_all x1, waiting for transfers between devices: 41.3 us -> 0.01 us  [local(): lax.all_to_all(wire.reshape(GROUPS, 64, SLOTS), 'fft', split_axis=0, conc...]
    pallas_call x5, Pallas kernels: 138 us -> 111 us  [the longest x1 87.1 us: plane_call(): pl.pallas_call(plane_kernel, grid=(PAIRS // PB,), in_specs=[pl.BlockSpec(...]
    ppermute x7 -> x8, starting transfers between devices: 19.9 us -> 9.71 us  [the longest x6 9.35 us: spread_blocks(): lax.ppermute(pair, axis, [(i, (i // 2 + shift) % 4 * 2 + i % 2) for i in...]
    all_to_all x1, blocking collectives: 16.3 us -> 7.98 us  [summed(): lax.all_to_all(copies, axis, split_axis=0, concat_axis=0, tiled=True)]
    slice x1 -> x0, local copies, waits for them, and re-layouts: 5.72 us -> none  [local(): left = shared[:, 128:].reshape(8, 2, 2, 2, 16, SLOTS)]
    concatenate x1 -> x8, other arithmetic: 0.01 us -> 4.69 us  [spread_blocks(): jnp.concatenate([lax.dynamic_slice_in_dim(kept, target, 1, 0), lax.dynami...]
    scatter x1 -> x0, local copies, waits for them, and re-layouts: 4.42 us -> none  [local(): shared = share.at[:, 128:].set(incoming.reshape(8, 128, SLOTS))]
  transfers between devices with their start and end apart: 11 -> 12, of which waited for: 4 -> 5; matrix products, arithmetic and copies ran while one was open for 4% -> 5% of each run, Pallas kernels for 47% -> 43%
where the time goes in v3:
time: 277 us; the launch traced here: 276 us
  Pallas kernels  125 us (45%)
  waiting for transfers between devices  79.9 us (29%)
  starting transfers between devices  39.8 us (14%)
  local copies, waits for them, and re-layouts  14.1 us (5%)
  other arithmetic  8.42 us (3%)
  blocking collectives  7.98 us (3%)
    pallas_call x1, Pallas kernels, plane_call(): pl.pallas_call(plane_kernel, grid=(PAIRS // PB,), in_specs=[pl.BlockSpec(...  87.1 us
    ppermute x6, waiting for transfers between devices, spread_blocks(): lax.ppermute(pair, axis, [(i, (i // 2 + shift) % 4 * 2 + i % 2) for i in...  77.3 us
    pallas_call x1, Pallas kernels, field_call(): pl.pallas_call(field_kernel, grid=(PAIRS // 8,), in_specs=[pl.BlockSpec((...  13.9 us
    pallas_call x2, Pallas kernels, gram_call(): pl.pallas_call(functools.partial(gram_kernel, left_blocks=len(lefts), rig...  12.4 us
    all_to_all x1, starting transfers between devices, summed(): lax.all_to_all(copies, axis, split_axis=0, concat_axis=0, tiled=True)  10.5 us
    ppermute x6, starting transfers between devices, spread_blocks(): lax.ppermute(pair, axis, [(i, (i // 2 + shift) % 4 * 2 + i % 2) for i in...  9.35 us
    all_to_all x1, starting transfers between devices, local(): lax.all_to_all(wire.reshape(GROUPS, 64, SLOTS), 'fft', split_axis=0, conc...  8.29 us
    all_to_all x1, blocking collectives, summed(): lax.all_to_all(copies, axis, split_axis=0, concat_axis=0, tiled=True)  7.98 us
  transfers between devices with their start and end apart: 12, of which 5 were waited for; matrix products, arithmetic and copies ran while one was open for 5% of the time, Pallas kernels for 43%

profile of v3, /device:TPU:0, one launch (start us, length us, event | category | flops | bytes accessed | tf_op | source)
XLA Modules:
  0.0 276.0 jit_solution(6188303569524178888)
XLA Ops:
  0.6 0.8 fusion.2
  1.4 0.6 reshape.51.live_ref
  2.0 6.3 %z_forward.1 = (bf16[16,2,2,16,1920]{4,3,2,1,0:T(8,128)(2,1)}, bf16[8,2,2,2,16,1920]{5,4,3,2,1,0:T(8,128)(2,1)}) custom-call(bf16[2,480,1920]{2,1,0:T(8,128)(2,1)} %bitcast.39, f32[1,1920]{1,0:T(1,128)} %reshape.51.live_ref, bf16[512,480]{1,0:T(8,128)(2,1)} %constant.398.clone.table_ref), custom_call_target="tpu_custom_call" | custom-call | flops 1800000000 | bytes 12000000 | tf_op jit(solution)/shard_map/z_forward/pallas_call | solution.py:73
  8.3 3.0 %dynamic-slice_bitcast_fusion.1 = bf16[4,2,2,2,16,1920]{5,4,3,2,1,0:T(8,128)(2,1)} fusion(bf16[4,2,2,2,2,16,1920]{6,5,4,3,2,1,0:T(8,128)(2,1)} %bitcast.35, s32[]{:T(128)S(6)} %select_n.124), kind=kLoop, calls=%fused_computation.1 | loop fusion | bytes 3932164 | tf_op jit(solution)/shard_map/jit(dynamic_index_in_dim)/squeeze | solution.py:197
  11.3 0.0 collective-permute-start
  11.3 0.0 copy-start.3
  11.3 8.3 %all-to-all-start = ((bf16[16,64,1920]{2,1,0:T(8,128)(2,1)}), bf16[16,64,1920]{2,1,0:T(8,128)(2,1)}, u32[]{:S(2)}, u32[]{:S(2)}) async-start(bf16[16,64,1920]{2,1,0:T(8,128)(2,1)} %bitcast.34), calls=%async_computation | async-start | bytes 7864320 | tf_op jit(solution)/shard_map/all_to_all | solution.py:446
  19.7 0.0 copy-done.3
  19.7 0.7 convert_bitcast_fusion
  20.5 0.1 reduce_sum.27
  20.6 13.9 %field.1.field_ref = f32[120,240,128]{2,1,0:T(8,128)} custom-call(f32[15,57600]{1,0:T(8,128)} %upper_ref.1, f32[15,57600]{1,0:T(8,128)} %upper_ref.1), custom_call_target="tpu_custom_call" | custom-call | bytes 18000000 | tf_op jit(solution)/shard_map/field/pallas_call | solution.py:416
  34.5 0.5 and_select_fusion.count_ref
  35.0 0.0 copy-done
  35.0 0.2 dynamic-slice_bitcast_fusion.6
  35.2 0.0 collective-permute-done
  35.2 1.6 constant_dynamic-slice_fusion.4
  36.8 0.1 pad_maximum_fusion.3
  37.0 2.8 %collective-permute-start.3 = (bf16[2,2,2,2,16,1920]{5,4,3,2,1,0:T(8,128)(2,1)S(1)}, bf16[2,2,2,2,16,1920]{5,4,3,2,1,0:T(8,128)(2,1)S(1)}, u32[]{:S(2)}, u32[]{:S(2)}) collective-permute-start(bf16[2,2,2,2,16,1920]{5,4,3,2,1,0:T(8,128)(2,1)S(1)} %pad_maximum_fusion.3), channel_id=1, source_target_pairs={{0,96},{16,112},{32,0},{48,16},{64,32},{80,48},{96,64},{112,80},{1... | collective-permute-start | bytes 2949128 | tf_op jit(solution)/shard_map/ppermute | solution.py:206
  39.8 0.1 pad_maximum_fusion.2
  39.9 0.9 collective-permute-start.2
  40.8 0.1 pad_maximum_fusion.1
  40.9 0.9 collective-permute-start.1
  41.8 0.8 add_select_fusion.2.place_ref
  42.7 1.1 pad_maximum_fusion.refs_0_
  43.7 38.6 %collective-permute-done.3.refs_3_ = bf16[2,2,2,2,16,1920]{5,4,3,2,1,0:T(8,128)(2,1)S(1)} collective-permute-done((bf16[2,2,2,2,16,1920]{5,4,3,2,1,0:T(8,128)(2,1)S(1)}, bf16[2,2,2,2,16,1920]{5,4,3,2,1,0:T(8,128)(2,1)S(1)}, u32[]{:S(2)}, u32[]{:S(2)}) %collective-permute-start.3) | collective-permute-done | bytes 983072 | tf_op jit(solution)/shard_map/ppermute | solution.py:206
  82.3 0.0 collective-permute-done.2.refs_2_
  82.3 1.0 copy-done.5
  83.3 1.0 copy-done.6
  84.3 2.0 collective-permute-done.1.refs_1_
  86.3 0.0 all-to-all-done.wire_ref
  86.3 4.5 %all-to-all-start.1 = ((bf16[8,128,1920]{2,1,0:T(8,128)(2,1)}), bf16[8,128,1920]{2,1,0:T(8,128)(2,1)}, u32[]{:S(2)}, u32[]{:S(2)}) async-start(bf16[8,128,1920]{2,1,0:T(8,128)(2,1)} %bitcast.10), calls=%async_computation.1 | async-start | bytes 7864320 | tf_op jit(solution)/shard_map/all_to_all | solution.py:451
  90.8 87.1 %planes.1 = bf16[16,64,1920]{2,1,0:T(8,128)(2,1)} custom-call(s32[30720]{0:T(1024)} %add_select_fusion.2.place_ref, s32[16]{0:T(128)} %and_select_fusion.count_ref, f32[240,128]{1,0:T(8,128)} %get-tuple-element.22.upper_ref, bf16[16,64,1920]{2,1,0:T(8,128)(2,1)} %all-to-all-done.wire_ref, f32[120,240,128]{2,1,0:T(8,128)} %field.1.field_ref, ...), custom_call_target="tpu_custom_call" | custom-call | flops 12999999488 | bytes 24000000 | tf_op jit(solution)/shard_map/planes/pallas_call | solution.py:378
  177.9 3.0 %dynamic-slice_bitcast_fusion = bf16[4,2,2,2,16,1920]{5,4,3,2,1,0:T(8,128)(2,1)} fusion(bf16[4,2,2,2,2,16,1920]{6,5,4,3,2,1,0:T(8,128)(2,1)} %bitcast.32, s32[]{:T(128)S(6)} %select_n.124), kind=kLoop, calls=%fused_computation | loop fusion | bytes 3932164 | tf_op jit(solution)/shard_map/jit(dynamic_index_in_dim)/squeeze | solution.py:197
  180.9 0.3 collective-permute-start.4
  181.2 0.0 all-to-all-done.1
  181.2 6.8 %all-to-all-start.2 = ((bf16[16,64,1920]{2,1,0:T(8,128)(2,1)}), bf16[16,64,1920]{2,1,0:T(8,128)(2,1)}, u32[]{:S(2)}, u32[]{:S(2)}) async-start(bf16[16,64,1920]{2,1,0:T(8,128)(2,1)} %planes.1), calls=%async_computation.2 | async-start | bytes 7864320 | tf_op jit(solution)/shard_map/all_to_all | solution.py:453
  188.0 1.6 dynamic-slice_bitcast_fusion.2
  189.7 0.0 collective-permute-done.4
  189.7 0.2 constant_dynamic-slice_fusion
  189.9 0.1 pad_maximum_fusion.7
  190.0 3.0 %collective-permute-start.7 = (bf16[2,2,2,2,16,1920]{5,4,3,2,1,0:T(8,128)(2,1)S(1)}, bf16[2,2,2,2,16,1920]{5,4,3,2,1,0:T(8,128)(2,1)S(1)}, u32[]{:S(2)}, u32[]{:S(2)}) collective-permute-start(bf16[2,2,2,2,16,1920]{5,4,3,2,1,0:T(8,128)(2,1)S(1)} %pad_maximum_fusion.7), channel_id=1, source_target_pairs={{0,96},{16,112},{32,0},{48,16},{64,32},{80,48},{96,64},{112,80},{1... | collective-permute-start | bytes 2949128 | tf_op jit(solution)/shard_map/ppermute | solution.py:206
  192.9 1.1 pad_maximum_fusion.6
  194.0 0.8 collective-permute-start.6
  194.9 1.1 pad_maximum_fusion.5
  195.9 0.9 collective-permute-start.5
  196.8 5.8 %gram_s.1 = f32[16,128]{1,0:T(8,128)} custom-call(s32[1]{0:T(128)} %bitcast.me_ref, bf16[2,2,2,2,16,1920]{5,4,3,2,1,0:T(8,128)(2,1)} %pad_maximum_fusion.refs_0_, bf16[2,2,2,2,16,1920]{5,4,3,2,1,0:T(8,128)(2,1)} %collective-permute-done.1.refs_1_, bf16[2,2,2,2,16,1920]{5,4,3,2,1,0:T(8,128)(2,1)} %copy-done.6, bf16[2,2,2,2,16,1920]{5,4,3,2,1,0:T(8,128)(2,1)} %copy-done.5), custom_call_target="tpu_custom_call" | custom-call | flops 2000000000 | bytes 8000000 | tf_op jit(solution)/shard_map/gram_s/pallas_call | solution.py:171
  202.6 1.0 pad_maximum_fusion.4.refs_1_
  203.6 31.6 %collective-permute-done.7.refs_4_ = bf16[2,2,2,2,16,1920]{5,4,3,2,1,0:T(8,128)(2,1)S(1)} collective-permute-done((bf16[2,2,2,2,16,1920]{5,4,3,2,1,0:T(8,128)(2,1)S(1)}, bf16[2,2,2,2,16,1920]{5,4,3,2,1,0:T(8,128)(2,1)S(1)}, u32[]{:S(2)}, u32[]{:S(2)}) %collective-permute-start.7) | collective-permute-done | bytes 983072 | tf_op jit(solution)/shard_map/ppermute | solution.py:206
  235.2 0.0 collective-permute-done.6.refs_3_
  235.3 5.1 %collective-permute-done.5.refs_2_ = bf16[2,2,2,2,16,1920]{5,4,3,2,1,0:T(8,128)(2,1)} collective-permute-done((bf16[2,2,2,2,16,1920]{5,4,3,2,1,0:T(8,128)(2,1)}, bf16[2,2,2,2,16,1920]{5,4,3,2,1,0:T(8,128)(2,1)}, u32[]{:S(2)}, u32[]{:S(2)}) %collective-permute-start.5) | collective-permute-done | bytes 983072 | tf_op jit(solution)/shard_map/ppermute | solution.py:206
  240.4 0.0 copy-done.1
  240.4 0.0 copy-done.2
  240.4 6.6 %gram_h.1 = f32[16,128]{1,0:T(8,128)} custom-call(s32[1]{0:T(128)} %bitcast.me_ref, bf16[8,2,2,2,16,1920]{5,4,3,2,1,0:T(8,128)(2,1)} %bitcast.11.refs_0_, bf16[2,2,2,2,16,1920]{5,4,3,2,1,0:T(8,128)(2,1)} %pad_maximum_fusion.4.refs_1_, bf16[2,2,2,2,16,1920]{5,4,3,2,1,0:T(8,128)(2,1)} %collective-permute-done.5.refs_2_, ...), custom_call_target="tpu_custom_call" | custom-call | flops 2000000000 | bytes 8000000 | tf_op jit(solution)/shard_map/gram_h/pallas_call | solution.py:171
  247.0 0.0 all-to-all-done.2
  247.0 0.0 copy-done.4
  247.0 0.7 add.172
  247.7 8.0 %all_to_all.25 = f32[8,16,128]{2,1,0:T(8,128)S(1)} all-to-all(f32[8,16,128]{2,1,0:T(8,128)S(1)} %broadcast_in_dim.28), channel_id=1, replica_groups=mesh['band'=8,'fft'=16] {'band'}, dimensions={0} | all-to-all | bytes 131072 | tf_op jit(solution)/shard_map/all_to_all | solution.py:189
  255.7 0.6 broadcast_in_dim.29
  256.4 10.5 %all-to-all-start.4 = ((f32[16,16,128]{2,1,0:T(8,128)}), f32[16,16,128]{2,1,0:T(8,128)S(1)}, u32[]{:S(2)}, u32[]{:S(2)}) async-start(f32[16,16,128]{2,1,0:T(8,128)} %broadcast_in_dim.29), calls=%async_computation.4 | async-start | bytes 262144 | tf_op jit(solution)/shard_map/all_to_all | solution.py:189
  266.9 5.3 %z_backward.1 = bf16[2,480,1920]{2,1,0:T(8,128)(2,1)} custom-call(bf16[16,2,2,16,1920]{4,3,2,1,0:T(8,128)(2,1)} %bitcast.18.wire_ref, f32[1,1920]{1,0:T(1,128)} %reshape.51.live_ref, bf16[480,512]{1,0:T(8,128)(2,1)} %constant.399.clone.table_ref), custom_call_target="tpu_custom_call" | custom-call | flops 1800000000 | bytes 8000000 | tf_op jit(solution)/shard_map/z_backward/pallas_call | solution.py:103
  272.1 2.5 all-to-all-done.4
  274.7 0.1 reshape.50
  274.8 0.6 copy.12
  275.4 0.6 copy.13
  (12 shorter events, 0.1 us)
Async XLA Ops:
  11.3 23.9 %collective-permute-start = (bf16[4,2,2,2,16,1920]{5,4,3,2,1,0:T(8,128)(2,1)}, bf16[4,2,2,2,16,1920]{5,4,3,2,1,0:T(8,128)(2,1)}, u32[]{:S(2)}, u32[]{:S(2)}) collective-permute-start(bf16[4,2,2,2,16,1920]{5,4,3,2,1,0:T(8,128)(2,1)} %dynamic-slice_bitcast_fusion.1), channel_id=1, source_target_pairs={{0,16},{16,0},{32,48},{48,32},{64,80},{80,64},{96,112},{112,96},{1... | collective-permute-start | bytes 5898248 | tf_op jit(solution)/shard_map/ppermute | solution.py:198
  11.3 8.4 %copy-start.3 = (s32[30720]{0:T(1024)S(1)}, s32[30720]{0:T(1024)}, u32[]{:S(2)}) copy-start(s32[30720]{0:T(1024)} %param.10) | copy-start | bytes 368644
  11.3 75.0 %all-to-all-start = ((bf16[16,64,1920]{2,1,0:T(8,128)(2,1)}), bf16[16,64,1920]{2,1,0:T(8,128)(2,1)}, u32[]{:S(2)}, u32[]{:S(2)}) async-start(bf16[16,64,1920]{2,1,0:T(8,128)(2,1)} %bitcast.34), calls=%async_computation | async-start | bytes 7864320 | tf_op jit(solution)/shard_map/all_to_all | solution.py:446
  20.6 14.4 %copy-start = (bf16[8,2,2,2,16,1920]{5,4,3,2,1,0:T(8,128)(2,1)S(1)}, bf16[8,2,2,2,16,1920]{5,4,3,2,1,0:T(8,128)(2,1)}, u32[]{:S(2)}) copy-start(bf16[8,2,2,2,16,1920]{5,4,3,2,1,0:T(8,128)(2,1)} %get-tuple-element.18) | copy-start | bytes 11796484
  37.0 45.3 %collective-permute-start.3 = (bf16[2,2,2,2,16,1920]{5,4,3,2,1,0:T(8,128)(2,1)S(1)}, bf16[2,2,2,2,16,1920]{5,4,3,2,1,0:T(8,128)(2,1)S(1)}, u32[]{:S(2)}, u32[]{:S(2)}) collective-permute-start(bf16[2,2,2,2,16,1920]{5,4,3,2,1,0:T(8,128)(2,1)S(1)} %pad_maximum_fusion.3), channel_id=1, source_target_pairs={{0,96},{16,112},{32,0},{48,16},{64,32},{80,48},{96,64},{112,80},{1... | collective-permute-start | bytes 2949128 | tf_op jit(solution)/shard_map/ppermute | solution.py:206
  39.9 42.4 %collective-permute-start.2 = (bf16[2,2,2,2,16,1920]{5,4,3,2,1,0:T(8,128)(2,1)S(1)}, bf16[2,2,2,2,16,1920]{5,4,3,2,1,0:T(8,128)(2,1)S(1)}, u32[]{:S(2)}, u32[]{:S(2)}) collective-permute-start(bf16[2,2,2,2,16,1920]{5,4,3,2,1,0:T(8,128)(2,1)S(1)} %pad_maximum_fusion.2), channel_id=1, source_target_pairs={{0,64},{16,80},{32,96},{48,112},{64,0},{80,16},{96,32},{112,48},{1... | collective-permute-start | bytes 2949128 | tf_op jit(solution)/shard_map/ppermute | solution.py:206
  40.9 45.4 %collective-permute-start.1 = (bf16[2,2,2,2,16,1920]{5,4,3,2,1,0:T(8,128)(2,1)S(1)}, bf16[2,2,2,2,16,1920]{5,4,3,2,1,0:T(8,128)(2,1)}, u32[]{:S(2)}, u32[]{:S(2)}) collective-permute-start(bf16[2,2,2,2,16,1920]{5,4,3,2,1,0:T(8,128)(2,1)S(1)} %pad_maximum_fusion.1), channel_id=1, source_target_pairs={{0,32},{16,48},{32,64},{48,80},{64,96},{80,112},{96,0},{112,16},{1... | collective-permute-start | bytes 2949128 | tf_op jit(solution)/shard_map/ppermute | solution.py:206
  82.3 1.0 copy-start.5
  83.3 1.0 copy-start.6
  86.3 94.9 %all-to-all-start.1 = ((bf16[8,128,1920]{2,1,0:T(8,128)(2,1)}), bf16[8,128,1920]{2,1,0:T(8,128)(2,1)}, u32[]{:S(2)}, u32[]{:S(2)}) async-start(bf16[8,128,1920]{2,1,0:T(8,128)(2,1)} %bitcast.10), calls=%async_computation.1 | async-start | bytes 7864320 | tf_op jit(solution)/shard_map/all_to_all | solution.py:451
  180.9 8.8 %collective-permute-start.4 = (bf16[4,2,2,2,16,1920]{5,4,3,2,1,0:T(8,128)(2,1)}, bf16[4,2,2,2,16,1920]{5,4,3,2,1,0:T(8,128)(2,1)S(1)}, u32[]{:S(2)}, u32[]{:S(2)}) collective-permute-start(bf16[4,2,2,2,16,1920]{5,4,3,2,1,0:T(8,128)(2,1)} %dynamic-slice_bitcast_fusion), channel_id=1, source_target_pairs={{0,16},{16,0},{32,48},{48,32},{64,80},{80,64},{96,112},{112,96},{1... | collective-permute-start | bytes 5898248 | tf_op jit(solution)/shard_map/ppermute | solution.py:198
  181.2 65.8 %all-to-all-start.2 = ((bf16[16,64,1920]{2,1,0:T(8,128)(2,1)}), bf16[16,64,1920]{2,1,0:T(8,128)(2,1)}, u32[]{:S(2)}, u32[]{:S(2)}) async-start(bf16[16,64,1920]{2,1,0:T(8,128)(2,1)} %planes.1), calls=%async_computation.2 | async-start | bytes 7864320 | tf_op jit(solution)/shard_map/all_to_all | solution.py:453
  190.0 45.3 %collective-permute-start.7 = (bf16[2,2,2,2,16,1920]{5,4,3,2,1,0:T(8,128)(2,1)S(1)}, bf16[2,2,2,2,16,1920]{5,4,3,2,1,0:T(8,128)(2,1)S(1)}, u32[]{:S(2)}, u32[]{:S(2)}) collective-permute-start(bf16[2,2,2,2,16,1920]{5,4,3,2,1,0:T(8,128)(2,1)S(1)} %pad_maximum_fusion.7), channel_id=1, source_target_pairs={{0,96},{16,112},{32,0},{48,16},{64,32},{80,48},{96,64},{112,80},{1... | collective-permute-start | bytes 2949128 | tf_op jit(solution)/shard_map/ppermute | solution.py:206
  194.0 41.2 %collective-permute-start.6 = (bf16[2,2,2,2,16,1920]{5,4,3,2,1,0:T(8,128)(2,1)}, bf16[2,2,2,2,16,1920]{5,4,3,2,1,0:T(8,128)(2,1)S(1)}, u32[]{:S(2)}, u32[]{:S(2)}) collective-permute-start(bf16[2,2,2,2,16,1920]{5,4,3,2,1,0:T(8,128)(2,1)} %pad_maximum_fusion.6), channel_id=1, source_target_pairs={{0,64},{16,80},{32,96},{48,112},{64,0},{80,16},{96,32},{112,48},{1... | collective-permute-start | bytes 2949128 | tf_op jit(solution)/shard_map/ppermute | solution.py:206
  195.9 44.5 %collective-permute-start.5 = (bf16[2,2,2,2,16,1920]{5,4,3,2,1,0:T(8,128)(2,1)}, bf16[2,2,2,2,16,1920]{5,4,3,2,1,0:T(8,128)(2,1)}, u32[]{:S(2)}, u32[]{:S(2)}) collective-permute-start(bf16[2,2,2,2,16,1920]{5,4,3,2,1,0:T(8,128)(2,1)} %pad_maximum_fusion.5), channel_id=1, source_target_pairs={{0,32},{16,48},{32,64},{48,80},{64,96},{80,112},{96,0},{112,16},{1... | collective-permute-start | bytes 2949128 | tf_op jit(solution)/shard_map/ppermute | solution.py:206
  235.2 5.1 %copy-start.1 = (bf16[2,2,2,2,16,1920]{5,4,3,2,1,0:T(8,128)(2,1)}, bf16[2,2,2,2,16,1920]{5,4,3,2,1,0:T(8,128)(2,1)S(1)}, u32[]{:S(2)}) copy-start(bf16[2,2,2,2,16,1920]{5,4,3,2,1,0:T(8,128)(2,1)S(1)} %collective-permute-done.7.refs_4_) | copy-start | bytes 2949124
  235.3 5.1 %copy-start.2 = (bf16[2,2,2,2,16,1920]{5,4,3,2,1,0:T(8,128)(2,1)}, bf16[2,2,2,2,16,1920]{5,4,3,2,1,0:T(8,128)(2,1)S(1)}, u32[]{:S(2)}) copy-start(bf16[2,2,2,2,16,1920]{5,4,3,2,1,0:T(8,128)(2,1)S(1)} %collective-permute-done.6.refs_3_) | copy-start | bytes 2949124
  240.4 6.6 %copy-start.4 = (f32[16,128]{1,0:T(8,128)S(1)}, f32[16,128]{1,0:T(8,128)}, u32[]{:S(2)}) copy-start(f32[16,128]{1,0:T(8,128)} %gram_s.1) | copy-start | bytes 24580
  256.4 18.3 %all-to-all-start.4 = ((f32[16,16,128]{2,1,0:T(8,128)}), f32[16,16,128]{2,1,0:T(8,128)S(1)}, u32[]{:S(2)}, u32[]{:S(2)}) async-start(f32[16,16,128]{2,1,0:T(8,128)} %broadcast_in_dim.29), calls=%async_computation.4 | async-start | bytes 262144 | tf_op jit(solution)/shard_map/all_to_all | solution.py:189

commit v4 on v3

--- a/solution.py
+++ b/solution.py
@@ -58,39 +58,44 @@
     return z_forward, z_backward, forward, backward
 
 
-def z_forward_kernel(orbit_ref, live_ref, table_ref, wire_ref, share_ref, masked_ref):
+def z_forward_kernel(core_ref, orbit_ref, live_ref, table_ref, wire_ref, kept_ref, given_ref, masked_ref):
     masked_ref[...] = (orbit_ref[0].astype(jnp.float32) * live_ref[...]).astype(jnp.bfloat16)
-    for c in range(2):
-        for q in range(15):
-            start = c * GRID + q * 16
-            share_ref[q // 2, q % 2, c, 0] = masked_ref[start : start + 16]
-        share_ref[7, 1, c, 0] = jnp.zeros((16, SLOTS), jnp.bfloat16)
+    for core in range(2):
+
+        @pl.when(core_ref[0] == core)
+        def _():
+            for q in range(15):
+                target = kept_ref if q // 2 % 2 == core else given_ref
+                for c in range(2):
+                    start = c * GRID + q * 16
+                    target[q // 4, q % 2, c, 0] = masked_ref[start : start + 16]
+            target = kept_ref if core == 1 else given_ref
+            for c in range(2):
+                target[3, 1, c, 0] = jnp.zeros((16, SLOTS), jnp.bfloat16)
+
     values = jnp.dot(table_ref[...], masked_ref[...], preferred_element_type=jnp.float32).astype(jnp.bfloat16)
     wire_ref[...] = values.reshape(GROUPS, 2, 1, ZPAD, SLOTS)
 
 
-def z_forward_call(orbits, live, table):
+def z_forward_call(core, orbits, live, table):
+    share = pl.BlockSpec((4, 2, 2, 1, 16, SLOTS), lambda b: (0, 0, 0, b, 0, 0))
     return pl.pallas_call(
         z_forward_kernel,
         grid=(2,),
         in_specs=[
+            pl.BlockSpec(memory_space=pltpu.SMEM),
             pl.BlockSpec((1, 2 * GRID, SLOTS), lambda b: (b, 0, 0)),
             pl.BlockSpec((1, SLOTS), lambda b: (0, 0)),
             pl.BlockSpec((512, 2 * GRID), lambda b: (0, 0)),
         ],
-        out_specs=[
-            pl.BlockSpec((GROUPS, 2, 1, ZPAD, SLOTS), lambda b: (0, 0, b, 0, 0)),
-            pl.BlockSpec((8, 2, 2, 1, 16, SLOTS), lambda b: (0, 0, 0, b, 0, 0)),
-        ],
-        out_shape=[
-            jax.ShapeDtypeStruct((GROUPS, 2, 2, ZPAD, SLOTS), jnp.bfloat16),
-            jax.ShapeDtypeStruct((8, 2, 2, 2, 16, SLOTS), jnp.bfloat16),
-        ],
+        out_specs=[pl.BlockSpec((GROUPS, 2, 1, ZPAD, SLOTS), lambda b: (0, 0, b, 0, 0)), share, share],
+        out_shape=[jax.ShapeDtypeStruct((GROUPS, 2, 2, ZPAD, SLOTS), jnp.bfloat16)]
+        + [jax.ShapeDtypeStruct((4, 2, 2, 2, 16, SLOTS), jnp.bfloat16)] * 2,
         scratch_shapes=[pltpu.VMEM((2 * GRID, SLOTS), jnp.bfloat16)],
         compiler_params=pltpu.CompilerParams(vmem_limit_bytes=60 * MIB),
         cost_estimate=pl.CostEstimate(flops=1_800_000_000, bytes_accessed=12_000_000, transcendentals=0),
         name="z_forward",
-    )(orbits, live, table)
+    )(core, orbits, live, table)
 
 
 def z_backward_kernel(wire_ref, live_ref, table_ref, out_ref):
@@ -116,101 +121,157 @@
     )(wire, live, table)
 
 
-def gram_kernel(me_ref, *refs, left_blocks, right_blocks, first_lane):
-    left_refs, right_refs = refs[:left_blocks], refs[left_blocks : left_blocks + right_blocks]
-    out_ref, total = refs[left_blocks + right_blocks :]
+def side_by_side(refs):
+    return jnp.concatenate([ref[...].reshape(-1, SLOTS) for ref in refs], axis=0)
+
+
+def products_of(left, right):
+    return lax.dot_general(left, right, (((1,), (1,)), ((), ())), preferred_element_type=jnp.float32)
+
+
+def exact(left, right, transposed):
+    dims = (((1,), (1 if transposed else 0,)), ((), ()))
+    return lax.dot_general(left, right, dims, preferred_element_type=jnp.float32, precision=lax.Precision.HIGHEST)
+
+
+def selector(me_ref, size, shifts):
+    row = lax.broadcasted_iota(jnp.int32, (32, size), 0)
+    index = lax.broadcasted_iota(jnp.int32, (32, size), 1)
+    source = index // 64
+    if shifts is not None:
+        shift = source // 2
+        for position, value in enumerate(shifts):
+            shift = jnp.where(source // 2 == position, value, shift)
+        source = (me_ref[0] // 2 + 4 - shift) % 4 * 2 + (me_ref[0] + source) % 2
+    band = source * 2 + index // 16 % 2
+    return jnp.where((row % 16 == band) & (row // 16 == index // 32 % 2), 1.0, 0.0)
+
+
+def matched(total):
+    row = lax.broadcasted_iota(jnp.int32, total.shape, 0)
+    column = lax.broadcasted_iota(jnp.int32, total.shape, 1)
+    return jnp.where(row % 16 == column % 16, total, 0.0)
+
+
+def complex_lanes(table, first_lane):
+    row = lax.broadcasted_iota(jnp.int32, (32, 128), 0)
+    lane = lax.broadcasted_iota(jnp.int32, (32, 128), 1) - first_lane
+    match = (lane >= 0) & (lane < 32) & (lane % 16 == row % 16)
+    second, imag = lane // 16 == 1, row // 16 == 1
+    with_real = jnp.where(match & (second == imag), 1.0, 0.0)
+    with_imag = jnp.where(match & (second != imag), jnp.where(second, -1.0, 1.0), 0.0)
+    return exact(table[:16], with_real, False) + exact(table[16:], with_imag, False)
+
+
+def overlap_kernel(me_ref, *refs):
+    *piece_refs, out_ref, total = refs
     step = pl.program_id(0)
-    left = jnp.concatenate([ref[...].reshape(-1, SLOTS) for ref in left_refs], axis=0)
-    if right_blocks:
-        right = jnp.concatenate([ref[...].reshape(-1, SLOTS) for ref in right_refs], axis=0)
-    else:
-        right = left
-    product = lax.dot_general(left, right, (((1,), (1,)), ((), ())), preferred_element_type=jnp.float32)
+    values = side_by_side(piece_refs)
+    product = products_of(values, values)
 
     @pl.when(step == 0)
     def _():
         total[...] = product
 
-    def band_of(index, rotated):
-        source = index // 64
-        if rotated:
-            chip, core = me_ref[0] // 2, me_ref[0] % 2
-            source = (chip + 4 - source // 2) % 4 * 2 + (core + source) % 2
-        return source * 2 + index // 16 % 2
-
     @pl.when(step == 1)
     def _():
-        row = lax.broadcasted_iota(jnp.int32, (512, 512), 0)
-        column = lax.broadcasted_iota(jnp.int32, (512, 512), 1)
-        diagonal = jnp.where(row % 16 == column % 16, total[...] + product, 0.0)
-        band = lax.broadcasted_iota(jnp.int32, (32, 512), 0)
-        index = lax.broadcasted_iota(jnp.int32, (32, 512), 1)
-        pick = (band % 16 == band_of(index, left_blocks > 1)) & (band // 16 == index // 32 % 2)
-        by_band = jnp.dot(
-            jnp.where(pick, 1.0, 0.0), diagonal, preferred_element_type=jnp.float32, precision=lax.Precision.HIGHEST
+        pick = selector(me_ref, 512, (0, 1, 2, 3))
+        table = exact(exact(pick, matched(total[...] + product), False), pick, True)
+        out_ref[...] = complex_lanes(table, 0)
+
+
+def hamiltonian_kernel(me_ref, left_ref, left_far_ref, near_ref, before_ref, after_ref, far_ref, out_ref, *totals):
+    total, total_far = totals
+    step = pl.program_id(0)
+    product = products_of(left_ref[...].reshape(512, SLOTS), side_by_side([near_ref, before_ref, after_ref]))
+    product_far = products_of(left_far_ref[...].reshape(512, SLOTS), far_ref[...].reshape(128, SLOTS))
+
+    @pl.when(step == 0)
+    def _():
+        total[...] = product
+        total_far[...] = product_far
+
+    @pl.when(step == 1)
+    def _():
+        pick = selector(me_ref, 512, None)
+        table = exact(exact(pick, matched(total[...] + product), False), selector(me_ref, 384, (0, 1, 3)), True)
+        table += exact(
+            exact(pick, matched(total_far[...] + product_far), False), selector(me_ref, 128, (0,)), True
         )
-        lane = lax.broadcasted_iota(jnp.int32, (128, 512), 0) - first_lane
-        index = lax.broadcasted_iota(jnp.int32, (128, 512), 1)
-        match = (lane >= 0) & (lane < 32) & (lane % 16 == band_of(index, right_blocks != 1))
-        part = index // 32 % 2
-        second = lane // 16 == 1
-        with_real = jnp.where(match & (part == jnp.where(second, 1, 0)), 1.0, 0.0)
-        with_imag = jnp.where(match & (part == jnp.where(second, 0, 1)), jnp.where(second, -1.0, 1.0), 0.0)
-        dims = (((1,), (1,)), ((), ()))
-        out_ref[...] = lax.dot_general(
-            by_band[:16], with_real, dims, preferred_element_type=jnp.float32, precision=lax.Precision.HIGHEST
-        ) + lax.dot_general(
-            by_band[16:], with_imag, dims, preferred_element_type=jnp.float32, precision=lax.Precision.HIGHEST
-        )
-
-
-def gram_call(me, lefts, rights, first_lane, name):
-    whole = pl.BlockSpec((8, 1, 2, 2, 16, SLOTS), lambda g: (0, g, 0, 0, 0, 0))
-    piece = pl.BlockSpec((2, 1, 2, 2, 16, SLOTS), lambda g: (0, g, 0, 0, 0, 0))
-    specs = [whole if len(lefts) == 1 else piece] * len(lefts) + [whole if len(rights) == 1 else piece] * len(rights)
+        out_ref[...] = complex_lanes(table, 32)
+
+
+def gram_call(kernel, me, operands, starts, scratch, name):
+    def spec(operand, start):
+        return pl.BlockSpec((operand.shape[0], 1, 2, 2, 16, SLOTS), lambda g: (0, start + g, 0, 0, 0, 0))
+
     return pl.pallas_call(
-        functools.partial(
-            gram_kernel, left_blocks=len(lefts), right_blocks=len(rights), first_lane=first_lane
-        ),
+        kernel,
         grid=(2,),
-        in_specs=[pl.BlockSpec(memory_space=pltpu.SMEM)] + specs,
+        in_specs=[pl.BlockSpec(memory_space=pltpu.SMEM)] + [spec(operand, start) for operand, start in zip(operands, starts)],
         out_specs=pl.BlockSpec((16, 128), lambda g: (0, 0)),
         out_shape=jax.ShapeDtypeStruct((16, 128), jnp.float32),
-        scratch_shapes=[pltpu.VMEM((512, 512), jnp.float32)],
+        scratch_shapes=[pltpu.VMEM(shape, jnp.float32) for shape in scratch],
         compiler_params=pltpu.CompilerParams(vmem_limit_bytes=60 * MIB),
         cost_estimate=pl.CostEstimate(flops=2_000_000_000, bytes_accessed=8_000_000, transcendentals=0),
         name=name,
-    )(me, *lefts, *rights)
-
-
-def summed(values, axis):
+    )(me, *operands)
+
+
+def twofold_kernel(in_ref, out_ref):
+    for half in range(2):
+        out_ref[half, :, 0] = in_ref[half]
+        out_ref[half, :, 1] = in_ref[1 - half]
+
+
+def twofold_call(blocks):
+    count = 2
+    result = pl.pallas_call(
+        twofold_kernel,
+        grid=(4 // count,),
+        in_specs=[pl.BlockSpec((2, count, 128, SLOTS), lambda i: (0, i, 0, 0))],
+        out_specs=pl.BlockSpec((2, count, 2, 128, SLOTS), lambda i: (0, i, 0, 0, 0)),
+        out_shape=jax.ShapeDtypeStruct((2, 4, 2, 128, SLOTS), jnp.bfloat16),
+        compiler_params=pltpu.CompilerParams(vmem_limit_bytes=60 * MIB),
+        cost_estimate=pl.CostEstimate(flops=0, bytes_accessed=12_000_000, transcendentals=0),
+        name="twofold",
+    )(blocks.reshape(2, 4, 128, SLOTS))
+    return result.reshape(8, 256, SLOTS)
+
+
+def summed(values, axis, steps, tied=None):
     size = lax.axis_size(axis)
-    copies = jnp.broadcast_to(values[None], (size,) + values.shape)
-    return jnp.sum(lax.all_to_all(copies, axis, split_axis=0, concat_axis=0, tiled=True), axis=0)
-
-
-def spread_blocks(blocks, axis):
-    me = lax.axis_index(axis)
-    chip, core = me // 2, me % 2
-    halves = blocks.reshape((4, 2) + blocks.shape[1:])
-    kept = lax.dynamic_index_in_dim(halves, core, 1, keepdims=False)
-    given = lax.dynamic_index_in_dim(halves, 1 - core, 1, keepdims=False)
+    for step in steps:
+        received = lax.ppermute(values, axis, [(i, i ^ step) for i in range(size)])
+        if tied is not None:
+            received, tied = lax.optimization_barrier((received, tied))
+        values = values + received
+    return values, tied
+
+
+def spread_blocks(kept, given, axis, tied, shifts):
+    chip = lax.axis_index(axis) // 2
     got = lax.ppermute(given, axis, [(i, i ^ 1) for i in range(8)])
-    result = []
+    pairs = []
     for shift in range(4):
         target = (chip + shift) % 4
-        pair = jnp.concatenate(
-            [lax.dynamic_slice_in_dim(kept, target, 1, 0), lax.dynamic_slice_in_dim(got, target, 1, 0)], axis=0
+        pairs.append(
+            jnp.concatenate(
+                [lax.dynamic_slice_in_dim(kept, target, 1, 0), lax.dynamic_slice_in_dim(got, target, 1, 0)], axis=0
+            )
         )
-        if shift:
-            pair = lax.ppermute(pair, axis, [(i, (i // 2 + shift) % 4 * 2 + i % 2) for i in range(8)])
-        result.append(pair)
-    return result
+    if tied is not None:
+        tied, *pairs = lax.optimization_barrier((tied, *pairs))
+    for shift in shifts:
+        pairs[shift] = lax.ppermute(
+            pairs[shift], axis, [(i, (i // 2 + shift) % 4 * 2 + i % 2) for i in range(8)]
+        )
+    return pairs, tied
 
 
 def plane_kernel(
-    place_ref, count_ref, upper_ref, wire_ref, field_ref, forward_ref, backward_ref, out_ref,
-    grid_ref, mid_ref, back_ref, stage_a, stage_b, list_ref
+    core_ref, place_ref, count_ref, upper_ref, wire_ref, field_ref, forward_ref, backward_ref,
+    out_ref, kept_ref, given_ref, grid_ref, mid_ref, back_ref, side_ref, stage_a, stage_b, list_ref, sems
 ):
     step = pl.program_id(0)
     lane = lax.broadcasted_iota(jnp.int32, (1, 128), 1)
@@ -304,7 +365,7 @@
         spatial = jnp.dot(forward_ref[...], jnp.concatenate(parts, axis=1), preferred_element_type=jnp.float32)
         parts = []
         for j in range(N2):
-            parts.append(doubled(spatial[:, j * 128 : (j + 1) * 128] * field_ref[i * N2 + j]))
+            parts.append(doubled(spatial[:, j * 128 : (j + 1) * 128] * field_ref[i * N2 + j].astype(jnp.float32)))
         result = jnp.dot(backward_ref[...], jnp.concatenate(parts, axis=1), preferred_element_type=jnp.float32)
         for j in range(N2):
             pair = step * PB + i * N2 + j
@@ -338,6 +399,9 @@
         select = jnp.where(select_column == source, 1.0, 0.0).astype(jnp.bfloat16)
         origin = pl.multiple_of((step - (pl.num_programs(0) - 1)) * 8, 8)
 
+        def side_of(p):
+            return (p // 2 + core_ref[0]) % 2
+
         def gather(entry, stage):
             for u in range(128):
                 stage[pl.ds(origin + u, 1), :] = grid_ref[pl.ds(place_ref[entry * 128 + u], 1), :]
@@ -349,7 +413,9 @@
                 select, stage[...].astype(jnp.bfloat16), (((1,), (1,)), ((), ())), preferred_element_type=jnp.float32
             )
             upper = upper_ref[pl.ds(entry, 1), :] > 0.0
-            out_ref[p, :, pl.ds(base, 128)] = jnp.where(upper, both[64:], both[:64]).astype(jnp.bfloat16)
+            values = jnp.where(upper, both[64:], both[:64]).astype(jnp.bfloat16)
+            out_ref[p, :, pl.ds(base, 128)] = values
+            side_ref[side_of(p), p // 4, p % 2, :, pl.ds(base, 128)] = values
 
         def pick(i, carry):
             entry = list_ref[2 * i]
@@ -363,7 +429,10 @@
 
         def group(p, carry):
             def blank(t, inner):
-                out_ref[p, :, pl.ds(pl.multiple_of(t * 128, 128), 128)] = jnp.zeros((64, 128), jnp.bfloat16)
+                base = pl.multiple_of(t * 128, 128)
+                blank = jnp.zeros((64, 128), jnp.bfloat16)
+                out_ref[p, :, pl.ds(base, 128)] = blank
+                side_ref[side_of(p), p // 4, p % 2, :, pl.ds(base, 128)] = blank
                 return inner
 
             return lax.fori_loop(count_ref[p], SLOTS // 128, blank, carry)
@@ -371,14 +440,23 @@
         lax.fori_loop(0, GROUPS, group, 0)
         gather(list_ref[0], stage_a)
         lax.fori_loop(0, list_ref[255], pick, 0)
-
-
-def plane_call(place, count, upper, wire, field, forward, backward):
+        copies = [
+            pltpu.make_async_copy(side_ref.at[0], kept_ref, sems.at[0]),
+            pltpu.make_async_copy(side_ref.at[1], given_ref, sems.at[1]),
+        ]
+        for copy in copies:
+            copy.start()
+        for copy in copies:
+            copy.wait()
+
+
+def plane_call(core, place, count, upper, wire, field, forward, backward):
     whole = lambda shape: pl.BlockSpec(shape, lambda i: (0,) * len(shape), pipeline_mode=pl.Buffered(1))
     return pl.pallas_call(
         plane_kernel,
         grid=(PAIRS // PB,),
         in_specs=[
+            pl.BlockSpec(memory_space=pltpu.SMEM),
             pl.BlockSpec(memory_space=pltpu.SMEM),
             pl.BlockSpec(memory_space=pltpu.SMEM),
             whole((GROUPS * SLOTS // 128, 128)),
@@ -387,41 +465,44 @@
             whole((GRID, 2 * BOX)),
             whole((BOX, 2 * GRID)),
         ],
-        out_specs=whole((GROUPS, 64, SLOTS)),
-        out_shape=jax.ShapeDtypeStruct((GROUPS, 64, SLOTS), jnp.bfloat16),
+        out_specs=[whole((GROUPS, 64, SLOTS)), pl.BlockSpec(memory_space=pl.ANY), pl.BlockSpec(memory_space=pl.ANY)],
+        out_shape=[jax.ShapeDtypeStruct((GROUPS, 64, SLOTS), jnp.bfloat16)]
+        + [jax.ShapeDtypeStruct((4, 2, 64, SLOTS), jnp.bfloat16)] * 2,
         scratch_shapes=[
             pltpu.VMEM((ROWS + 8, 128), jnp.float32),
             pltpu.VMEM((PAIRS * PITCH, 128), jnp.float32),
             pltpu.VMEM((BOX * PITCHB, 128), jnp.float32),
+            pltpu.VMEM((2, 4, 2, 64, SLOTS), jnp.bfloat16),
             pltpu.VMEM((128, 128), jnp.float32),
             pltpu.VMEM((128, 128), jnp.float32),
             pltpu.SMEM((256,), jnp.int32),
+            pltpu.SemaphoreType.DMA((2,)),
         ],
         compiler_params=pltpu.CompilerParams(vmem_limit_bytes=62 * MIB),
         cost_estimate=pl.CostEstimate(flops=13_000_000_000, bytes_accessed=24_000_000, transcendentals=0),
         name="planes",
-    )(place, count, upper, wire, field, forward, backward)
+    )(core, place, count, upper, wire, field, forward, backward)
 
 
 def field_kernel(lower_ref, upper_ref, out_ref):
     blank = jnp.zeros((1, lower_ref.shape[-1]), jnp.float32)
-    lower = jnp.concatenate([lower_ref[...], blank], axis=0)
-    upper = jnp.concatenate([upper_ref[...], blank], axis=0)
+    lower = jnp.concatenate([lower_ref[...], blank], axis=0).astype(jnp.bfloat16)
+    upper = jnp.concatenate([upper_ref[...], blank], axis=0).astype(jnp.bfloat16)
     once = jnp.concatenate([lower, lower, upper, upper], axis=0)
-    out_ref[...] = jnp.concatenate([once, once], axis=0).T.reshape(8, GRID, 128)
+    out_ref[...] = jnp.concatenate([once, once], axis=0).T.reshape(PB, GRID, 128)
 
 
 def field_call(potential):
-    lanes = 8 * GRID
+    lanes = PB * GRID
     return pl.pallas_call(
         field_kernel,
-        grid=(PAIRS // 8,),
+        grid=(PAIRS // PB,),
         in_specs=[
             pl.BlockSpec((PLANES, lanes), lambda i: (0, i)),
-            pl.BlockSpec((PLANES, lanes), lambda i: (0, i + PAIRS // 8)),
+            pl.BlockSpec((PLANES, lanes), lambda i: (0, i + PAIRS // PB)),
         ],
-        out_specs=pl.BlockSpec((8, GRID, 128), lambda i: (i, 0, 0)),
-        out_shape=jax.ShapeDtypeStruct((PAIRS, GRID, 128), jnp.float32),
+        out_specs=pl.BlockSpec((PB, GRID, 128), lambda i: (i, 0, 0)),
+        out_shape=jax.ShapeDtypeStruct((PAIRS, GRID, 128), jnp.bfloat16),
         compiler_params=pltpu.CompilerParams(vmem_limit_bytes=60 * MIB),
         cost_estimate=pl.CostEstimate(flops=0, bytes_accessed=18_000_000, transcendentals=0),
         name="field",
@@ -440,24 +521,38 @@
     count = (jnp.sum(live_all.reshape(GROUPS, SLOTS).astype(jnp.int32), axis=1) + 127) // 128
     upper = (live_all & (box_y >= HALF)).astype(jnp.float32).reshape(GROUPS * SLOTS // 128, 128)
     me = lax.axis_index("band").astype(jnp.int32)[None]
+    core = me % 2
+
+    wire, kept, given = z_forward_call(core, orbitals.transpose(0, 2, 1), live, z_forward)
+    incoming = lax.all_to_all(wire.reshape(GROUPS, 64, SLOTS), "fft", split_axis=0, concat_axis=0, tiled=True)
+    shares, potential = spread_blocks(kept, given, "band", potential, (1, 2, 3))
     field = field_call(potential)
-
-    wire, share = z_forward_call(orbitals.transpose(0, 2, 1), live, z_forward)
-    incoming = lax.all_to_all(wire.reshape(GROUPS, 64, SLOTS), "fft", split_axis=0, concat_axis=0, tiled=True)
-    shares = spread_blocks(share, "band")
     incoming, field, place, count, upper, *shares = lax.optimization_barrier(
         (incoming, field, place, count, upper, *shares)
     )
-    left = lax.all_to_all(incoming.reshape(8, 128, SLOTS), "band", split_axis=0, concat_axis=0, tiled=True)
-    outgoing = plane_call(place, count, upper, incoming, field, forward, backward)
+    left = lax.all_to_all(twofold_call(incoming), "band", split_axis=0, concat_axis=0, tiled=True)
+    left = left.reshape(8, 4, 2, 2, 16, SLOTS)
+    outgoing, kept, given = plane_call(core, place, count, upper, incoming, field, forward, backward)
     returned = lax.all_to_all(outgoing, "fft", split_axis=0, concat_axis=0, tiled=True)
-    rights = spread_blocks(outgoing.reshape(8, 2, 2, 2, 16, SLOTS), "band")
-    product_h = gram_call(me, [left.reshape(8, 2, 2, 2, 16, SLOTS)], rights, 32, "gram_h")
-    product_s = gram_call(me, shares, [], 0, "gram_s")
-    product_h, product_s, returned = lax.optimization_barrier((product_h, product_s, returned))
-    products = product_s + product_h
+    split = (4, 2, 2, 2, 16, SLOTS)
+    (near, before, opposite, after), _ = spread_blocks(
+        kept.reshape(split), given.reshape(split), "band", None, (1, 3)
+    )
+    product_s = gram_call(overlap_kernel, me, shares, (0, 0, 0, 0), [(512, 512)], "overlap")
+    product_h = gram_call(
+        hamiltonian_kernel,
+        me,
+        [left, left, near, before, after, opposite],
+        (0, 2, 0, 0, 0, 0),
+        [(512, 384), (512, 128)],
+        "hamiltonian",
+    )
     applied = z_backward_call(returned.reshape(GROUPS, 2, 2, ZPAD, SLOTS), live, z_backward)
-    products = summed(summed(products, "band"), "fft") * (1.0 / (2.0 * STICKS * GRID))
+    products, _ = summed(product_s + product_h, "band", (1, 2, 4))
+    products, _ = summed(products, "fft", (1, 2))
+    products, applied = summed(products, "fft", (4,), applied)
+    products, _ = summed(products, "fft", (8,))
+    products = products * (1.0 / (2.0 * STICKS * GRID))
     products = products[:, :64].reshape(16, 4, 16).transpose(1, 0, 2)
     return (applied.transpose(0, 2, 1), products[0:2], products[2:4])
 

time: 277 us -> 256 us (0.924)
  waiting for transfers between devices: 79.9 us -> 60 us
  starting transfers between devices: 39.8 us -> 50.5 us
  local copies, waits for them, and re-layouts: 14.1 us -> 5.86 us
  blocking collectives: 7.98 us -> 0 us
    ppermute x6 -> x12, waiting for transfers between devices: 77.3 us -> 58.7 us  [the longest x5 47.5 us: spread_blocks(): lax.ppermute(pairs[shift], axis, [(i, (i // 2 + shift) % 4 * 2 + i % 2) f...]
    ppermute x6 -> x12, starting transfers between devices: 9.35 us -> 24.4 us  [the longest x7 15.4 us: summed(): received = lax.ppermute(values, axis, [(i, i ^ step) for i in range(size)])]
    all_to_all x2 -> x1, starting transfers between devices: 15 us -> 4.92 us  [local(): lax.all_to_all(twofold_call(incoming), 'band', split_axis=0, concat_axis=...]
    all_to_all x1 -> x0, blocking collectives: 7.98 us -> none  [summed(): lax.all_to_all(copies, axis, split_axis=0, concat_axis=0, tiled=True)]
    squeeze x2 -> x0, local copies, waits for them, and re-layouts: 5.91 us -> none  [spread_blocks(): given = lax.dynamic_index_in_dim(halves, 1 - core, 1, keepdims=False)]
    all_to_all x1, starting transfers between devices: 6.83 us -> 12.5 us  [local(): lax.all_to_all(outgoing, 'fft', split_axis=0, concat_axis=0, tiled=True)]
    pallas_call x4 -> x5, Pallas kernels: 32.6 us -> 32.5 us  [the longest x2 13.7 us: gram_call(): pl.pallas_call(kernel, grid=(2,), in_specs=[pl.BlockSpec(memory_space=plt...]
  transfers between devices with their start and end apart: 12 -> 17, of which waited for: 5 -> 11; matrix products, arithmetic and copies ran while one was open for 5% -> 4% of each run, Pallas kernels for 43% -> 45%
where the time goes in v4:
time: 256 us; the launch traced here: 252 us
  Pallas kernels  127 us (50%)
  waiting for transfers between devices  60 us (23%)
  starting transfers between devices  50.5 us (20%)
  other arithmetic  8.4 us (3%)
  local copies, waits for them, and re-layouts  5.86 us (2%)
    pallas_call x1, Pallas kernels, plane_call(): pl.pallas_call(plane_kernel, grid=(PAIRS // PB,), in_specs=[pl.BlockSpec(...  88.9 us
    ppermute x5, waiting for transfers between devices, spread_blocks(): lax.ppermute(pairs[shift], axis, [(i, (i // 2 + shift) % 4 * 2 + i % 2) f...  47.5 us
    ppermute x7, starting transfers between devices, summed(): received = lax.ppermute(values, axis, [(i, i ^ step) for i in range(size)])  15.4 us
    pallas_call x2, Pallas kernels, gram_call(): pl.pallas_call(kernel, grid=(2,), in_specs=[pl.BlockSpec(memory_space=plt...  13.7 us
    all_to_all x1, starting transfers between devices, local(): lax.all_to_all(outgoing, 'fft', split_axis=0, concat_axis=0, tiled=True)  12.5 us
    ppermute x7, waiting for transfers between devices, summed(): received = lax.ppermute(values, axis, [(i, i ^ step) for i in range(size)])  11.2 us
    ppermute x5, starting transfers between devices, spread_blocks(): lax.ppermute(pairs[shift], axis, [(i, (i // 2 + shift) % 4 * 2 + i % 2) f...  8.95 us
    all_to_all x1, starting transfers between devices, local(): lax.all_to_all(wire.reshape(GROUPS, 64, SLOTS), 'fft', split_axis=0, conc...  8.32 us
  transfers between devices with their start and end apart: 17, of which 11 were waited for; matrix products, arithmetic and copies ran while one was open for 4% of the time, Pallas kernels for 45%

profile of v4, /device:TPU:0, one launch (start us, length us, event | category | flops | bytes accessed | tf_op | source)
XLA Modules:
  0.0 252.4 jit_solution(15916418286382879796)
XLA Ops:
  0.6 0.8 fusion.3
  1.4 0.6 reshape.51.live_ref
  2.0 7.0 %z_forward.1 = (bf16[16,2,2,16,1920]{4,3,2,1,0:T(8,128)(2,1)}, bf16[4,2,2,2,16,1920]{5,4,3,2,1,0:T(8,128)(2,1)}, bf16[4,2,2,2,16,1920]{5,4,3,2,1,0:T(8,128)(2,1)}) custom-call(s32[1]{0:T(128)S(6)} %select_n.91.core_ref, bf16[2,480,1920]{2,1,0:T(8,128)(2,1)} %bitcast.20, f32[1,1920]{1,0:T(1,128)} %reshape.51.live_ref, bf16[512,480]{1,0:T(8,128)(2,1)} %constant.138.clone.table_ref), custom_call_target="tpu_custom_call" | custom-call | flops 1800000000 | bytes 12000000 | tf_op jit(solution)/shard_map/z_forward/pallas_call | solution.py:82
  9.1 0.0 collective-permute-start
  9.1 8.3 %all-to-all-start = ((bf16[16,64,1920]{2,1,0:T(8,128)(2,1)}), bf16[16,64,1920]{2,1,0:T(8,128)(2,1)}, u32[]{:S(2)}, u32[]{:S(2)}) async-start(bf16[16,64,1920]{2,1,0:T(8,128)(2,1)} %bitcast.16), calls=%async_computation | async-start | bytes 7864320 | tf_op jit(solution)/shard_map/all_to_all | solution.py:527
  17.5 0.0 copy-done.2
  17.5 0.8 convert_bitcast_fusion
  18.3 0.1 reduce_sum.9
  18.4 1.6 constant_dynamic-slice_fusion.9
  20.1 0.0 collective-permute-done
  20.1 0.2 constant_dynamic-slice_fusion.8
  20.2 0.2 pad_maximum_fusion.2
  20.4 1.2 pad_maximum_fusion
  21.6 1.5 collective-permute-start.1
  23.1 2.7 %collective-permute-start.2 = (bf16[2,2,2,2,16,1920]{5,4,3,2,1,0:T(8,128)(2,1)S(1)}, bf16[2,2,2,2,16,1920]{5,4,3,2,1,0:T(8,128)(2,1)}, u32[]{:S(2)}, u32[]{:S(2)}) collective-permute-start(bf16[2,2,2,2,16,1920]{5,4,3,2,1,0:T(8,128)(2,1)S(1)} %get-tuple-element.31), channel_id=1, source_target_pairs={{0,64},{16,80},{32,96},{48,112},{64,0},{80,16},{96,32},{112,48},{1... | collective-permute-start | bytes 2949128 | tf_op jit(solution)/shard_map/ppermute | solution.py:266
  25.8 1.4 collective-permute-start.3
  27.2 0.5 and_select_fusion.count_ref
  27.8 0.8 add_select_fusion.2.place_ref
  28.6 7.0 %field.1.field_ref = bf16[120,240,128]{2,1,0:T(8,128)(2,1)} custom-call(f32[15,57600]{1,0:T(8,128)} %upper_ref, f32[15,57600]{1,0:T(8,128)} %upper_ref), custom_call_target="tpu_custom_call" | custom-call | bytes 18000000 | tf_op jit(solution)/shard_map/field/pallas_call | solution.py:497
  35.5 11.1 %collective-permute-done.1.refs_1_ = bf16[2,2,2,2,16,1920]{5,4,3,2,1,0:T(8,128)(2,1)S(1)} collective-permute-done((bf16[2,2,2,2,16,1920]{5,4,3,2,1,0:T(8,128)(2,1)S(1)}, bf16[2,2,2,2,16,1920]{5,4,3,2,1,0:T(8,128)(2,1)S(1)}, u32[]{:S(2)}, u32[]{:S(2)}) %collective-permute-start.1) | collective-permute-done | bytes 983072 | tf_op jit(solution)/shard_map/ppermute | solution.py:266
  46.7 22.1 %collective-permute-done.2.refs_2_ = bf16[2,2,2,2,16,1920]{5,4,3,2,1,0:T(8,128)(2,1)} collective-permute-done((bf16[2,2,2,2,16,1920]{5,4,3,2,1,0:T(8,128)(2,1)S(1)}, bf16[2,2,2,2,16,1920]{5,4,3,2,1,0:T(8,128)(2,1)}, u32[]{:S(2)}, u32[]{:S(2)}) %collective-permute-start.2) | collective-permute-done | bytes 983072 | tf_op jit(solution)/shard_map/ppermute | solution.py:266
  68.8 0.0 collective-permute-done.3.refs_3_
  68.8 1.3 all-to-all-done.wire_ref
  70.1 4.9 %twofold.1 = bf16[2,4,2,128,1920]{4,3,2,1,0:T(8,128)(2,1)} custom-call(bf16[2,4,128,1920]{3,2,1,0:T(8,128)(2,1)} %bitcast.4.in_ref), custom_call_target="tpu_custom_call" | custom-call | bytes 12000000 | tf_op jit(solution)/shard_map/twofold/pallas_call | solution.py:229
  75.0 0.0 copy-done.4
  75.0 4.9 %all-to-all-start.1 = ((bf16[8,256,1920]{2,1,0:T(8,128)(2,1)}), bf16[8,256,1920]{2,1,0:T(8,128)(2,1)}, u32[]{:S(2)}, u32[]{:S(2)}) async-start(bf16[8,256,1920]{2,1,0:T(8,128)(2,1)} %bitcast.15), calls=%async_computation.1 | async-start | bytes 15728640 | tf_op jit(solution)/shard_map/all_to_all | solution.py:533
  79.9 88.9 %planes.1 = (bf16[16,64,1920]{2,1,0:T(8,128)(2,1)}, bf16[4,2,64,1920]{3,2,1,0:T(8,128)(2,1)}, bf16[4,2,64,1920]{3,2,1,0:T(8,128)(2,1)}) custom-call(s32[1]{0:T(128)S(6)} %select_n.91.core_ref, s32[30720]{0:T(1024)} %add_select_fusion.2.place_ref, s32[16]{0:T(128)} %and_select_fusion.count_ref, f32[240,128]{1,0:T(8,128)} %get-tuple-element.40.upper_ref, ...), custom_call_target="tpu_custom_call" | custom-call | flops 12999999488 | bytes 24000000 | tf_op jit(solution)/shard_map/planes/pallas_call | solution.py:455
  168.8 0.4 collective-permute-start.4
  169.2 0.0 all-to-all-done.1
  169.2 12.5 %all-to-all-start.2 = ((bf16[16,64,1920]{2,1,0:T(8,128)(2,1)}), bf16[16,64,1920]{2,1,0:T(8,128)(2,1)}, u32[]{:S(2)}, u32[]{:S(2)}) async-start(bf16[16,64,1920]{2,1,0:T(8,128)(2,1)} %get-tuple-element.44), calls=%async_computation.2 | async-start | bytes 7864320 | tf_op jit(solution)/shard_map/all_to_all | solution.py:536
  181.7 0.0 copy-done
  181.7 0.2 constant_dynamic-slice_fusion.1
  181.9 0.0 collective-permute-done.4
  181.9 1.6 constant_dynamic-slice_fusion
  183.5 0.1 pad_maximum_fusion.5
  183.6 1.8 collective-permute-start.5
  185.4 1.1 pad_maximum_fusion.6
  186.5 1.5 collective-permute-start.6
  188.0 5.8 %overlap.1 = f32[16,128]{1,0:T(8,128)} custom-call(s32[1]{0:T(128)} %bitcast.me_ref, bf16[2,2,2,2,16,1920]{5,4,3,2,1,0:T(8,128)(2,1)} %get-tuple-element.33.refs_0_, bf16[2,2,2,2,16,1920]{5,4,3,2,1,0:T(8,128)(2,1)} %copy-done.4, bf16[2,2,2,2,16,1920]{5,4,3,2,1,0:T(8,128)(2,1)} %collective-permute-done.2.refs_2_, ...), custom_call_target="tpu_custom_call" | custom-call | flops 2000000000 | bytes 8000000 | tf_op jit(solution)/shard_map/overlap/pallas_call | solution.py:208
  193.8 1.1 pad_maximum_fusion.7.far_ref
  194.9 1.0 pad_maximum_fusion.4.near_ref
  195.9 12.8 %collective-permute-done.5.before_ref = bf16[2,2,2,2,16,1920]{5,4,3,2,1,0:T(8,128)(2,1)} collective-permute-done((bf16[2,2,2,2,16,1920]{5,4,3,2,1,0:T(8,128)(2,1)S(1)}, bf16[2,2,2,2,16,1920]{5,4,3,2,1,0:T(8,128)(2,1)}, u32[]{:S(2)}, u32[]{:S(2)}) %collective-permute-start.5) | collective-permute-done | bytes 983072 | tf_op jit(solution)/shard_map/ppermute | solution.py:266
  208.7 1.4 collective-permute-done.6.after_ref
  210.1 0.9 copy-done.1
  211.1 7.9 %hamiltonian.1 = f32[16,128]{1,0:T(8,128)} custom-call(s32[1]{0:T(128)} %bitcast.me_ref, bf16[8,4,2,2,16,1920]{5,4,3,2,1,0:T(8,128)(2,1)} %bitcast.6.left_ref.left_far_ref, bf16[8,4,2,2,16,1920]{5,4,3,2,1,0:T(8,128)(2,1)} %bitcast.6.left_ref.left_far_ref, bf16[2,2,2,2,16,1920]{5,4,3,2,1,0:T(8,128)(2,1)} %pad_maximum_fusion.4.near_ref, ...), custom_call_target="tpu_custom_call" | custom-call | flops 2000000000 | bytes 8000000 | tf_op jit(solution)/shard_map/hamiltonian/pallas_call | solution.py:208
  219.0 0.7 add.127
  219.7 0.0 collective-permute-start.7
  219.7 1.2 collective-permute-done.7
  220.9 1.5 collective-permute-start.8
  222.3 2.2 collective-permute-done.8
  224.5 2.7 %collective-permute-start.9 = (f32[16,128]{1,0:T(8,128)S(1)}, f32[16,128]{1,0:T(8,128)S(1)}, u32[]{:S(2)}, u32[]{:S(2)}) collective-permute-start(f32[16,128]{1,0:T(8,128)S(1)} %add.129), channel_id=1, source_target_pairs={{0,64},{16,80},{32,96},{48,112},{64,0},{80,16},{96,32},{112,48},{1... | collective-permute-start | bytes 24584 | tf_op jit(solution)/shard_map/ppermute | solution.py:245
  227.2 2.5 collective-permute-done.9
  229.7 1.6 collective-permute-start.10
  231.3 2.1 collective-permute-done.10
  233.3 3.4 %collective-permute-start.11 = (f32[16,128]{1,0:T(8,128)S(1)}, f32[16,128]{1,0:T(8,128)S(1)}, u32[]{:S(2)}, u32[]{:S(2)}) collective-permute-start(f32[16,128]{1,0:T(8,128)S(1)} %add.131), channel_id=1, source_target_pairs={{0,2},{1,3},{2,0},{3,1},{4,6},{5,7},{6,4},{7,5},{8,10},{9,11},{10,... | collective-permute-start | bytes 24584 | tf_op jit(solution)/shard_map/ppermute | solution.py:245
  236.8 1.7 collective-permute-done.11
  238.5 1.8 collective-permute-start.12
  240.3 0.0 all-to-all-done.2
  240.3 5.3 %z_backward.1 = bf16[2,480,1920]{2,1,0:T(8,128)(2,1)} custom-call(bf16[16,2,2,16,1920]{4,3,2,1,0:T(8,128)(2,1)} %bitcast.9.wire_ref, f32[1,1920]{1,0:T(1,128)} %reshape.51.live_ref, bf16[480,512]{1,0:T(8,128)(2,1)} %constant.139.clone.table_ref), custom_call_target="tpu_custom_call" | custom-call | flops 1800000000 | bytes 8000000 | tf_op jit(solution)/shard_map/z_backward/pallas_call | solution.py:108
  245.6 0.0 collective-permute-done.12
  245.6 4.4 %collective-permute-start.13 = (f32[16,128]{1,0:T(8,128)S(1)}, f32[16,128]{1,0:T(8,128)S(1)}, u32[]{:S(2)}, u32[]{:S(2)}) collective-permute-start(f32[16,128]{1,0:T(8,128)S(1)} %add.133), channel_id=1, source_target_pairs={{0,8},{1,9},{2,10},{3,11},{4,12},{5,13},{6,14},{7,15},{8,0},{9,1},... | collective-permute-start | bytes 24584 | tf_op jit(solution)/shard_map/ppermute | solution.py:245
  250.0 1.6 collective-permute-done.13
  251.6 0.1 reshape.50
  251.7 0.6 fusion.4
  (15 shorter events, 0.1 us)
Async XLA Ops:
  9.1 11.0 %collective-permute-start = (bf16[4,2,2,2,16,1920]{5,4,3,2,1,0:T(8,128)(2,1)}, bf16[4,2,2,2,16,1920]{5,4,3,2,1,0:T(8,128)(2,1)S(1)}, u32[]{:S(2)}, u32[]{:S(2)}) collective-permute-start(bf16[4,2,2,2,16,1920]{5,4,3,2,1,0:T(8,128)(2,1)} %get-tuple-element.27), channel_id=1, source_target_pairs={{0,16},{16,0},{32,48},{48,32},{64,80},{80,64},{96,112},{112,96},{1... | collective-permute-start | bytes 5898248 | tf_op jit(solution)/shard_map/ppermute | solution.py:254
  9.1 8.4 %copy-start.2 = (s32[30720]{0:T(1024)S(1)}, s32[30720]{0:T(1024)}, u32[]{:S(2)}) copy-start(s32[30720]{0:T(1024)} %param.10) | copy-start | bytes 368644
  9.1 61.0 %all-to-all-start = ((bf16[16,64,1920]{2,1,0:T(8,128)(2,1)}), bf16[16,64,1920]{2,1,0:T(8,128)(2,1)}, u32[]{:S(2)}, u32[]{:S(2)}) async-start(bf16[16,64,1920]{2,1,0:T(8,128)(2,1)} %bitcast.16), calls=%async_computation | async-start | bytes 7864320 | tf_op jit(solution)/shard_map/all_to_all | solution.py:527
  21.6 25.1 %collective-permute-start.1 = (bf16[2,2,2,2,16,1920]{5,4,3,2,1,0:T(8,128)(2,1)S(1)}, bf16[2,2,2,2,16,1920]{5,4,3,2,1,0:T(8,128)(2,1)S(1)}, u32[]{:S(2)}, u32[]{:S(2)}) collective-permute-start(bf16[2,2,2,2,16,1920]{5,4,3,2,1,0:T(8,128)(2,1)S(1)} %get-tuple-element.30), channel_id=1, source_target_pairs={{0,32},{16,48},{32,64},{48,80},{64,96},{80,112},{96,0},{112,16},{1... | collective-permute-start | bytes 2949128 | tf_op jit(solution)/shard_map/ppermute | solution.py:266
  23.1 45.7 %collective-permute-start.2 = (bf16[2,2,2,2,16,1920]{5,4,3,2,1,0:T(8,128)(2,1)S(1)}, bf16[2,2,2,2,16,1920]{5,4,3,2,1,0:T(8,128)(2,1)}, u32[]{:S(2)}, u32[]{:S(2)}) collective-permute-start(bf16[2,2,2,2,16,1920]{5,4,3,2,1,0:T(8,128)(2,1)S(1)} %get-tuple-element.31), channel_id=1, source_target_pairs={{0,64},{16,80},{32,96},{48,112},{64,0},{80,16},{96,32},{112,48},{1... | collective-permute-start | bytes 2949128 | tf_op jit(solution)/shard_map/ppermute | solution.py:266
  25.8 43.0 %collective-permute-start.3 = (bf16[2,2,2,2,16,1920]{5,4,3,2,1,0:T(8,128)(2,1)S(1)}, bf16[2,2,2,2,16,1920]{5,4,3,2,1,0:T(8,128)(2,1)}, u32[]{:S(2)}, u32[]{:S(2)}) collective-permute-start(bf16[2,2,2,2,16,1920]{5,4,3,2,1,0:T(8,128)(2,1)S(1)} %get-tuple-element.32), channel_id=1, source_target_pairs={{0,96},{16,112},{32,0},{48,16},{64,32},{80,48},{96,64},{112,80},{1... | collective-permute-start | bytes 2949128 | tf_op jit(solution)/shard_map/ppermute | solution.py:266
  46.7 28.3 %copy-start.4 = (bf16[2,2,2,2,16,1920]{5,4,3,2,1,0:T(8,128)(2,1)}, bf16[2,2,2,2,16,1920]{5,4,3,2,1,0:T(8,128)(2,1)S(1)}, u32[]{:S(2)}) copy-start(bf16[2,2,2,2,16,1920]{5,4,3,2,1,0:T(8,128)(2,1)S(1)} %collective-permute-done.1.refs_1_) | copy-start | bytes 2949124
  75.0 94.2 %all-to-all-start.1 = ((bf16[8,256,1920]{2,1,0:T(8,128)(2,1)}), bf16[8,256,1920]{2,1,0:T(8,128)(2,1)}, u32[]{:S(2)}, u32[]{:S(2)}) async-start(bf16[8,256,1920]{2,1,0:T(8,128)(2,1)} %bitcast.15), calls=%async_computation.1 | async-start | bytes 15728640 | tf_op jit(solution)/shard_map/all_to_all | solution.py:533
  168.8 13.1 %collective-permute-start.4 = (bf16[4,2,2,2,16,1920]{5,4,3,2,1,0:T(8,128)(2,1)}, bf16[4,2,2,2,16,1920]{5,4,3,2,1,0:T(8,128)(2,1)}, u32[]{:S(2)}, u32[]{:S(2)}) collective-permute-start(bf16[4,2,2,2,16,1920]{5,4,3,2,1,0:T(8,128)(2,1)} %bitcast.21), channel_id=1, source_target_pairs={{0,16},{16,0},{32,48},{48,32},{64,80},{80,64},{96,112},{112,96},{1... | collective-permute-start | bytes 5898248 | tf_op jit(solution)/shard_map/ppermute | solution.py:254
  169.2 12.5 %copy-start = (bf16[4,2,64,1920]{3,2,1,0:T(8,128)(2,1)S(1)}, bf16[4,2,64,1920]{3,2,1,0:T(8,128)(2,1)}, u32[]{:S(2)}) copy-start(bf16[4,2,64,1920]{3,2,1,0:T(8,128)(2,1)} %get-tuple-element.42) | copy-start | bytes 5898244
  169.2 71.1 %all-to-all-start.2 = ((bf16[16,64,1920]{2,1,0:T(8,128)(2,1)}), bf16[16,64,1920]{2,1,0:T(8,128)(2,1)}, u32[]{:S(2)}, u32[]{:S(2)}) async-start(bf16[16,64,1920]{2,1,0:T(8,128)(2,1)} %get-tuple-element.44), calls=%async_computation.2 | async-start | bytes 7864320 | tf_op jit(solution)/shard_map/all_to_all | solution.py:536
  183.6 25.1 %collective-permute-start.5 = (bf16[2,2,2,2,16,1920]{5,4,3,2,1,0:T(8,128)(2,1)S(1)}, bf16[2,2,2,2,16,1920]{5,4,3,2,1,0:T(8,128)(2,1)}, u32[]{:S(2)}, u32[]{:S(2)}) collective-permute-start(bf16[2,2,2,2,16,1920]{5,4,3,2,1,0:T(8,128)(2,1)S(1)} %pad_maximum_fusion.5), channel_id=1, source_target_pairs={{0,32},{16,48},{32,64},{48,80},{64,96},{80,112},{96,0},{112,16},{1... | collective-permute-start | bytes 2949128 | tf_op jit(solution)/shard_map/ppermute | solution.py:266
  186.5 23.7 %collective-permute-start.6 = (bf16[2,2,2,2,16,1920]{5,4,3,2,1,0:T(8,128)(2,1)}, bf16[2,2,2,2,16,1920]{5,4,3,2,1,0:T(8,128)(2,1)S(1)}, u32[]{:S(2)}, u32[]{:S(2)}) collective-permute-start(bf16[2,2,2,2,16,1920]{5,4,3,2,1,0:T(8,128)(2,1)} %pad_maximum_fusion.6), channel_id=1, source_target_pairs={{0,96},{16,112},{32,0},{48,16},{64,32},{80,48},{96,64},{112,80},{1... | collective-permute-start | bytes 2949128 | tf_op jit(solution)/shard_map/ppermute | solution.py:266
  210.1 0.9 copy-start.1
  211.1 7.9 %copy-start.3 = (f32[16,128]{1,0:T(8,128)S(1)}, f32[16,128]{1,0:T(8,128)}, u32[]{:S(2)}) copy-start(f32[16,128]{1,0:T(8,128)} %overlap.1) | copy-start | bytes 24580
  219.7 1.2 collective-permute-start.7
  220.9 3.7 %collective-permute-start.8 = (f32[16,128]{1,0:T(8,128)S(1)}, f32[16,128]{1,0:T(8,128)S(1)}, u32[]{:S(2)}, u32[]{:S(2)}) collective-permute-start(f32[16,128]{1,0:T(8,128)S(1)} %add.128), channel_id=1, source_target_pairs={{0,32},{16,48},{32,0},{48,16},{64,96},{80,112},{96,64},{112,80},{1... | collective-permute-start | bytes 24584 | tf_op jit(solution)/shard_map/ppermute | solution.py:245
  224.5 5.2 %collective-permute-start.9 = (f32[16,128]{1,0:T(8,128)S(1)}, f32[16,128]{1,0:T(8,128)S(1)}, u32[]{:S(2)}, u32[]{:S(2)}) collective-permute-start(f32[16,128]{1,0:T(8,128)S(1)} %add.129), channel_id=1, source_target_pairs={{0,64},{16,80},{32,96},{48,112},{64,0},{80,16},{96,32},{112,48},{1... | collective-permute-start | bytes 24584 | tf_op jit(solution)/shard_map/ppermute | solution.py:245
  229.7 3.7 %collective-permute-start.10 = (f32[16,128]{1,0:T(8,128)S(1)}, f32[16,128]{1,0:T(8,128)S(1)}, u32[]{:S(2)}, u32[]{:S(2)}) collective-permute-start(f32[16,128]{1,0:T(8,128)S(1)} %add.130), channel_id=1, source_target_pairs={{0,1},{1,0},{2,3},{3,2},{4,5},{5,4},{6,7},{7,6},{8,9},{9,8},{10,11... | collective-permute-start | bytes 24584 | tf_op jit(solution)/shard_map/ppermute | solution.py:245
  233.3 5.2 %collective-permute-start.11 = (f32[16,128]{1,0:T(8,128)S(1)}, f32[16,128]{1,0:T(8,128)S(1)}, u32[]{:S(2)}, u32[]{:S(2)}) collective-permute-start(f32[16,128]{1,0:T(8,128)S(1)} %add.131), channel_id=1, source_target_pairs={{0,2},{1,3},{2,0},{3,1},{4,6},{5,7},{6,4},{7,5},{8,10},{9,11},{10,... | collective-permute-start | bytes 24584 | tf_op jit(solution)/shard_map/ppermute | solution.py:245
  238.5 7.1 %collective-permute-start.12 = (f32[16,128]{1,0:T(8,128)S(1)}, f32[16,128]{1,0:T(8,128)S(1)}, u32[]{:S(2)}, u32[]{:S(2)}) collective-permute-start(f32[16,128]{1,0:T(8,128)S(1)} %add.132), channel_id=1, source_target_pairs={{0,4},{1,5},{2,6},{3,7},{4,0},{5,1},{6,2},{7,3},{8,12},{9,13},{10,... | collective-permute-start | bytes 24584 | tf_op jit(solution)/shard_map/ppermute | solution.py:245
  245.6 6.1 %collective-permute-start.13 = (f32[16,128]{1,0:T(8,128)S(1)}, f32[16,128]{1,0:T(8,128)S(1)}, u32[]{:S(2)}, u32[]{:S(2)}) collective-permute-start(f32[16,128]{1,0:T(8,128)S(1)} %add.133), channel_id=1, source_target_pairs={{0,8},{1,9},{2,10},{3,11},{4,12},{5,13},{6,14},{7,15},{8,0},{9,1},... | collective-permute-start | bytes 24584 | tf_op jit(solution)/shard_map/ppermute | solution.py:245

commit v5 on v4

--- a/solution.py
+++ b/solution.py
@@ -180,42 +180,55 @@
         out_ref[...] = complex_lanes(table, 0)
 
 
-def hamiltonian_kernel(me_ref, left_ref, left_far_ref, near_ref, before_ref, after_ref, far_ref, out_ref, *totals):
-    total, total_far = totals
+def near_kernel(me_ref, left_ref, left_far_ref, kept_near, got_near, kept_far, got_far, out_ref, total):
     step = pl.program_id(0)
-    product = products_of(left_ref[...].reshape(512, SLOTS), side_by_side([near_ref, before_ref, after_ref]))
-    product_far = products_of(left_far_ref[...].reshape(512, SLOTS), far_ref[...].reshape(128, SLOTS))
+    product = products_of(left_ref[...].reshape(512, SLOTS), side_by_side([kept_near, got_near]))
+    product += products_of(left_far_ref[...].reshape(512, SLOTS), side_by_side([kept_far, got_far]))
 
     @pl.when(step == 0)
     def _():
         total[...] = product
-        total_far[...] = product_far
 
     @pl.when(step == 1)
     def _():
         pick = selector(me_ref, 512, None)
-        table = exact(exact(pick, matched(total[...] + product), False), selector(me_ref, 384, (0, 1, 3)), True)
-        table += exact(
-            exact(pick, matched(total_far[...] + product_far), False), selector(me_ref, 128, (0,)), True
-        )
+        table = exact(exact(pick, matched(total[...] + product), False), selector(me_ref, 128, (0,)), True)
         out_ref[...] = complex_lanes(table, 32)
 
 
-def gram_call(kernel, me, operands, starts, scratch, name):
-    def spec(operand, start):
-        return pl.BlockSpec((operand.shape[0], 1, 2, 2, 16, SLOTS), lambda g: (0, start + g, 0, 0, 0, 0))
+def next_kernel(me_ref, left_ref, before_same, before_other, after_same, after_other, out_ref, total):
+    step = pl.program_id(0)
+    product = products_of(
+        left_ref[...].reshape(512, SLOTS), side_by_side([before_same, before_other, after_same, after_other])
+    )
+
+    @pl.when(step == 0)
+    def _():
+        total[...] = product
+
+    @pl.when(step == 1)
+    def _():
+        pick = selector(me_ref, 512, None)
+        table = exact(exact(pick, matched(total[...] + product), False), selector(me_ref, 256, (1, 3)), True)
+        out_ref[...] = complex_lanes(table, 32)
+
+
+def gram_call(kernel, me, operands, shape, name):
+    def spec(operand):
+        _, size, block, start = operand
+        return pl.BlockSpec((size, 1, 2, 2, 16, SLOTS), lambda g: (block, start + g, 0, 0, 0, 0))
 
     return pl.pallas_call(
         kernel,
         grid=(2,),
-        in_specs=[pl.BlockSpec(memory_space=pltpu.SMEM)] + [spec(operand, start) for operand, start in zip(operands, starts)],
+        in_specs=[pl.BlockSpec(memory_space=pltpu.SMEM)] + [spec(operand) for operand in operands],
         out_specs=pl.BlockSpec((16, 128), lambda g: (0, 0)),
         out_shape=jax.ShapeDtypeStruct((16, 128), jnp.float32),
-        scratch_shapes=[pltpu.VMEM(shape, jnp.float32) for shape in scratch],
+        scratch_shapes=[pltpu.VMEM(shape, jnp.float32)],
         compiler_params=pltpu.CompilerParams(vmem_limit_bytes=60 * MIB),
         cost_estimate=pl.CostEstimate(flops=2_000_000_000, bytes_accessed=8_000_000, transcendentals=0),
         name=name,
-    )(me, *operands)
+    )(me, *[operand[0] for operand in operands])
 
 
 def twofold_kernel(in_ref, out_ref):
@@ -249,9 +262,15 @@
     return values, tied
 
 
-def spread_blocks(kept, given, axis, tied, shifts):
-    chip = lax.axis_index(axis) // 2
-    got = lax.ppermute(given, axis, [(i, i ^ 1) for i in range(8)])
+def moved(values, shift, other):
+    return lax.ppermute(
+        values, "band", [(i, (i // 2 + shift) % 4 * 2 + (i % 2 + other) % 2) for i in range(8)]
+    )
+
+
+def spread_blocks(kept, given, tied):
+    chip = lax.axis_index("band") // 2
+    got = moved(given, 0, 1)
     pairs = []
     for shift in range(4):
         target = (chip + shift) % 4
@@ -260,18 +279,13 @@
                 [lax.dynamic_slice_in_dim(kept, target, 1, 0), lax.dynamic_slice_in_dim(got, target, 1, 0)], axis=0
             )
         )
-    if tied is not None:
-        tied, *pairs = lax.optimization_barrier((tied, *pairs))
-    for shift in shifts:
-        pairs[shift] = lax.ppermute(
-            pairs[shift], axis, [(i, (i // 2 + shift) % 4 * 2 + i % 2) for i in range(8)]
-        )
-    return pairs, tied
+    tied, *pairs = lax.optimization_barrier((tied, *pairs))
+    return [pairs[0]] + [moved(pairs[shift], shift, 0) for shift in (1, 2, 3)], tied
 
 
 def plane_kernel(
-    core_ref, place_ref, count_ref, upper_ref, wire_ref, field_ref, forward_ref, backward_ref,
-    out_ref, kept_ref, given_ref, grid_ref, mid_ref, back_ref, side_ref, stage_a, stage_b, list_ref, sems
+    me_ref, place_ref, count_ref, upper_ref, wire_hbm, field_ref, forward_ref, backward_ref,
+    out_ref, kept_ref, given_ref, next_same, next_other, last_same, last_other, grid_ref, mid_ref, back_ref, side_ref, wire_ref, stage_a, stage_b, list_ref, sems
 ):
     step = pl.program_id(0)
     lane = lax.broadcasted_iota(jnp.int32, (1, 128), 1)
@@ -290,6 +304,9 @@
 
     @pl.when(step == 0)
     def _():
+        fetch = pltpu.make_async_copy(wire_hbm, wire_ref, sems.at[0])
+        fetch.start()
+
         def clear(i, carry):
             grid_ref[pl.ds(pl.multiple_of(i * 512, 512), 512), :] = jnp.zeros((512, 128), jnp.float32)
             return carry
@@ -333,6 +350,7 @@
             spread(entry_b, stage_b)
             return carry
 
+        fetch.wait()
         stage_a[...] = rows_of(list_ref[0])
         lax.fori_loop(0, list_ref[255], scatter, 0)
 
@@ -400,7 +418,7 @@
         origin = pl.multiple_of((step - (pl.num_programs(0) - 1)) * 8, 8)
 
         def side_of(p):
-            return (p // 2 + core_ref[0]) % 2
+            return (p // 2 + me_ref[0]) % 2
 
         def gather(entry, stage):
             for u in range(128):
@@ -440,17 +458,26 @@
         lax.fori_loop(0, GROUPS, group, 0)
         gather(list_ref[0], stage_a)
         lax.fori_loop(0, list_ref[255], pick, 0)
-        copies = [
-            pltpu.make_async_copy(side_ref.at[0], kept_ref, sems.at[0]),
-            pltpu.make_async_copy(side_ref.at[1], given_ref, sems.at[1]),
+        chip = me_ref[0] // 2
+        after, far, before = (chip + 1) % 4, (chip + 2) % 4, (chip + 3) % 4
+        routes = [
+            (side_ref.at[0, after], next_same),
+            (side_ref.at[1, after], next_other),
+            (side_ref.at[0, before], last_same),
+            (side_ref.at[1, before], last_other),
+            (side_ref.at[1, chip], given_ref.at[0]),
+            (side_ref.at[1, far], given_ref.at[1]),
+            (side_ref.at[0, chip], kept_ref.at[0]),
+            (side_ref.at[0, far], kept_ref.at[1]),
         ]
+        copies = [pltpu.make_async_copy(*route, sems.at[1 + n]) for n, route in enumerate(routes)]
         for copy in copies:
             copy.start()
         for copy in copies:
             copy.wait()
 
 
-def plane_call(core, place, count, upper, wire, field, forward, backward):
+def plane_call(me, place, count, upper, wire, field, forward, backward):
     whole = lambda shape: pl.BlockSpec(shape, lambda i: (0,) * len(shape), pipeline_mode=pl.Buffered(1))
     return pl.pallas_call(
         plane_kernel,
@@ -460,28 +487,30 @@
             pl.BlockSpec(memory_space=pltpu.SMEM),
             pl.BlockSpec(memory_space=pltpu.SMEM),
             whole((GROUPS * SLOTS // 128, 128)),
-            whole((GROUPS, 64, SLOTS)),
+            pl.BlockSpec(memory_space=pl.ANY),
             pl.BlockSpec((PB, GRID, 128), lambda i: (i, 0, 0)),
             whole((GRID, 2 * BOX)),
             whole((BOX, 2 * GRID)),
         ],
-        out_specs=[whole((GROUPS, 64, SLOTS)), pl.BlockSpec(memory_space=pl.ANY), pl.BlockSpec(memory_space=pl.ANY)],
+        out_specs=[whole((GROUPS, 64, SLOTS))] + [pl.BlockSpec(memory_space=pl.ANY)] * 6,
         out_shape=[jax.ShapeDtypeStruct((GROUPS, 64, SLOTS), jnp.bfloat16)]
-        + [jax.ShapeDtypeStruct((4, 2, 64, SLOTS), jnp.bfloat16)] * 2,
+        + [jax.ShapeDtypeStruct((2, 2, 64, SLOTS), jnp.bfloat16)] * 2
+        + [jax.ShapeDtypeStruct((2, 64, SLOTS), jnp.bfloat16)] * 4,
         scratch_shapes=[
             pltpu.VMEM((ROWS + 8, 128), jnp.float32),
             pltpu.VMEM((PAIRS * PITCH, 128), jnp.float32),
             pltpu.VMEM((BOX * PITCHB, 128), jnp.float32),
             pltpu.VMEM((2, 4, 2, 64, SLOTS), jnp.bfloat16),
+            pltpu.VMEM((GROUPS, 64, SLOTS), jnp.bfloat16),
             pltpu.VMEM((128, 128), jnp.float32),
             pltpu.VMEM((128, 128), jnp.float32),
             pltpu.SMEM((256,), jnp.int32),
-            pltpu.SemaphoreType.DMA((2,)),
+            pltpu.SemaphoreType.DMA((9,)),
         ],
         compiler_params=pltpu.CompilerParams(vmem_limit_bytes=62 * MIB),
         cost_estimate=pl.CostEstimate(flops=13_000_000_000, bytes_accessed=24_000_000, transcendentals=0),
         name="planes",
-    )(core, place, count, upper, wire, field, forward, backward)
+    )(me, place, count, upper, wire, field, forward, backward)
 
 
 def field_kernel(lower_ref, upper_ref, out_ref):
@@ -525,30 +554,26 @@
 
     wire, kept, given = z_forward_call(core, orbitals.transpose(0, 2, 1), live, z_forward)
     incoming = lax.all_to_all(wire.reshape(GROUPS, 64, SLOTS), "fft", split_axis=0, concat_axis=0, tiled=True)
-    shares, potential = spread_blocks(kept, given, "band", potential, (1, 2, 3))
+    shares, potential = spread_blocks(kept, given, potential)
     field = field_call(potential)
     incoming, field, place, count, upper, *shares = lax.optimization_barrier(
         (incoming, field, place, count, upper, *shares)
     )
     left = lax.all_to_all(twofold_call(incoming), "band", split_axis=0, concat_axis=0, tiled=True)
     left = left.reshape(8, 4, 2, 2, 16, SLOTS)
-    outgoing, kept, given = plane_call(core, place, count, upper, incoming, field, forward, backward)
+    outgoing, kept, given, *sides = plane_call(me, place, count, upper, incoming, field, forward, backward)
+    piece = (1, 2, 2, 2, 16, SLOTS)
+    sides = [side.reshape(piece) for side in sides]
+    arrived = [moved(side, shift, other) for side, (shift, other) in zip(sides, ((1, 0), (1, 1), (3, 0), (3, 1)))]
+    kept, got = kept.reshape(2, 2, 2, 2, 16, SLOTS), moved(given.reshape(2, 2, 2, 2, 16, SLOTS), 0, 1)
     returned = lax.all_to_all(outgoing, "fft", split_axis=0, concat_axis=0, tiled=True)
-    split = (4, 2, 2, 2, 16, SLOTS)
-    (near, before, opposite, after), _ = spread_blocks(
-        kept.reshape(split), given.reshape(split), "band", None, (1, 3)
-    )
-    product_s = gram_call(overlap_kernel, me, shares, (0, 0, 0, 0), [(512, 512)], "overlap")
-    product_h = gram_call(
-        hamiltonian_kernel,
-        me,
-        [left, left, near, before, after, opposite],
-        (0, 2, 0, 0, 0, 0),
-        [(512, 384), (512, 128)],
-        "hamiltonian",
-    )
+    products = gram_call(overlap_kernel, me, [(share, 2, 0, 0) for share in shares], (512, 512), "overlap")
+    lefts = [(left, 8, 0, 0), (left, 8, 0, 2)]
+    nears = [(kept, 1, 0, 0), (got, 1, 0, 0), (kept, 1, 1, 0), (got, 1, 1, 0)]
+    products += gram_call(near_kernel, me, lefts + nears, (512, 128), "near")
+    products += gram_call(next_kernel, me, lefts[:1] + [(side, 1, 0, 0) for side in arrived], (512, 256), "next")
     applied = z_backward_call(returned.reshape(GROUPS, 2, 2, ZPAD, SLOTS), live, z_backward)
-    products, _ = summed(product_s + product_h, "band", (1, 2, 4))
+    products, _ = summed(products, "band", (1, 2, 4))
     products, _ = summed(products, "fft", (1, 2))
     products, applied = summed(products, "fft", (4,), applied)
     products, _ = summed(products, "fft", (8,))

time: 256 us -> 257 us (level)
  Pallas kernels: 127 us -> 132 us
  waiting for transfers between devices: 60 us -> 56.4 us
  other arithmetic: 8.4 us -> 5.11 us
  starting transfers between devices: 50.5 us -> 53.2 us
    ppermute x7 -> x9, waiting for transfers between devices: 47.5 us -> 42.2 us  [moved(): lax.ppermute(values, 'band', [(i, (i // 2 + shift) % 4 * 2 + (i % 2 + oth...]
    concatenate x6 -> x2, other arithmetic: 4.67 us -> 1.38 us  [spread_blocks(): jnp.concatenate([lax.dynamic_slice_in_dim(kept, target, 1, 0), lax.dynami...]
    pallas_call x2 -> x3, Pallas kernels: 13.7 us -> 16.7 us  [gram_call(): pl.pallas_call(kernel, grid=(2,), in_specs=[pl.BlockSpec(memory_space=plt...]
    ppermute x7 -> x9, starting transfers between devices: 9.38 us -> 10.7 us  [moved(): lax.ppermute(values, 'band', [(i, (i // 2 + shift) % 4 * 2 + (i % 2 + oth...]
  transfers between devices with their start and end apart: 17 -> 19, of which waited for: 11 -> 11; matrix products, arithmetic and copies ran while one was open for 4% -> 2% of each run, Pallas kernels for 45% -> 48%
where the time goes in v5:
time: 257 us; the launch traced here: 252 us
  Pallas kernels  132 us (51%)
  waiting for transfers between devices  56.4 us (22%)
  starting transfers between devices  53.2 us (21%)
  other arithmetic  5.11 us (2%)
  local copies, waits for them, and re-layouts  4.93 us (2%)
    pallas_call x1, Pallas kernels, plane_call(): pl.pallas_call(plane_kernel, grid=(PAIRS // PB,), in_specs=[pl.BlockSpec(...  90.9 us
    ppermute x9, waiting for transfers between devices, moved(): lax.ppermute(values, 'band', [(i, (i // 2 + shift) % 4 * 2 + (i % 2 + oth...  42.2 us
    ppermute x7, starting transfers between devices, summed(): received = lax.ppermute(values, axis, [(i, i ^ step) for i in range(size)])  16.8 us
    pallas_call x3, Pallas kernels, gram_call(): pl.pallas_call(kernel, grid=(2,), in_specs=[pl.BlockSpec(memory_space=plt...  16.7 us
    ppermute x7, waiting for transfers between devices, summed(): received = lax.ppermute(values, axis, [(i, i ^ step) for i in range(size)])  12.9 us
    all_to_all x1, starting transfers between devices, local(): lax.all_to_all(outgoing, 'fft', split_axis=0, concat_axis=0, tiled=True)  12.5 us
    ppermute x9, starting transfers between devices, moved(): lax.ppermute(values, 'band', [(i, (i // 2 + shift) % 4 * 2 + (i % 2 + oth...  10.7 us
    all_to_all x1, starting transfers between devices, local(): lax.all_to_all(wire.reshape(GROUPS, 64, SLOTS), 'fft', split_axis=0, conc...  8.32 us
  transfers between devices with their start and end apart: 19, of which 11 were waited for; matrix products, arithmetic and copies ran while one was open for 2% of the time, Pallas kernels for 48%

profile of v5, /device:TPU:0, one launch (start us, length us, event | category | flops | bytes accessed | tf_op | source)
XLA Modules:
  0.0 252.2 jit_solution(6690895253922914030)
XLA Ops:
  0.6 0.8 fusion.3
  1.4 0.6 reshape.67.live_ref
  2.0 7.0 %z_forward.1 = (bf16[16,2,2,16,1920]{4,3,2,1,0:T(8,128)(2,1)}, bf16[4,2,2,2,16,1920]{5,4,3,2,1,0:T(8,128)(2,1)}, bf16[4,2,2,2,16,1920]{5,4,3,2,1,0:T(8,128)(2,1)}) custom-call(s32[1]{0:T(128)S(6)} %select_n.74.core_ref, bf16[2,480,1920]{2,1,0:T(8,128)(2,1)} %bitcast.25, f32[1,1920]{1,0:T(1,128)} %reshape.67.live_ref, bf16[512,480]{1,0:T(8,128)(2,1)} %constant.128.clone.table_ref), custom_call_target="tpu_custom_call" | custom-call | flops 1800000000 | bytes 12000000 | tf_op jit(solution)/shard_map/z_forward/pallas_call | solution.py:82
  9.0 0.0 collective-permute-start
  9.0 8.3 %all-to-all-start = ((bf16[16,64,1920]{2,1,0:T(8,128)(2,1)}), bf16[16,64,1920]{2,1,0:T(8,128)(2,1)}, u32[]{:S(2)}, u32[]{:S(2)}) async-start(bf16[16,64,1920]{2,1,0:T(8,128)(2,1)} %bitcast.20), calls=%async_computation | async-start | bytes 7864320 | tf_op jit(solution)/shard_map/all_to_all | solution.py:556
  17.4 0.7 convert_bitcast_fusion
  18.2 0.1 reduce_sum.9
  18.3 1.6 constant_dynamic-slice_fusion.1
  19.9 0.0 collective-permute-done
  20.0 0.2 constant_dynamic-slice_fusion
  20.1 0.2 pad_maximum_fusion.2
  20.3 1.2 pad_maximum_fusion
  21.5 1.5 collective-permute-start.1
  23.0 2.7 %collective-permute-start.2 = (bf16[2,2,2,2,16,1920]{5,4,3,2,1,0:T(8,128)(2,1)S(1)}, bf16[2,2,2,2,16,1920]{5,4,3,2,1,0:T(8,128)(2,1)}, u32[]{:S(2)}, u32[]{:S(2)}) collective-permute-start(bf16[2,2,2,2,16,1920]{5,4,3,2,1,0:T(8,128)(2,1)S(1)} %get-tuple-element.35), channel_id=1, source_target_pairs={{0,64},{16,80},{32,96},{48,112},{64,0},{80,16},{96,32},{112,48},{1... | collective-permute-start | bytes 2949128 | tf_op jit(solution)/shard_map/ppermute | solution.py:266
  25.7 1.4 collective-permute-start.3
  27.2 0.5 and_select_fusion.count_ref
  27.7 0.8 add_select_fusion.2.place_ref
  28.5 7.0 %field.1.field_ref = bf16[120,240,128]{2,1,0:T(8,128)(2,1)} custom-call(f32[15,57600]{1,0:T(8,128)} %upper_ref, f32[15,57600]{1,0:T(8,128)} %upper_ref), custom_call_target="tpu_custom_call" | custom-call | bytes 18000000 | tf_op jit(solution)/shard_map/field/pallas_call | solution.py:526
  35.5 11.1 %collective-permute-done.1.refs_1_ = bf16[2,2,2,2,16,1920]{5,4,3,2,1,0:T(8,128)(2,1)S(1)} collective-permute-done((bf16[2,2,2,2,16,1920]{5,4,3,2,1,0:T(8,128)(2,1)S(1)}, bf16[2,2,2,2,16,1920]{5,4,3,2,1,0:T(8,128)(2,1)S(1)}, u32[]{:S(2)}, u32[]{:S(2)}) %collective-permute-start.1) | collective-permute-done | bytes 983072 | tf_op jit(solution)/shard_map/ppermute | solution.py:266
  46.6 22.2 %collective-permute-done.2.refs_2_ = bf16[2,2,2,2,16,1920]{5,4,3,2,1,0:T(8,128)(2,1)} collective-permute-done((bf16[2,2,2,2,16,1920]{5,4,3,2,1,0:T(8,128)(2,1)S(1)}, bf16[2,2,2,2,16,1920]{5,4,3,2,1,0:T(8,128)(2,1)}, u32[]{:S(2)}, u32[]{:S(2)}) %collective-permute-start.2) | collective-permute-done | bytes 983072 | tf_op jit(solution)/shard_map/ppermute | solution.py:266
  68.8 0.0 collective-permute-done.3.refs_3_
  68.8 1.3 all-to-all-done.wire_hbm
  70.0 4.9 %twofold.1 = bf16[2,4,2,128,1920]{4,3,2,1,0:T(8,128)(2,1)} custom-call(bf16[2,4,128,1920]{3,2,1,0:T(8,128)(2,1)} %bitcast.4.in_ref), custom_call_target="tpu_custom_call" | custom-call | bytes 12000000 | tf_op jit(solution)/shard_map/twofold/pallas_call | solution.py:242
  74.9 0.0 copy-done.8
  74.9 4.9 %all-to-all-start.1 = ((bf16[8,256,1920]{2,1,0:T(8,128)(2,1)}), bf16[8,256,1920]{2,1,0:T(8,128)(2,1)}, u32[]{:S(2)}, u32[]{:S(2)}) async-start(bf16[8,256,1920]{2,1,0:T(8,128)(2,1)} %bitcast.19), calls=%async_computation.1 | async-start | bytes 15728640 | tf_op jit(solution)/shard_map/all_to_all | solution.py:562
  79.8 90.9 %planes.1 = (bf16[16,64,1920]{2,1,0:T(8,128)(2,1)}, bf16[2,2,64,1920]{3,2,1,0:T(8,128)(2,1)}, bf16[2,2,64,1920]{3,2,1,0:T(8,128)(2,1)}, bf16[2,64,1920]{2,1,0:T(...) custom-call(s32[1]{0:T(128)} %bitcast.me_ref, ...), custom_call_target="tpu_custom_call" | custom-call | flops 12999999488 | bytes 24000000 | tf_op jit(solution)/shard_map/planes/pallas_call | solution.py:482
  170.7 0.0 all-to-all-done.1
  170.7 12.5 %all-to-all-start.2 = ((bf16[16,64,1920]{2,1,0:T(8,128)(2,1)}), bf16[16,64,1920]{2,1,0:T(8,128)(2,1)}, u32[]{:S(2)}, u32[]{:S(2)}) async-start(bf16[16,64,1920]{2,1,0:T(8,128)(2,1)} %get-tuple-element.52), calls=%async_computation.2 | async-start | bytes 7864320 | tf_op jit(solution)/shard_map/all_to_all | solution.py:569
  183.3 0.1 collective-permute-start.4
  183.4 1.9 collective-permute-start.5
  185.2 1.3 collective-permute-start.6
  186.5 1.8 collective-permute-start.7
  188.3 0.0 collective-permute-start.8
  188.3 5.8 %overlap.1 = f32[16,128]{1,0:T(8,128)} custom-call(s32[1]{0:T(128)} %bitcast.me_ref, bf16[2,2,2,2,16,1920]{5,4,3,2,1,0:T(8,128)(2,1)} %get-tuple-element.37.refs_0_, bf16[2,2,2,2,16,1920]{5,4,3,2,1,0:T(8,128)(2,1)} %copy-done.8, bf16[2,2,2,2,16,1920]{5,4,3,2,1,0:T(8,128)(2,1)} %collective-permute-done.2.refs_2_, ...), custom_call_target="tpu_custom_call" | custom-call | flops 2000000000 | bytes 8000000 | tf_op jit(solution)/shard_map/overlap/pallas_call | solution.py:221
  194.1 0.0 collective-permute-done.4.got_near.got_far
  194.1 1.0 copy-done
  195.1 6.2 %near.1 = f32[16,128]{1,0:T(8,128)} custom-call(s32[1]{0:T(128)} %bitcast.me_ref, bf16[8,4,2,2,16,1920]{5,4,3,2,1,0:T(8,128)(2,1)} %bitcast.6.left_ref.left_far_ref, bf16[8,4,2,2,16,1920]{5,4,3,2,1,0:T(8,128)(2,1)} %bitcast.6.left_ref.left_far_ref, bf16[2,2,2,2,16,1920]{5,4,3,2,1,0:T(8,128)(2,1)} %bitcast.21, bf16[2,2,2,2,16,1920]{5,4,3,2,1,0:T(8,128)(2,1)} %copy-done, ...), custom_call_target="tpu_custom_call" | custom-call | flops 2000000000 | bytes 8000000 | tf_op jit(solution)/shard_map/near/pallas_call | solution.py:221
  201.2 0.0 collective-permute-done.5.before_same
  201.2 0.0 copy-start.2
  201.3 7.5 %collective-permute-done.6.before_other = bf16[1,2,2,2,16,1920]{5,4,3,2,1,0:T(8,128)(2,1)S(1)} collective-permute-done((bf16[1,2,2,2,16,1920]{5,4,3,2,1,0:T(8,128)(2,1)}, bf16[1,2,2,2,16,1920]{5,4,3,2,1,0:T(8,128)(2,1)S(1)}, u32[]{:S(2)}, u32[]{:S(2)}) %collective-permute-start.6) | collective-permute-done | bytes 491552 | tf_op jit(solution)/shard_map/ppermute | solution.py:266
  208.7 0.0 collective-permute-done.7.after_same
  208.7 1.4 collective-permute-done.8.after_other
  210.1 0.0 copy-done.2
  210.2 0.8 copy-done.5
  211.0 4.8 %next.1 = f32[16,128]{1,0:T(8,128)} custom-call(s32[1]{0:T(128)} %bitcast.me_ref, bf16[8,4,2,2,16,1920]{5,4,3,2,1,0:T(8,128)(2,1)} %bitcast.6.left_ref.left_far_ref, bf16[1,2,2,2,16,1920]{5,4,3,2,1,0:T(8,128)(2,1)} %copy-done.2, bf16[1,2,2,2,16,1920]{5,4,3,2,1,0:T(8,128)(2,1)} %copy-done.3, bf16[1,2,2,2,16,1920]{5,4,3,2,1,0:T(8,128)(2,1)} %copy-done.4, ...), custom_call_target="tpu_custom_call" | custom-call | flops 2000000000 | bytes 8000000 | tf_op jit(solution)/shard_map/next/pallas_call | solution.py:221
  215.8 0.7 add_add_fusion
  216.5 0.8 collective-permute-start.9
  217.3 0.8 collective-permute-done.9
  218.1 1.2 collective-permute-start.10
  219.3 2.5 collective-permute-done.10
  221.7 2.4 collective-permute-start.11
  224.1 2.8 %collective-permute-done.11 = f32[16,128]{1,0:T(8,128)S(1)} collective-permute-done((f32[16,128]{1,0:T(8,128)S(1)}, f32[16,128]{1,0:T(8,128)S(1)}, u32[]{:S(2)}, u32[]{:S(2)}) %collective-permute-start.11) | collective-permute-done | bytes 8224 | tf_op jit(solution)/shard_map/ppermute | solution.py:258
  226.9 1.9 collective-permute-start.12
  228.8 2.6 %collective-permute-done.12 = f32[16,128]{1,0:T(8,128)S(1)} collective-permute-done((f32[16,128]{1,0:T(8,128)S(1)}, f32[16,128]{1,0:T(8,128)S(1)}, u32[]{:S(2)}, u32[]{:S(2)}) %collective-permute-start.12) | collective-permute-done | bytes 8224 | tf_op jit(solution)/shard_map/ppermute | solution.py:258
  231.4 7.2 %collective-permute-start.13 = (f32[16,128]{1,0:T(8,128)S(1)}, f32[16,128]{1,0:T(8,128)S(1)}, u32[]{:S(2)}, u32[]{:S(2)}) collective-permute-start(f32[16,128]{1,0:T(8,128)S(1)} %add.120), channel_id=1, source_target_pairs={{0,2},{1,3},{2,0},{3,1},{4,6},{5,7},{6,4},{7,5},{8,10},{9,11},{10,... | collective-permute-start | bytes 24584 | tf_op jit(solution)/shard_map/ppermute | solution.py:258
  238.5 1.6 collective-permute-done.13
  240.2 0.8 collective-permute-start.14
  241.0 0.0 all-to-all-done.2
  241.0 5.3 %z_backward.1 = bf16[2,480,1920]{2,1,0:T(8,128)(2,1)} custom-call(bf16[16,2,2,16,1920]{4,3,2,1,0:T(8,128)(2,1)} %bitcast.13.wire_ref, f32[1,1920]{1,0:T(1,128)} %reshape.67.live_ref, bf16[480,512]{1,0:T(8,128)(2,1)} %constant.129.clone.table_ref), custom_call_target="tpu_custom_call" | custom-call | flops 1800000000 | bytes 8000000 | tf_op jit(solution)/shard_map/z_backward/pallas_call | solution.py:108
  246.3 0.0 collective-permute-done.14
  246.3 2.6 %collective-permute-start.15 = (f32[16,128]{1,0:T(8,128)S(1)}, f32[16,128]{1,0:T(8,128)S(1)}, u32[]{:S(2)}, u32[]{:S(2)}) collective-permute-start(f32[16,128]{1,0:T(8,128)S(1)} %add.122), channel_id=1, source_target_pairs={{0,8},{1,9},{2,10},{3,11},{4,12},{5,13},{6,14},{7,15},{8,0},{9,1},... | collective-permute-start | bytes 24584 | tf_op jit(solution)/shard_map/ppermute | solution.py:258
  248.8 2.7 %collective-permute-done.15 = f32[16,128]{1,0:T(8,128)S(1)} collective-permute-done((f32[16,128]{1,0:T(8,128)S(1)}, f32[16,128]{1,0:T(8,128)S(1)}, u32[]{:S(2)}, u32[]{:S(2)}) %collective-permute-start.15) | collective-permute-done | bytes 8224 | tf_op jit(solution)/shard_map/ppermute | solution.py:258
  251.5 0.1 reshape.66
  251.6 0.6 fusion.4
  (24 shorter events, 0.1 us)
Async XLA Ops:
  9.0 11.0 %collective-permute-start = (bf16[4,2,2,2,16,1920]{5,4,3,2,1,0:T(8,128)(2,1)}, bf16[4,2,2,2,16,1920]{5,4,3,2,1,0:T(8,128)(2,1)S(1)}, u32[]{:S(2)}, u32[]{:S(2)}) collective-permute-start(bf16[4,2,2,2,16,1920]{5,4,3,2,1,0:T(8,128)(2,1)} %get-tuple-element.31), channel_id=1, source_target_pairs={{0,16},{16,0},{32,48},{48,32},{64,80},{80,64},{96,112},{112,96},{1... | collective-permute-start | bytes 5898248 | tf_op jit(solution)/shard_map/ppermute | solution.py:266
  9.0 8.4 %copy-start.1 = (s32[30720]{0:T(1024)S(1)}, s32[30720]{0:T(1024)}, u32[]{:S(2)}) copy-start(s32[30720]{0:T(1024)} %param.10) | copy-start | bytes 368644
  9.0 61.0 %all-to-all-start = ((bf16[16,64,1920]{2,1,0:T(8,128)(2,1)}), bf16[16,64,1920]{2,1,0:T(8,128)(2,1)}, u32[]{:S(2)}, u32[]{:S(2)}) async-start(bf16[16,64,1920]{2,1,0:T(8,128)(2,1)} %bitcast.20), calls=%async_computation | async-start | bytes 7864320 | tf_op jit(solution)/shard_map/all_to_all | solution.py:556
  21.5 25.1 %collective-permute-start.1 = (bf16[2,2,2,2,16,1920]{5,4,3,2,1,0:T(8,128)(2,1)S(1)}, bf16[2,2,2,2,16,1920]{5,4,3,2,1,0:T(8,128)(2,1)S(1)}, u32[]{:S(2)}, u32[]{:S(2)}) collective-permute-start(bf16[2,2,2,2,16,1920]{5,4,3,2,1,0:T(8,128)(2,1)S(1)} %get-tuple-element.34), channel_id=1, source_target_pairs={{0,32},{16,48},{32,64},{48,80},{64,96},{80,112},{96,0},{112,16},{1... | collective-permute-start | bytes 2949128 | tf_op jit(solution)/shard_map/ppermute | solution.py:266
  23.0 45.7 %collective-permute-start.2 = (bf16[2,2,2,2,16,1920]{5,4,3,2,1,0:T(8,128)(2,1)S(1)}, bf16[2,2,2,2,16,1920]{5,4,3,2,1,0:T(8,128)(2,1)}, u32[]{:S(2)}, u32[]{:S(2)}) collective-permute-start(bf16[2,2,2,2,16,1920]{5,4,3,2,1,0:T(8,128)(2,1)S(1)} %get-tuple-element.35), channel_id=1, source_target_pairs={{0,64},{16,80},{32,96},{48,112},{64,0},{80,16},{96,32},{112,48},{1... | collective-permute-start | bytes 2949128 | tf_op jit(solution)/shard_map/ppermute | solution.py:266
  25.7 43.0 %collective-permute-start.3 = (bf16[2,2,2,2,16,1920]{5,4,3,2,1,0:T(8,128)(2,1)S(1)}, bf16[2,2,2,2,16,1920]{5,4,3,2,1,0:T(8,128)(2,1)}, u32[]{:S(2)}, u32[]{:S(2)}) collective-permute-start(bf16[2,2,2,2,16,1920]{5,4,3,2,1,0:T(8,128)(2,1)S(1)} %get-tuple-element.36), channel_id=1, source_target_pairs={{0,96},{16,112},{32,0},{48,16},{64,32},{80,48},{96,64},{112,80},{1... | collective-permute-start | bytes 2949128 | tf_op jit(solution)/shard_map/ppermute | solution.py:266
  46.6 28.3 %copy-start.8 = (bf16[2,2,2,2,16,1920]{5,4,3,2,1,0:T(8,128)(2,1)}, bf16[2,2,2,2,16,1920]{5,4,3,2,1,0:T(8,128)(2,1)S(1)}, u32[]{:S(2)}) copy-start(bf16[2,2,2,2,16,1920]{5,4,3,2,1,0:T(8,128)(2,1)S(1)} %collective-permute-done.1.refs_1_) | copy-start | bytes 2949124
  74.9 95.8 %all-to-all-start.1 = ((bf16[8,256,1920]{2,1,0:T(8,128)(2,1)}), bf16[8,256,1920]{2,1,0:T(8,128)(2,1)}, u32[]{:S(2)}, u32[]{:S(2)}) async-start(bf16[8,256,1920]{2,1,0:T(8,128)(2,1)} %bitcast.19), calls=%async_computation.1 | async-start | bytes 15728640 | tf_op jit(solution)/shard_map/all_to_all | solution.py:562
  170.7 12.5 %copy-start.9 = (bf16[2,2,64,1920]{3,2,1,0:T(8,128)(2,1)S(1)}, bf16[2,2,64,1920]{3,2,1,0:T(8,128)(2,1)}, u32[]{:S(2)}) copy-start(bf16[2,2,64,1920]{3,2,1,0:T(8,128)(2,1)} %get-tuple-element.47) | copy-start | bytes 2949124
  170.7 70.2 %all-to-all-start.2 = ((bf16[16,64,1920]{2,1,0:T(8,128)(2,1)}), bf16[16,64,1920]{2,1,0:T(8,128)(2,1)}, u32[]{:S(2)}, u32[]{:S(2)}) async-start(bf16[16,64,1920]{2,1,0:T(8,128)(2,1)} %get-tuple-element.52), calls=%async_computation.2 | async-start | bytes 7864320 | tf_op jit(solution)/shard_map/all_to_all | solution.py:569
  183.3 10.8 %collective-permute-start.4 = (bf16[2,2,2,2,16,1920]{5,4,3,2,1,0:T(8,128)(2,1)S(1)}, bf16[2,2,2,2,16,1920]{5,4,3,2,1,0:T(8,128)(2,1)S(1)}, u32[]{:S(2)}, u32[]{:S(2)}) collective-permute-start(bf16[2,2,2,2,16,1920]{5,4,3,2,1,0:T(8,128)(2,1)S(1)} %bitcast.26), channel_id=1, source_target_pairs={{0,16},{16,0},{32,48},{48,32},{64,80},{80,64},{96,112},{112,96},{1... | collective-permute-start | bytes 2949128 | tf_op jit(solution)/shard_map/ppermute | solution.py:266
  183.4 17.9 %collective-permute-start.5 = (bf16[1,2,2,2,16,1920]{5,4,3,2,1,0:T(8,128)(2,1)}, bf16[1,2,2,2,16,1920]{5,4,3,2,1,0:T(8,128)(2,1)S(1)}, u32[]{:S(2)}, u32[]{:S(2)}) collective-permute-start(bf16[1,2,2,2,16,1920]{5,4,3,2,1,0:T(8,128)(2,1)} %bitcast.9), channel_id=1, source_target_pairs={{0,32},{16,48},{32,64},{48,80},{64,96},{80,112},{96,0},{112,16},{1... | collective-permute-start | bytes 1474568 | tf_op jit(solution)/shard_map/ppermute | solution.py:266
  185.2 23.5 %collective-permute-start.6 = (bf16[1,2,2,2,16,1920]{5,4,3,2,1,0:T(8,128)(2,1)}, bf16[1,2,2,2,16,1920]{5,4,3,2,1,0:T(8,128)(2,1)S(1)}, u32[]{:S(2)}, u32[]{:S(2)}) collective-permute-start(bf16[1,2,2,2,16,1920]{5,4,3,2,1,0:T(8,128)(2,1)} %bitcast.10), channel_id=1, source_target_pairs={{0,48},{16,32},{32,80},{48,64},{64,112},{80,96},{96,16},{112,0},{1... | collective-permute-start | bytes 1474568 | tf_op jit(solution)/shard_map/ppermute | solution.py:266
  186.5 22.2 %collective-permute-start.7 = (bf16[1,2,2,2,16,1920]{5,4,3,2,1,0:T(8,128)(2,1)}, bf16[1,2,2,2,16,1920]{5,4,3,2,1,0:T(8,128)(2,1)S(1)}, u32[]{:S(2)}, u32[]{:S(2)}) collective-permute-start(bf16[1,2,2,2,16,1920]{5,4,3,2,1,0:T(8,128)(2,1)} %bitcast.11), channel_id=1, source_target_pairs={{0,96},{16,112},{32,0},{48,16},{64,32},{80,48},{96,64},{112,80},{1... | collective-permute-start | bytes 1474568 | tf_op jit(solution)/shard_map/ppermute | solution.py:266
  188.3 21.9 %collective-permute-start.8 = (bf16[1,2,2,2,16,1920]{5,4,3,2,1,0:T(8,128)(2,1)}, bf16[1,2,2,2,16,1920]{5,4,3,2,1,0:T(8,128)(2,1)S(1)}, u32[]{:S(2)}, u32[]{:S(2)}) collective-permute-start(bf16[1,2,2,2,16,1920]{5,4,3,2,1,0:T(8,128)(2,1)} %bitcast.27), channel_id=1, source_target_pairs={{0,112},{16,96},{32,16},{48,0},{64,48},{80,32},{96,80},{112,64},{1... | collective-permute-start | bytes 1474568 | tf_op jit(solution)/shard_map/ppermute | solution.py:266
  194.1 1.0 copy-start
  201.2 14.5 %copy-start.6 = (f32[16,128]{1,0:T(8,128)S(1)}, f32[16,128]{1,0:T(8,128)}, u32[]{:S(2)}) copy-start(f32[16,128]{1,0:T(8,128)} %near.1) | copy-start | bytes 24580
  201.2 14.5 %copy-start.7 = (f32[16,128]{1,0:T(8,128)S(1)}, f32[16,128]{1,0:T(8,128)}, u32[]{:S(2)}) copy-start(f32[16,128]{1,0:T(8,128)} %overlap.1) | copy-start | bytes 24580
  201.2 8.9 %copy-start.2 = (bf16[1,2,2,2,16,1920]{5,4,3,2,1,0:T(8,128)(2,1)}, bf16[1,2,2,2,16,1920]{5,4,3,2,1,0:T(8,128)(2,1)S(1)}, u32[]{:S(2)}) copy-start(bf16[1,2,2,2,16,1920]{5,4,3,2,1,0:T(8,128)(2,1)S(1)} %collective-permute-done.5.before_same) | copy-start | bytes 1474564
  208.7 1.4 copy-start.3
  208.7 1.4 copy-start.4
  210.2 0.8 copy-start.5
  216.5 1.6 collective-permute-start.9
  218.1 3.7 %collective-permute-start.10 = (f32[16,128]{1,0:T(8,128)S(1)}, f32[16,128]{1,0:T(8,128)S(1)}, u32[]{:S(2)}, u32[]{:S(2)}) collective-permute-start(f32[16,128]{1,0:T(8,128)S(1)} %add.117), channel_id=1, source_target_pairs={{0,32},{16,48},{32,0},{48,16},{64,96},{80,112},{96,64},{112,80},{1... | collective-permute-start | bytes 24584 | tf_op jit(solution)/shard_map/ppermute | solution.py:258
  221.7 5.2 %collective-permute-start.11 = (f32[16,128]{1,0:T(8,128)S(1)}, f32[16,128]{1,0:T(8,128)S(1)}, u32[]{:S(2)}, u32[]{:S(2)}) collective-permute-start(f32[16,128]{1,0:T(8,128)S(1)} %add.118), channel_id=1, source_target_pairs={{0,64},{16,80},{32,96},{48,112},{64,0},{80,16},{96,32},{112,48},{1... | collective-permute-start | bytes 24584 | tf_op jit(solution)/shard_map/ppermute | solution.py:258
  226.9 4.5 %collective-permute-start.12 = (f32[16,128]{1,0:T(8,128)S(1)}, f32[16,128]{1,0:T(8,128)S(1)}, u32[]{:S(2)}, u32[]{:S(2)}) collective-permute-start(f32[16,128]{1,0:T(8,128)S(1)} %add.119), channel_id=1, source_target_pairs={{0,1},{1,0},{2,3},{3,2},{4,5},{5,4},{6,7},{7,6},{8,9},{9,8},{10,11... | collective-permute-start | bytes 24584 | tf_op jit(solution)/shard_map/ppermute | solution.py:258
  231.4 8.8 %collective-permute-start.13 = (f32[16,128]{1,0:T(8,128)S(1)}, f32[16,128]{1,0:T(8,128)S(1)}, u32[]{:S(2)}, u32[]{:S(2)}) collective-permute-start(f32[16,128]{1,0:T(8,128)S(1)} %add.120), channel_id=1, source_target_pairs={{0,2},{1,3},{2,0},{3,1},{4,6},{5,7},{6,4},{7,5},{8,10},{9,11},{10,... | collective-permute-start | bytes 24584 | tf_op jit(solution)/shard_map/ppermute | solution.py:258
  240.2 6.1 %collective-permute-start.14 = (f32[16,128]{1,0:T(8,128)S(1)}, f32[16,128]{1,0:T(8,128)S(1)}, u32[]{:S(2)}, u32[]{:S(2)}) collective-permute-start(f32[16,128]{1,0:T(8,128)S(1)} %add.121), channel_id=1, source_target_pairs={{0,4},{1,5},{2,6},{3,7},{4,0},{5,1},{6,2},{7,3},{8,12},{9,13},{10,... | collective-permute-start | bytes 24584 | tf_op jit(solution)/shard_map/ppermute | solution.py:258
  246.3 5.2 %collective-permute-start.15 = (f32[16,128]{1,0:T(8,128)S(1)}, f32[16,128]{1,0:T(8,128)S(1)}, u32[]{:S(2)}, u32[]{:S(2)}) collective-permute-start(f32[16,128]{1,0:T(8,128)S(1)} %add.122), channel_id=1, source_target_pairs={{0,8},{1,9},{2,10},{3,11},{4,12},{5,13},{6,14},{7,15},{8,0},{9,1},... | collective-permute-start | bytes 24584 | tf_op jit(solution)/shard_map/ppermute | solution.py:258

commit v6 on v5

--- a/solution.py
+++ b/solution.py
@@ -23,9 +23,9 @@
 PITCH = 200
 PITCHB = 120
 PB = 24
-N1 = 8
+N1 = 12
 N2 = 12
-N4 = 8
+N4 = 12
 MIB = 1 << 20
 
 
@@ -285,7 +285,7 @@
 
 def plane_kernel(
     me_ref, place_ref, count_ref, upper_ref, wire_hbm, field_ref, forward_ref, backward_ref,
-    out_ref, kept_ref, given_ref, next_same, next_other, last_same, last_other, grid_ref, mid_ref, back_ref, side_ref, wire_ref, stage_a, stage_b, list_ref, sems
+    out_hbm, kept_ref, given_ref, next_same, next_other, last_same, last_other, grid_ref, mid_ref, back_ref, side_ref, wire_ref, out_ref, stage_a, stage_b, stage_c, stage_d, list_ref, sems
 ):
     step = pl.program_id(0)
     lane = lax.broadcasted_iota(jnp.int32, (1, 128), 1)
@@ -324,8 +324,9 @@
         total = lax.fori_loop(0, GROUPS, group, 0)
         list_ref[total] = list_ref[total - 1]
         list_ref[total + 1] = list_ref[total - 1]
-        list_ref[total + 2] = list_ref[total - 1]
-        list_ref[255] = (total + 1) // 2
+        for extra in range(2, 7):
+            list_ref[total + extra] = list_ref[total - 1]
+        list_ref[263] = (total + 1) // 2
         eye_row = lax.broadcasted_iota(jnp.int32, (128, 128), 0)
         eye_column = lax.broadcasted_iota(jnp.int32, (128, 128), 1)
         eye = jnp.where(eye_row == eye_column, 1.0, 0.0).astype(jnp.bfloat16)
@@ -352,7 +353,7 @@
 
         fetch.wait()
         stage_a[...] = rows_of(list_ref[0])
-        lax.fori_loop(0, list_ref[255], scatter, 0)
+        lax.fori_loop(0, list_ref[263], scatter, 0)
 
         def x_forward(i, carry):
             parts = []
@@ -420,29 +421,30 @@
         def side_of(p):
             return (p // 2 + me_ref[0]) % 2
 
-        def gather(entry, stage):
-            for u in range(128):
-                stage[pl.ds(origin + u, 1), :] = grid_ref[pl.ds(place_ref[entry * 128 + u], 1), :]
-
-        def write(entry, stage):
-            p = entry // 15
-            base = pl.multiple_of((entry - p * 15) * 128, 128)
+        def write_two(entry, entry_b, stage):
             both = lax.dot_general(
                 select, stage[...].astype(jnp.bfloat16), (((1,), (1,)), ((), ())), preferred_element_type=jnp.float32
             )
-            upper = upper_ref[pl.ds(entry, 1), :] > 0.0
-            values = jnp.where(upper, both[64:], both[:64]).astype(jnp.bfloat16)
-            out_ref[p, :, pl.ds(base, 128)] = values
-            side_ref[side_of(p), p // 4, p % 2, :, pl.ds(base, 128)] = values
-
-        def pick(i, carry):
-            entry = list_ref[2 * i]
-            entry_b = list_ref[2 * i + 1]
-            entry_c = list_ref[2 * i + 2]
-            gather(entry_b, stage_b)
-            write(entry, stage_a)
-            gather(entry_c, stage_a)
-            write(entry_b, stage_b)
+            for n, e in enumerate((entry, entry_b)):
+                p = e // 15
+                base = pl.multiple_of((e - p * 15) * 128, 128)
+                upper = upper_ref[pl.ds(e, 1), :] > 0.0
+                part = both[:, n * 128 : (n + 1) * 128]
+                values = jnp.where(upper, part[64:], part[:64]).astype(jnp.bfloat16)
+                out_ref[p, :, pl.ds(base, 128)] = values
+                side_ref[side_of(p), p // 4, p % 2, :, pl.ds(base, 128)] = values
+
+        def gather_two(entry, entry_b, stage):
+            for n, e in enumerate((entry, entry_b)):
+                for u in range(128):
+                    stage[pl.ds(origin + n * 128 + u, 1), :] = grid_ref[pl.ds(place_ref[e * 128 + u], 1), :]
+
+        def pick_four(i, carry):
+            e = [list_ref[4 * i + n] for n in range(6)]
+            gather_two(e[2], e[3], stage_d)
+            write_two(e[0], e[1], stage_c)
+            gather_two(e[4], e[5], stage_c)
+            write_two(e[2], e[3], stage_d)
             return carry
 
         def group(p, carry):
@@ -456,8 +458,8 @@
             return lax.fori_loop(count_ref[p], SLOTS // 128, blank, carry)
 
         lax.fori_loop(0, GROUPS, group, 0)
-        gather(list_ref[0], stage_a)
-        lax.fori_loop(0, list_ref[255], pick, 0)
+        gather_two(list_ref[0], list_ref[1], stage_c)
+        lax.fori_loop(0, (list_ref[263] + 1) // 2, pick_four, 0)
         chip = me_ref[0] // 2
         after, far, before = (chip + 1) % 4, (chip + 2) % 4, (chip + 3) % 4
         routes = [
@@ -470,6 +472,7 @@
             (side_ref.at[0, chip], kept_ref.at[0]),
             (side_ref.at[0, far], kept_ref.at[1]),
         ]
+        routes.append((out_ref, out_hbm))
         copies = [pltpu.make_async_copy(*route, sems.at[1 + n]) for n, route in enumerate(routes)]
         for copy in copies:
             copy.start()
@@ -492,7 +495,7 @@
             whole((GRID, 2 * BOX)),
             whole((BOX, 2 * GRID)),
         ],
-        out_specs=[whole((GROUPS, 64, SLOTS))] + [pl.BlockSpec(memory_space=pl.ANY)] * 6,
+        out_specs=[pl.BlockSpec(memory_space=pl.ANY)] * 7,
         out_shape=[jax.ShapeDtypeStruct((GROUPS, 64, SLOTS), jnp.bfloat16)]
         + [jax.ShapeDtypeStruct((2, 2, 64, SLOTS), jnp.bfloat16)] * 2
         + [jax.ShapeDtypeStruct((2, 64, SLOTS), jnp.bfloat16)] * 4,
@@ -502,10 +505,13 @@
             pltpu.VMEM((BOX * PITCHB, 128), jnp.float32),
             pltpu.VMEM((2, 4, 2, 64, SLOTS), jnp.bfloat16),
             pltpu.VMEM((GROUPS, 64, SLOTS), jnp.bfloat16),
+            pltpu.VMEM((GROUPS, 64, SLOTS), jnp.bfloat16),
             pltpu.VMEM((128, 128), jnp.float32),
             pltpu.VMEM((128, 128), jnp.float32),
-            pltpu.SMEM((256,), jnp.int32),
-            pltpu.SemaphoreType.DMA((9,)),
+            pltpu.VMEM((256, 128), jnp.float32),
+            pltpu.VMEM((256, 128), jnp.float32),
+            pltpu.SMEM((264,), jnp.int32),
+            pltpu.SemaphoreType.DMA((10,)),
         ],
         compiler_params=pltpu.CompilerParams(vmem_limit_bytes=62 * MIB),
         cost_estimate=pl.CostEstimate(flops=13_000_000_000, bytes_accessed=24_000_000, transcendentals=0),

time: 257 us -> 252 us (0.981); the launches traced: 252 us -> 252 us
  waiting for transfers between devices: 56.4 us -> 63.6 us
  Pallas kernels: 132 us -> 125 us
    pallas_call x1, Pallas kernels: 90.9 us -> 84.3 us  [plane_call(): pl.pallas_call(plane_kernel, grid=(PAIRS // PB,), in_specs=[pl.BlockSpec(...]
    all_to_all x1, waiting for transfers between devices: 0.01 us -> 4.71 us  [local(): lax.all_to_all(twofold_call(incoming), 'band', split_axis=0, concat_axis=...]
    ppermute x7, waiting for transfers between devices: 12.9 us -> 16.6 us  [summed(): received = lax.ppermute(values, axis, [(i, i ^ step) for i in range(size)])]
  transfers between devices with their start and end apart: 19 -> 19, of which waited for: 11 -> 12; matrix products, arithmetic and copies ran while one was open for 2% -> 2% of each run, Pallas kernels for 48% -> 45%
where the time goes in v6:
time: 252 us
  Pallas kernels  125 us (50%)
  waiting for transfers between devices  63.6 us (25%)
  starting transfers between devices  51.5 us (20%)
  local copies, waits for them, and re-layouts  5.51 us (2%)
  other arithmetic  5.11 us (2%)
    pallas_call x1, Pallas kernels, plane_call(): pl.pallas_call(plane_kernel, grid=(PAIRS // PB,), in_specs=[pl.BlockSpec(...  84.3 us
    ppermute x9, waiting for transfers between devices, moved(): lax.ppermute(values, 'band', [(i, (i // 2 + shift) % 4 * 2 + (i % 2 + oth...  41 us
    pallas_call x3, Pallas kernels, gram_call(): pl.pallas_call(kernel, grid=(2,), in_specs=[pl.BlockSpec(memory_space=plt...  16.7 us
    ppermute x7, waiting for transfers between devices, summed(): received = lax.ppermute(values, axis, [(i, i ^ step) for i in range(size)])  16.6 us
    ppermute x7, starting transfers between devices, summed(): received = lax.ppermute(values, axis, [(i, i ^ step) for i in range(size)])  15.3 us
    all_to_all x1, starting transfers between devices, local(): lax.all_to_all(outgoing, 'fft', split_axis=0, concat_axis=0, tiled=True)  12.5 us
    ppermute x9, starting transfers between devices, moved(): lax.ppermute(values, 'band', [(i, (i // 2 + shift) % 4 * 2 + (i % 2 + oth...  10.5 us
    all_to_all x1, starting transfers between devices, local(): lax.all_to_all(wire.reshape(GROUPS, 64, SLOTS), 'fft', split_axis=0, conc...  8.32 us
  transfers between devices with their start and end apart: 19, of which 12 were waited for; matrix products, arithmetic and copies ran while one was open for 2% of the time, Pallas kernels for 45%

profile of v6, /device:TPU:0, one launch (start us, length us, event | category | flops | bytes accessed | tf_op | source)
XLA Modules:
  0.0 251.7 jit_solution(11233619128625329140)
XLA Ops:
  0.6 0.8 fusion.3
  1.4 0.6 reshape.67.live_ref
  2.0 7.0 %z_forward.1 = (bf16[16,2,2,16,1920]{4,3,2,1,0:T(8,128)(2,1)}, bf16[4,2,2,2,16,1920]{5,4,3,2,1,0:T(8,128)(2,1)}, bf16[4,2,2,2,16,1920]{5,4,3,2,1,0:T(8,128)(2,1)}) custom-call(s32[1]{0:T(128)S(6)} %select_n.74.core_ref, bf16[2,480,1920]{2,1,0:T(8,128)(2,1)} %bitcast.25, f32[1,1920]{1,0:T(1,128)} %reshape.67.live_ref, bf16[512,480]{1,0:T(8,128)(2,1)} %constant.128.clone.table_ref), custom_call_target="tpu_custom_call" | custom-call | flops 1800000000 | bytes 12000000 | tf_op jit(solution)/shard_map/z_forward/pallas_call | solution.py:82
  9.0 0.0 collective-permute-start
  9.0 8.3 %all-to-all-start = ((bf16[16,64,1920]{2,1,0:T(8,128)(2,1)}), bf16[16,64,1920]{2,1,0:T(8,128)(2,1)}, u32[]{:S(2)}, u32[]{:S(2)}) async-start(bf16[16,64,1920]{2,1,0:T(8,128)(2,1)} %bitcast.20), calls=%async_computation | async-start | bytes 7864320 | tf_op jit(solution)/shard_map/all_to_all | solution.py:562
  17.4 0.7 convert_bitcast_fusion
  18.2 0.1 reduce_sum.9
  18.3 1.6 constant_dynamic-slice_fusion.1
  19.9 0.0 collective-permute-done
  20.0 0.2 constant_dynamic-slice_fusion
  20.1 0.2 pad_maximum_fusion.2
  20.3 1.2 pad_maximum_fusion
  21.5 1.5 collective-permute-start.1
  23.0 2.7 %collective-permute-start.2 = (bf16[2,2,2,2,16,1920]{5,4,3,2,1,0:T(8,128)(2,1)S(1)}, bf16[2,2,2,2,16,1920]{5,4,3,2,1,0:T(8,128)(2,1)}, u32[]{:S(2)}, u32[]{:S(2)}) collective-permute-start(bf16[2,2,2,2,16,1920]{5,4,3,2,1,0:T(8,128)(2,1)S(1)} %get-tuple-element.35), channel_id=1, source_target_pairs={{0,64},{16,80},{32,96},{48,112},{64,0},{80,16},{96,32},{112,48},{1... | collective-permute-start | bytes 2949128 | tf_op jit(solution)/shard_map/ppermute | solution.py:266
  25.7 1.4 collective-permute-start.3
  27.2 0.5 and_select_fusion.count_ref
  27.7 0.8 add_select_fusion.2.place_ref
  28.5 7.0 %field.1.field_ref = bf16[120,240,128]{2,1,0:T(8,128)(2,1)} custom-call(f32[15,57600]{1,0:T(8,128)} %upper_ref, f32[15,57600]{1,0:T(8,128)} %upper_ref), custom_call_target="tpu_custom_call" | custom-call | bytes 18000000 | tf_op jit(solution)/shard_map/field/pallas_call | solution.py:532
  35.5 11.1 %collective-permute-done.1.refs_1_ = bf16[2,2,2,2,16,1920]{5,4,3,2,1,0:T(8,128)(2,1)S(1)} collective-permute-done((bf16[2,2,2,2,16,1920]{5,4,3,2,1,0:T(8,128)(2,1)S(1)}, bf16[2,2,2,2,16,1920]{5,4,3,2,1,0:T(8,128)(2,1)S(1)}, u32[]{:S(2)}, u32[]{:S(2)}) %collective-permute-start.1) | collective-permute-done | bytes 983072 | tf_op jit(solution)/shard_map/ppermute | solution.py:266
  46.6 22.2 %collective-permute-done.2.refs_2_ = bf16[2,2,2,2,16,1920]{5,4,3,2,1,0:T(8,128)(2,1)} collective-permute-done((bf16[2,2,2,2,16,1920]{5,4,3,2,1,0:T(8,128)(2,1)S(1)}, bf16[2,2,2,2,16,1920]{5,4,3,2,1,0:T(8,128)(2,1)}, u32[]{:S(2)}, u32[]{:S(2)}) %collective-permute-start.2) | collective-permute-done | bytes 983072 | tf_op jit(solution)/shard_map/ppermute | solution.py:266
  68.8 0.0 collective-permute-done.3.refs_3_
  68.8 1.3 all-to-all-done.wire_hbm
  70.0 4.9 %twofold.1 = bf16[2,4,2,128,1920]{4,3,2,1,0:T(8,128)(2,1)} custom-call(bf16[2,4,128,1920]{3,2,1,0:T(8,128)(2,1)} %bitcast.4.in_ref), custom_call_target="tpu_custom_call" | custom-call | bytes 12000000 | tf_op jit(solution)/shard_map/twofold/pallas_call | solution.py:242
  74.9 4.9 %all-to-all-start.1 = ((bf16[8,256,1920]{2,1,0:T(8,128)(2,1)}), bf16[8,256,1920]{2,1,0:T(8,128)(2,1)}, u32[]{:S(2)}, u32[]{:S(2)}) async-start(bf16[8,256,1920]{2,1,0:T(8,128)(2,1)} %bitcast.19), calls=%async_computation.1 | async-start | bytes 15728640 | tf_op jit(solution)/shard_map/all_to_all | solution.py:568
  79.8 84.3 %planes.1 = (bf16[16,64,1920]{2,1,0:T(8,128)(2,1)}, bf16[2,2,64,1920]{3,2,1,0:T(8,128)(2,1)}, bf16[2,2,64,1920]{3,2,1,0:T(8,128)(2,1)}, bf16[2,64,1920]{2,1,0:T(...) custom-call(s32[1]{0:T(128)} %bitcast.me_ref, ...), custom_call_target="tpu_custom_call" | custom-call | flops 12999999488 | bytes 24000000 | tf_op jit(solution)/shard_map/planes/pallas_call | solution.py:485
  164.1 4.7 %all-to-all-done.1 = bf16[8,256,1920]{2,1,0:T(8,128)(2,1)} async-done(((bf16[8,256,1920]{2,1,0:T(8,128)(2,1)}), bf16[8,256,1920]{2,1,0:T(8,128)(2,1)}, u32[]{:S(2)}, u32[]{:S(2)}) %all-to-all-start.1) | async-done | bytes 7864352 | tf_op jit(solution)/shard_map/all_to_all | solution.py:568
  168.8 12.5 %all-to-all-start.2 = ((bf16[16,64,1920]{2,1,0:T(8,128)(2,1)}), bf16[16,64,1920]{2,1,0:T(8,128)(2,1)}, u32[]{:S(2)}, u32[]{:S(2)}) async-start(bf16[16,64,1920]{2,1,0:T(8,128)(2,1)} %get-tuple-element.52), calls=%async_computation.2 | async-start | bytes 7864320 | tf_op jit(solution)/shard_map/all_to_all | solution.py:575
  181.3 0.1 collective-permute-start.4
  181.4 0.6 collective-permute-start.5
  182.0 0.1 collective-permute-start.6
  182.1 2.9 %collective-permute-start.7 = (bf16[1,2,2,2,16,1920]{5,4,3,2,1,0:T(8,128)(2,1)}, bf16[1,2,2,2,16,1920]{5,4,3,2,1,0:T(8,128)(2,1)S(1)}, u32[]{:S(2)}, u32[]{:S(2)}) collective-permute-start(bf16[1,2,2,2,16,1920]{5,4,3,2,1,0:T(8,128)(2,1)} %bitcast.11), channel_id=1, source_target_pairs={{0,96},{16,112},{32,0},{48,16},{64,32},{80,48},{96,64},{112,80},{1... | collective-permute-start | bytes 1474568 | tf_op jit(solution)/shard_map/ppermute | solution.py:266
  185.1 1.1 collective-permute-start.8
  186.2 5.8 %overlap.1 = f32[16,128]{1,0:T(8,128)} custom-call(s32[1]{0:T(128)} %bitcast.me_ref, bf16[2,2,2,2,16,1920]{5,4,3,2,1,0:T(8,128)(2,1)} %get-tuple-element.37.refs_0_, bf16[2,2,2,2,16,1920]{5,4,3,2,1,0:T(8,128)(2,1)} %copy-done.8, bf16[2,2,2,2,16,1920]{5,4,3,2,1,0:T(8,128)(2,1)} %collective-permute-done.2.refs_2_, ...), custom_call_target="tpu_custom_call" | custom-call | flops 2000000000 | bytes 8000000 | tf_op jit(solution)/shard_map/overlap/pallas_call | solution.py:221
  192.0 0.0 collective-permute-done.4.got_near.got_far
  192.0 1.0 copy-done
  193.0 6.2 %near.1 = f32[16,128]{1,0:T(8,128)} custom-call(s32[1]{0:T(128)} %bitcast.me_ref, bf16[8,4,2,2,16,1920]{5,4,3,2,1,0:T(8,128)(2,1)} %bitcast.6.left_ref.left_far_ref, bf16[8,4,2,2,16,1920]{5,4,3,2,1,0:T(8,128)(2,1)} %bitcast.6.left_ref.left_far_ref, bf16[2,2,2,2,16,1920]{5,4,3,2,1,0:T(8,128)(2,1)} %bitcast.21, bf16[2,2,2,2,16,1920]{5,4,3,2,1,0:T(8,128)(2,1)} %copy-done, ...), custom_call_target="tpu_custom_call" | custom-call | flops 2000000000 | bytes 8000000 | tf_op jit(solution)/shard_map/near/pallas_call | solution.py:221
  199.1 0.0 collective-permute-done.5.before_same
  199.1 0.0 copy-start.2
  199.2 7.4 %collective-permute-done.6.before_other = bf16[1,2,2,2,16,1920]{5,4,3,2,1,0:T(8,128)(2,1)S(1)} collective-permute-done((bf16[1,2,2,2,16,1920]{5,4,3,2,1,0:T(8,128)(2,1)}, bf16[1,2,2,2,16,1920]{5,4,3,2,1,0:T(8,128)(2,1)S(1)}, u32[]{:S(2)}, u32[]{:S(2)}) %collective-permute-start.6) | collective-permute-done | bytes 491552 | tf_op jit(solution)/shard_map/ppermute | solution.py:266
  206.5 0.0 collective-permute-done.7.after_same
  206.5 0.4 collective-permute-done.8.after_other
  206.9 0.4 copy-done.3
  207.3 0.2 copy-done.4
  207.5 0.8 copy-done.5
  208.3 4.8 %next.1 = f32[16,128]{1,0:T(8,128)} custom-call(s32[1]{0:T(128)} %bitcast.me_ref, bf16[8,4,2,2,16,1920]{5,4,3,2,1,0:T(8,128)(2,1)} %bitcast.6.left_ref.left_far_ref, bf16[1,2,2,2,16,1920]{5,4,3,2,1,0:T(8,128)(2,1)} %copy-done.2, bf16[1,2,2,2,16,1920]{5,4,3,2,1,0:T(8,128)(2,1)} %copy-done.3, bf16[1,2,2,2,16,1920]{5,4,3,2,1,0:T(8,128)(2,1)} %copy-done.4, ...), custom_call_target="tpu_custom_call" | custom-call | flops 2000000000 | bytes 8000000 | tf_op jit(solution)/shard_map/next/pallas_call | solution.py:221
  213.1 0.7 add_add_fusion
  213.8 0.7 collective-permute-start.9
  214.5 0.8 collective-permute-done.9
  215.3 0.4 collective-permute-start.10
  215.7 3.2 %collective-permute-done.10 = f32[16,128]{1,0:T(8,128)S(1)} collective-permute-done((f32[16,128]{1,0:T(8,128)S(1)}, f32[16,128]{1,0:T(8,128)S(1)}, u32[]{:S(2)}, u32[]{:S(2)}) %collective-permute-start.10) | collective-permute-done | bytes 8224 | tf_op jit(solution)/shard_map/ppermute | solution.py:258
  219.0 2.2 collective-permute-start.11
  221.2 2.9 %collective-permute-done.11 = f32[16,128]{1,0:T(8,128)S(1)} collective-permute-done((f32[16,128]{1,0:T(8,128)S(1)}, f32[16,128]{1,0:T(8,128)S(1)}, u32[]{:S(2)}, u32[]{:S(2)}) %collective-permute-start.11) | collective-permute-done | bytes 8224 | tf_op jit(solution)/shard_map/ppermute | solution.py:258
  224.1 1.9 collective-permute-start.12
  226.0 2.8 %collective-permute-done.12 = f32[16,128]{1,0:T(8,128)S(1)} collective-permute-done((f32[16,128]{1,0:T(8,128)S(1)}, f32[16,128]{1,0:T(8,128)S(1)}, u32[]{:S(2)}, u32[]{:S(2)}) %collective-permute-start.12) | collective-permute-done | bytes 8224 | tf_op jit(solution)/shard_map/ppermute | solution.py:258
  228.8 6.9 %collective-permute-start.13 = (f32[16,128]{1,0:T(8,128)S(1)}, f32[16,128]{1,0:T(8,128)S(1)}, u32[]{:S(2)}, u32[]{:S(2)}) collective-permute-start(f32[16,128]{1,0:T(8,128)S(1)} %add.120), channel_id=1, source_target_pairs={{0,2},{1,3},{2,0},{3,1},{4,6},{5,7},{6,4},{7,5},{8,10},{9,11},{10,... | collective-permute-start | bytes 24584 | tf_op jit(solution)/shard_map/ppermute | solution.py:258
  235.8 1.6 collective-permute-done.13
  237.4 3.1 %collective-permute-start.14 = (f32[16,128]{1,0:T(8,128)S(1)}, f32[16,128]{1,0:T(8,128)S(1)}, u32[]{:S(2)}, u32[]{:S(2)}) collective-permute-start(f32[16,128]{1,0:T(8,128)S(1)} %add.121), channel_id=1, source_target_pairs={{0,4},{1,5},{2,6},{3,7},{4,0},{5,1},{6,2},{7,3},{8,12},{9,13},{10,... | collective-permute-start | bytes 24584 | tf_op jit(solution)/shard_map/ppermute | solution.py:258
  240.5 0.0 all-to-all-done.2
  240.5 5.3 %z_backward.1 = bf16[2,480,1920]{2,1,0:T(8,128)(2,1)} custom-call(bf16[16,2,2,16,1920]{4,3,2,1,0:T(8,128)(2,1)} %bitcast.13.wire_ref, f32[1,1920]{1,0:T(1,128)} %reshape.67.live_ref, bf16[480,512]{1,0:T(8,128)(2,1)} %constant.129.clone.table_ref), custom_call_target="tpu_custom_call" | custom-call | flops 1800000000 | bytes 8000000 | tf_op jit(solution)/shard_map/z_backward/pallas_call | solution.py:108
  245.7 0.0 collective-permute-done.14
  245.7 0.1 collective-permute-start.15
  245.8 5.1 %collective-permute-done.15 = f32[16,128]{1,0:T(8,128)S(1)} collective-permute-done((f32[16,128]{1,0:T(8,128)S(1)}, f32[16,128]{1,0:T(8,128)S(1)}, u32[]{:S(2)}, u32[]{:S(2)}) %collective-permute-start.15) | collective-permute-done | bytes 8224 | tf_op jit(solution)/shard_map/ppermute | solution.py:258
  251.0 0.1 reshape.66
  251.1 0.6 fusion.4
  (24 shorter events, 0.1 us)
Async XLA Ops:
  9.0 11.0 %collective-permute-start = (bf16[4,2,2,2,16,1920]{5,4,3,2,1,0:T(8,128)(2,1)}, bf16[4,2,2,2,16,1920]{5,4,3,2,1,0:T(8,128)(2,1)S(1)}, u32[]{:S(2)}, u32[]{:S(2)}) collective-permute-start(bf16[4,2,2,2,16,1920]{5,4,3,2,1,0:T(8,128)(2,1)} %get-tuple-element.31), channel_id=1, source_target_pairs={{0,16},{16,0},{32,48},{48,32},{64,80},{80,64},{96,112},{112,96},{1... | collective-permute-start | bytes 5898248 | tf_op jit(solution)/shard_map/ppermute | solution.py:266
  9.0 8.4 %copy-start.1 = (s32[30720]{0:T(1024)S(1)}, s32[30720]{0:T(1024)}, u32[]{:S(2)}) copy-start(s32[30720]{0:T(1024)} %param.10) | copy-start | bytes 368644
  9.0 61.0 %all-to-all-start = ((bf16[16,64,1920]{2,1,0:T(8,128)(2,1)}), bf16[16,64,1920]{2,1,0:T(8,128)(2,1)}, u32[]{:S(2)}, u32[]{:S(2)}) async-start(bf16[16,64,1920]{2,1,0:T(8,128)(2,1)} %bitcast.20), calls=%async_computation | async-start | bytes 7864320 | tf_op jit(solution)/shard_map/all_to_all | solution.py:562
  21.5 25.1 %collective-permute-start.1 = (bf16[2,2,2,2,16,1920]{5,4,3,2,1,0:T(8,128)(2,1)S(1)}, bf16[2,2,2,2,16,1920]{5,4,3,2,1,0:T(8,128)(2,1)S(1)}, u32[]{:S(2)}, u32[]{:S(2)}) collective-permute-start(bf16[2,2,2,2,16,1920]{5,4,3,2,1,0:T(8,128)(2,1)S(1)} %get-tuple-element.34), channel_id=1, source_target_pairs={{0,32},{16,48},{32,64},{48,80},{64,96},{80,112},{96,0},{112,16},{1... | collective-permute-start | bytes 2949128 | tf_op jit(solution)/shard_map/ppermute | solution.py:266
  23.0 45.7 %collective-permute-start.2 = (bf16[2,2,2,2,16,1920]{5,4,3,2,1,0:T(8,128)(2,1)S(1)}, bf16[2,2,2,2,16,1920]{5,4,3,2,1,0:T(8,128)(2,1)}, u32[]{:S(2)}, u32[]{:S(2)}) collective-permute-start(bf16[2,2,2,2,16,1920]{5,4,3,2,1,0:T(8,128)(2,1)S(1)} %get-tuple-element.35), channel_id=1, source_target_pairs={{0,64},{16,80},{32,96},{48,112},{64,0},{80,16},{96,32},{112,48},{1... | collective-permute-start | bytes 2949128 | tf_op jit(solution)/shard_map/ppermute | solution.py:266
  25.7 43.0 %collective-permute-start.3 = (bf16[2,2,2,2,16,1920]{5,4,3,2,1,0:T(8,128)(2,1)S(1)}, bf16[2,2,2,2,16,1920]{5,4,3,2,1,0:T(8,128)(2,1)}, u32[]{:S(2)}, u32[]{:S(2)}) collective-permute-start(bf16[2,2,2,2,16,1920]{5,4,3,2,1,0:T(8,128)(2,1)S(1)} %get-tuple-element.36), channel_id=1, source_target_pairs={{0,96},{16,112},{32,0},{48,16},{64,32},{80,48},{96,64},{112,80},{1... | collective-permute-start | bytes 2949128 | tf_op jit(solution)/shard_map/ppermute | solution.py:266
  46.6 28.3 %copy-start.8 = (bf16[2,2,2,2,16,1920]{5,4,3,2,1,0:T(8,128)(2,1)}, bf16[2,2,2,2,16,1920]{5,4,3,2,1,0:T(8,128)(2,1)S(1)}, u32[]{:S(2)}) copy-start(bf16[2,2,2,2,16,1920]{5,4,3,2,1,0:T(8,128)(2,1)S(1)} %collective-permute-done.1.refs_1_) | copy-start | bytes 2949124
  74.9 93.9 %all-to-all-start.1 = ((bf16[8,256,1920]{2,1,0:T(8,128)(2,1)}), bf16[8,256,1920]{2,1,0:T(8,128)(2,1)}, u32[]{:S(2)}, u32[]{:S(2)}) async-start(bf16[8,256,1920]{2,1,0:T(8,128)(2,1)} %bitcast.19), calls=%async_computation.1 | async-start | bytes 15728640 | tf_op jit(solution)/shard_map/all_to_all | solution.py:568
  168.8 12.5 %copy-start.9 = (bf16[2,2,64,1920]{3,2,1,0:T(8,128)(2,1)S(1)}, bf16[2,2,64,1920]{3,2,1,0:T(8,128)(2,1)}, u32[]{:S(2)}) copy-start(bf16[2,2,64,1920]{3,2,1,0:T(8,128)(2,1)} %get-tuple-element.47) | copy-start | bytes 2949124
  168.8 71.7 %all-to-all-start.2 = ((bf16[16,64,1920]{2,1,0:T(8,128)(2,1)}), bf16[16,64,1920]{2,1,0:T(8,128)(2,1)}, u32[]{:S(2)}, u32[]{:S(2)}) async-start(bf16[16,64,1920]{2,1,0:T(8,128)(2,1)} %get-tuple-element.52), calls=%async_computation.2 | async-start | bytes 7864320 | tf_op jit(solution)/shard_map/all_to_all | solution.py:575
  181.3 10.7 %collective-permute-start.4 = (bf16[2,2,2,2,16,1920]{5,4,3,2,1,0:T(8,128)(2,1)S(1)}, bf16[2,2,2,2,16,1920]{5,4,3,2,1,0:T(8,128)(2,1)S(1)}, u32[]{:S(2)}, u32[]{:S(2)}) collective-permute-start(bf16[2,2,2,2,16,1920]{5,4,3,2,1,0:T(8,128)(2,1)S(1)} %bitcast.26), channel_id=1, source_target_pairs={{0,16},{16,0},{32,48},{48,32},{64,80},{80,64},{96,112},{112,96},{1... | collective-permute-start | bytes 2949128 | tf_op jit(solution)/shard_map/ppermute | solution.py:266
  181.4 17.7 %collective-permute-start.5 = (bf16[1,2,2,2,16,1920]{5,4,3,2,1,0:T(8,128)(2,1)}, bf16[1,2,2,2,16,1920]{5,4,3,2,1,0:T(8,128)(2,1)S(1)}, u32[]{:S(2)}, u32[]{:S(2)}) collective-permute-start(bf16[1,2,2,2,16,1920]{5,4,3,2,1,0:T(8,128)(2,1)} %bitcast.9), channel_id=1, source_target_pairs={{0,32},{16,48},{32,64},{48,80},{64,96},{80,112},{96,0},{112,16},{1... | collective-permute-start | bytes 1474568 | tf_op jit(solution)/shard_map/ppermute | solution.py:266
  182.0 24.5 %collective-permute-start.6 = (bf16[1,2,2,2,16,1920]{5,4,3,2,1,0:T(8,128)(2,1)}, bf16[1,2,2,2,16,1920]{5,4,3,2,1,0:T(8,128)(2,1)S(1)}, u32[]{:S(2)}, u32[]{:S(2)}) collective-permute-start(bf16[1,2,2,2,16,1920]{5,4,3,2,1,0:T(8,128)(2,1)} %bitcast.10), channel_id=1, source_target_pairs={{0,48},{16,32},{32,80},{48,64},{64,112},{80,96},{96,16},{112,0},{1... | collective-permute-start | bytes 1474568 | tf_op jit(solution)/shard_map/ppermute | solution.py:266
  182.1 24.4 %collective-permute-start.7 = (bf16[1,2,2,2,16,1920]{5,4,3,2,1,0:T(8,128)(2,1)}, bf16[1,2,2,2,16,1920]{5,4,3,2,1,0:T(8,128)(2,1)S(1)}, u32[]{:S(2)}, u32[]{:S(2)}) collective-permute-start(bf16[1,2,2,2,16,1920]{5,4,3,2,1,0:T(8,128)(2,1)} %bitcast.11), channel_id=1, source_target_pairs={{0,96},{16,112},{32,0},{48,16},{64,32},{80,48},{96,64},{112,80},{1... | collective-permute-start | bytes 1474568 | tf_op jit(solution)/shard_map/ppermute | solution.py:266
  185.1 21.8 %collective-permute-start.8 = (bf16[1,2,2,2,16,1920]{5,4,3,2,1,0:T(8,128)(2,1)}, bf16[1,2,2,2,16,1920]{5,4,3,2,1,0:T(8,128)(2,1)S(1)}, u32[]{:S(2)}, u32[]{:S(2)}) collective-permute-start(bf16[1,2,2,2,16,1920]{5,4,3,2,1,0:T(8,128)(2,1)} %bitcast.27), channel_id=1, source_target_pairs={{0,112},{16,96},{32,16},{48,0},{64,48},{80,32},{96,80},{112,64},{1... | collective-permute-start | bytes 1474568 | tf_op jit(solution)/shard_map/ppermute | solution.py:266
  192.0 1.0 copy-start
  199.1 13.9 %copy-start.6 = (f32[16,128]{1,0:T(8,128)S(1)}, f32[16,128]{1,0:T(8,128)}, u32[]{:S(2)}) copy-start(f32[16,128]{1,0:T(8,128)} %near.1) | copy-start | bytes 24580
  199.1 13.9 %copy-start.7 = (f32[16,128]{1,0:T(8,128)S(1)}, f32[16,128]{1,0:T(8,128)}, u32[]{:S(2)}) copy-start(f32[16,128]{1,0:T(8,128)} %overlap.1) | copy-start | bytes 24580
  199.1 7.7 %copy-start.2 = (bf16[1,2,2,2,16,1920]{5,4,3,2,1,0:T(8,128)(2,1)}, bf16[1,2,2,2,16,1920]{5,4,3,2,1,0:T(8,128)(2,1)S(1)}, u32[]{:S(2)}) copy-start(bf16[1,2,2,2,16,1920]{5,4,3,2,1,0:T(8,128)(2,1)S(1)} %collective-permute-done.5.before_same) | copy-start | bytes 1474564
  206.5 0.8 copy-start.3
  206.5 0.9 copy-start.4
  207.5 0.8 copy-start.5
  213.8 1.5 collective-permute-start.9
  215.3 3.7 %collective-permute-start.10 = (f32[16,128]{1,0:T(8,128)S(1)}, f32[16,128]{1,0:T(8,128)S(1)}, u32[]{:S(2)}, u32[]{:S(2)}) collective-permute-start(f32[16,128]{1,0:T(8,128)S(1)} %add.117), channel_id=1, source_target_pairs={{0,32},{16,48},{32,0},{48,16},{64,96},{80,112},{96,64},{112,80},{1... | collective-permute-start | bytes 24584 | tf_op jit(solution)/shard_map/ppermute | solution.py:258
  219.0 5.2 %collective-permute-start.11 = (f32[16,128]{1,0:T(8,128)S(1)}, f32[16,128]{1,0:T(8,128)S(1)}, u32[]{:S(2)}, u32[]{:S(2)}) collective-permute-start(f32[16,128]{1,0:T(8,128)S(1)} %add.118), channel_id=1, source_target_pairs={{0,64},{16,80},{32,96},{48,112},{64,0},{80,16},{96,32},{112,48},{1... | collective-permute-start | bytes 24584 | tf_op jit(solution)/shard_map/ppermute | solution.py:258
  224.1 4.7 %collective-permute-start.12 = (f32[16,128]{1,0:T(8,128)S(1)}, f32[16,128]{1,0:T(8,128)S(1)}, u32[]{:S(2)}, u32[]{:S(2)}) collective-permute-start(f32[16,128]{1,0:T(8,128)S(1)} %add.119), channel_id=1, source_target_pairs={{0,1},{1,0},{2,3},{3,2},{4,5},{5,4},{6,7},{7,6},{8,9},{9,8},{10,11... | collective-permute-start | bytes 24584 | tf_op jit(solution)/shard_map/ppermute | solution.py:258
  228.8 8.6 %collective-permute-start.13 = (f32[16,128]{1,0:T(8,128)S(1)}, f32[16,128]{1,0:T(8,128)S(1)}, u32[]{:S(2)}, u32[]{:S(2)}) collective-permute-start(f32[16,128]{1,0:T(8,128)S(1)} %add.120), channel_id=1, source_target_pairs={{0,2},{1,3},{2,0},{3,1},{4,6},{5,7},{6,4},{7,5},{8,10},{9,11},{10,... | collective-permute-start | bytes 24584 | tf_op jit(solution)/shard_map/ppermute | solution.py:258
  237.4 8.4 %collective-permute-start.14 = (f32[16,128]{1,0:T(8,128)S(1)}, f32[16,128]{1,0:T(8,128)S(1)}, u32[]{:S(2)}, u32[]{:S(2)}) collective-permute-start(f32[16,128]{1,0:T(8,128)S(1)} %add.121), channel_id=1, source_target_pairs={{0,4},{1,5},{2,6},{3,7},{4,0},{5,1},{6,2},{7,3},{8,12},{9,13},{10,... | collective-permute-start | bytes 24584 | tf_op jit(solution)/shard_map/ppermute | solution.py:258
  245.7 5.2 %collective-permute-start.15 = (f32[16,128]{1,0:T(8,128)S(1)}, f32[16,128]{1,0:T(8,128)S(1)}, u32[]{:S(2)}, u32[]{:S(2)}) collective-permute-start(f32[16,128]{1,0:T(8,128)S(1)} %add.122), channel_id=1, source_target_pairs={{0,8},{1,9},{2,10},{3,11},{4,12},{5,13},{6,14},{7,15},{8,0},{9,1},... | collective-permute-start | bytes 24584 | tf_op jit(solution)/shard_map/ppermute | solution.py:258

commit v7 on v6

--- a/solution.py
+++ b/solution.py
@@ -231,24 +231,36 @@
     )(me, *[operand[0] for operand in operands])
 
 
-def twofold_kernel(in_ref, out_ref):
-    for half in range(2):
-        out_ref[half, :, 0] = in_ref[half]
-        out_ref[half, :, 1] = in_ref[1 - half]
+def twofold_kernel(in_ref, out_ref, held, in_sems, out_sems):
+    loads = [pltpu.make_async_copy(in_ref.at[d], held.at[d], in_sems.at[d]) for d in range(8)]
+    for load in loads:
+        load.start()
+    stores = []
+    for d in range(8):
+        loads[d].wait()
+        for half, target in enumerate((d, (d + 4) % 8)):
+            store = pltpu.make_async_copy(held.at[d], out_ref.at[target, half], out_sems.at[2 * d + half])
+            store.start()
+            stores.append(store)
+    for store in stores:
+        store.wait()
 
 
 def twofold_call(blocks):
-    count = 2
     result = pl.pallas_call(
         twofold_kernel,
-        grid=(4 // count,),
-        in_specs=[pl.BlockSpec((2, count, 128, SLOTS), lambda i: (0, i, 0, 0))],
-        out_specs=pl.BlockSpec((2, count, 2, 128, SLOTS), lambda i: (0, i, 0, 0, 0)),
-        out_shape=jax.ShapeDtypeStruct((2, 4, 2, 128, SLOTS), jnp.bfloat16),
+        in_specs=[pl.BlockSpec(memory_space=pl.ANY)],
+        out_specs=pl.BlockSpec(memory_space=pl.ANY),
+        out_shape=jax.ShapeDtypeStruct((8, 2, 128, SLOTS), jnp.bfloat16),
+        scratch_shapes=[
+            pltpu.VMEM((8, 128, SLOTS), jnp.bfloat16),
+            pltpu.SemaphoreType.DMA((8,)),
+            pltpu.SemaphoreType.DMA((16,)),
+        ],
         compiler_params=pltpu.CompilerParams(vmem_limit_bytes=60 * MIB),
         cost_estimate=pl.CostEstimate(flops=0, bytes_accessed=12_000_000, transcendentals=0),
         name="twofold",
-    )(blocks.reshape(2, 4, 128, SLOTS))
+    )(blocks.reshape(8, 128, SLOTS))
     return result.reshape(8, 256, SLOTS)
 
 

time: 252 us -> 252 us (level)
  transfers between devices with their start and end apart: 19 -> 19, of which waited for: 12 -> 12; matrix products, arithmetic and copies ran while one was open for 2% -> 2% of each run, Pallas kernels for 45% -> 46%
where the time goes in v7:
time: 252 us; the launch traced here: 251 us
  Pallas kernels  125 us (50%)
  waiting for transfers between devices  62.5 us (25%)
  starting transfers between devices  51.5 us (20%)
  local copies, waits for them, and re-layouts  5.51 us (2%)
  other arithmetic  5.11 us (2%)
    pallas_call x1, Pallas kernels, plane_call(): pl.pallas_call(plane_kernel, grid=(PAIRS // PB,), in_specs=[pl.BlockSpec(...  85.3 us
    ppermute x9, waiting for transfers between devices, moved(): lax.ppermute(values, 'band', [(i, (i // 2 + shift) % 4 * 2 + (i % 2 + oth...  41 us
    pallas_call x3, Pallas kernels, gram_call(): pl.pallas_call(kernel, grid=(2,), in_specs=[pl.BlockSpec(memory_space=plt...  16.7 us
    ppermute x7, waiting for transfers between devices, summed(): received = lax.ppermute(values, axis, [(i, i ^ step) for i in range(size)])  16.6 us
    ppermute x7, starting transfers between devices, summed(): received = lax.ppermute(values, axis, [(i, i ^ step) for i in range(size)])  15.3 us
    all_to_all x1, starting transfers between devices, local(): lax.all_to_all(outgoing, 'fft', split_axis=0, concat_axis=0, tiled=True)  12.5 us
    ppermute x9, starting transfers between devices, moved(): lax.ppermute(values, 'band', [(i, (i // 2 + shift) % 4 * 2 + (i % 2 + oth...  10.5 us
    all_to_all x1, starting transfers between devices, local(): lax.all_to_all(wire.reshape(GROUPS, 64, SLOTS), 'fft', split_axis=0, conc...  8.32 us
  transfers between devices with their start and end apart: 19, of which 12 were waited for; matrix products, arithmetic and copies ran while one was open for 2% of the time, Pallas kernels for 46%

profile of v7, /device:TPU:0, one launch (start us, length us, event | category | flops | bytes accessed | tf_op | source)
XLA Modules:
  0.0 251.1 jit_solution(16457394865430571661)
XLA Ops:
  0.6 0.8 fusion.3
  1.4 0.6 reshape.67.live_ref
  2.0 7.0 %z_forward.1 = (bf16[16,2,2,16,1920]{4,3,2,1,0:T(8,128)(2,1)}, bf16[4,2,2,2,16,1920]{5,4,3,2,1,0:T(8,128)(2,1)}, bf16[4,2,2,2,16,1920]{5,4,3,2,1,0:T(8,128)(2,1)}) custom-call(s32[1]{0:T(128)S(6)} %select_n.74.core_ref, bf16[2,480,1920]{2,1,0:T(8,128)(2,1)} %bitcast.25, f32[1,1920]{1,0:T(1,128)} %reshape.67.live_ref, bf16[512,480]{1,0:T(8,128)(2,1)} %constant.128.clone.table_ref), custom_call_target="tpu_custom_call" | custom-call | flops 1800000000 | bytes 12000000 | tf_op jit(solution)/shard_map/z_forward/pallas_call | solution.py:82
  9.0 0.0 collective-permute-start
  9.0 8.3 %all-to-all-start = ((bf16[16,64,1920]{2,1,0:T(8,128)(2,1)}), bf16[16,64,1920]{2,1,0:T(8,128)(2,1)}, u32[]{:S(2)}, u32[]{:S(2)}) async-start(bf16[16,64,1920]{2,1,0:T(8,128)(2,1)} %bitcast.20), calls=%async_computation | async-start | bytes 7864320 | tf_op jit(solution)/shard_map/all_to_all | solution.py:574
  17.4 0.7 convert_bitcast_fusion
  18.2 0.1 reduce_sum.9
  18.3 1.6 constant_dynamic-slice_fusion.1
  19.9 0.0 collective-permute-done
  20.0 0.2 constant_dynamic-slice_fusion
  20.1 0.2 pad_maximum_fusion.2
  20.3 1.2 pad_maximum_fusion
  21.5 1.5 collective-permute-start.1
  23.0 2.7 %collective-permute-start.2 = (bf16[2,2,2,2,16,1920]{5,4,3,2,1,0:T(8,128)(2,1)S(1)}, bf16[2,2,2,2,16,1920]{5,4,3,2,1,0:T(8,128)(2,1)}, u32[]{:S(2)}, u32[]{:S(2)}) collective-permute-start(bf16[2,2,2,2,16,1920]{5,4,3,2,1,0:T(8,128)(2,1)S(1)} %get-tuple-element.35), channel_id=1, source_target_pairs={{0,64},{16,80},{32,96},{48,112},{64,0},{80,16},{96,32},{112,48},{1... | collective-permute-start | bytes 2949128 | tf_op jit(solution)/shard_map/ppermute | solution.py:278
  25.7 1.4 collective-permute-start.3
  27.2 0.5 and_select_fusion.count_ref
  27.7 0.8 add_select_fusion.2.place_ref
  28.5 7.0 %field.1.field_ref = bf16[120,240,128]{2,1,0:T(8,128)(2,1)} custom-call(f32[15,57600]{1,0:T(8,128)} %upper_ref, f32[15,57600]{1,0:T(8,128)} %upper_ref), custom_call_target="tpu_custom_call" | custom-call | bytes 18000000 | tf_op jit(solution)/shard_map/field/pallas_call | solution.py:544
  35.5 11.1 %collective-permute-done.1.refs_1_ = bf16[2,2,2,2,16,1920]{5,4,3,2,1,0:T(8,128)(2,1)S(1)} collective-permute-done((bf16[2,2,2,2,16,1920]{5,4,3,2,1,0:T(8,128)(2,1)S(1)}, bf16[2,2,2,2,16,1920]{5,4,3,2,1,0:T(8,128)(2,1)S(1)}, u32[]{:S(2)}, u32[]{:S(2)}) %collective-permute-start.1) | collective-permute-done | bytes 983072 | tf_op jit(solution)/shard_map/ppermute | solution.py:278
  46.6 22.2 %collective-permute-done.2.refs_2_ = bf16[2,2,2,2,16,1920]{5,4,3,2,1,0:T(8,128)(2,1)} collective-permute-done((bf16[2,2,2,2,16,1920]{5,4,3,2,1,0:T(8,128)(2,1)S(1)}, bf16[2,2,2,2,16,1920]{5,4,3,2,1,0:T(8,128)(2,1)}, u32[]{:S(2)}, u32[]{:S(2)}) %collective-permute-start.2) | collective-permute-done | bytes 983072 | tf_op jit(solution)/shard_map/ppermute | solution.py:278
  68.8 0.0 collective-permute-done.3.refs_3_
  68.8 1.3 all-to-all-done.wire_hbm
  70.0 4.3 %twofold.1 = bf16[8,2,128,1920]{3,2,1,0:T(8,128)(2,1)} custom-call(bf16[8,128,1920]{2,1,0:T(8,128)(2,1)} %bitcast.4.in_ref), custom_call_target="tpu_custom_call" | custom-call | bytes 12000000 | tf_op jit(solution)/shard_map/twofold/pallas_call | solution.py:250
  74.3 4.9 %all-to-all-start.1 = ((bf16[8,256,1920]{2,1,0:T(8,128)(2,1)}), bf16[8,256,1920]{2,1,0:T(8,128)(2,1)}, u32[]{:S(2)}, u32[]{:S(2)}) async-start(bf16[8,256,1920]{2,1,0:T(8,128)(2,1)} %bitcast.19), calls=%async_computation.1 | async-start | bytes 15728640 | tf_op jit(solution)/shard_map/all_to_all | solution.py:580
  79.2 85.3 %planes.1 = (bf16[16,64,1920]{2,1,0:T(8,128)(2,1)}, bf16[2,2,64,1920]{3,2,1,0:T(8,128)(2,1)}, bf16[2,2,64,1920]{3,2,1,0:T(8,128)(2,1)}, bf16[2,64,1920]{2,1,0:T(...) custom-call(s32[1]{0:T(128)} %bitcast.me_ref, ...), custom_call_target="tpu_custom_call" | custom-call | flops 12999999488 | bytes 24000000 | tf_op jit(solution)/shard_map/planes/pallas_call | solution.py:497
  164.5 3.7 %all-to-all-done.1 = bf16[8,256,1920]{2,1,0:T(8,128)(2,1)} async-done(((bf16[8,256,1920]{2,1,0:T(8,128)(2,1)}), bf16[8,256,1920]{2,1,0:T(8,128)(2,1)}, u32[]{:S(2)}, u32[]{:S(2)}) %all-to-all-start.1) | async-done | bytes 7864352 | tf_op jit(solution)/shard_map/all_to_all | solution.py:580
  168.2 12.5 %all-to-all-start.2 = ((bf16[16,64,1920]{2,1,0:T(8,128)(2,1)}), bf16[16,64,1920]{2,1,0:T(8,128)(2,1)}, u32[]{:S(2)}, u32[]{:S(2)}) async-start(bf16[16,64,1920]{2,1,0:T(8,128)(2,1)} %get-tuple-element.52), calls=%async_computation.2 | async-start | bytes 7864320 | tf_op jit(solution)/shard_map/all_to_all | solution.py:587
  180.7 0.1 collective-permute-start.4
  180.8 0.6 collective-permute-start.5
  181.5 0.1 collective-permute-start.6
  181.5 2.9 %collective-permute-start.7 = (bf16[1,2,2,2,16,1920]{5,4,3,2,1,0:T(8,128)(2,1)}, bf16[1,2,2,2,16,1920]{5,4,3,2,1,0:T(8,128)(2,1)S(1)}, u32[]{:S(2)}, u32[]{:S(2)}) collective-permute-start(bf16[1,2,2,2,16,1920]{5,4,3,2,1,0:T(8,128)(2,1)} %bitcast.11), channel_id=1, source_target_pairs={{0,96},{16,112},{32,0},{48,16},{64,32},{80,48},{96,64},{112,80},{1... | collective-permute-start | bytes 1474568 | tf_op jit(solution)/shard_map/ppermute | solution.py:278
  184.5 1.1 collective-permute-start.8
  185.6 5.8 %overlap.1 = f32[16,128]{1,0:T(8,128)} custom-call(s32[1]{0:T(128)} %bitcast.me_ref, bf16[2,2,2,2,16,1920]{5,4,3,2,1,0:T(8,128)(2,1)} %get-tuple-element.37.refs_0_, bf16[2,2,2,2,16,1920]{5,4,3,2,1,0:T(8,128)(2,1)} %copy-done.8, bf16[2,2,2,2,16,1920]{5,4,3,2,1,0:T(8,128)(2,1)} %collective-permute-done.2.refs_2_, ...), custom_call_target="tpu_custom_call" | custom-call | flops 2000000000 | bytes 8000000 | tf_op jit(solution)/shard_map/overlap/pallas_call | solution.py:221
  191.4 0.0 collective-permute-done.4.got_near.got_far
  191.4 1.0 copy-done
  192.4 6.2 %near.1 = f32[16,128]{1,0:T(8,128)} custom-call(s32[1]{0:T(128)} %bitcast.me_ref, bf16[8,4,2,2,16,1920]{5,4,3,2,1,0:T(8,128)(2,1)} %bitcast.6.left_ref.left_far_ref, bf16[8,4,2,2,16,1920]{5,4,3,2,1,0:T(8,128)(2,1)} %bitcast.6.left_ref.left_far_ref, bf16[2,2,2,2,16,1920]{5,4,3,2,1,0:T(8,128)(2,1)} %bitcast.21, bf16[2,2,2,2,16,1920]{5,4,3,2,1,0:T(8,128)(2,1)} %copy-done, ...), custom_call_target="tpu_custom_call" | custom-call | flops 2000000000 | bytes 8000000 | tf_op jit(solution)/shard_map/near/pallas_call | solution.py:221
  198.6 0.0 collective-permute-done.5.before_same
  198.6 0.0 copy-start.2
  198.6 7.4 %collective-permute-done.6.before_other = bf16[1,2,2,2,16,1920]{5,4,3,2,1,0:T(8,128)(2,1)S(1)} collective-permute-done((bf16[1,2,2,2,16,1920]{5,4,3,2,1,0:T(8,128)(2,1)}, bf16[1,2,2,2,16,1920]{5,4,3,2,1,0:T(8,128)(2,1)S(1)}, u32[]{:S(2)}, u32[]{:S(2)}) %collective-permute-start.6) | collective-permute-done | bytes 491552 | tf_op jit(solution)/shard_map/ppermute | solution.py:278
  205.9 0.0 collective-permute-done.7.after_same
  205.9 0.4 collective-permute-done.8.after_other
  206.3 0.4 copy-done.3
  206.7 0.2 copy-done.4
  206.9 0.8 copy-done.5
  207.7 4.8 %next.1 = f32[16,128]{1,0:T(8,128)} custom-call(s32[1]{0:T(128)} %bitcast.me_ref, bf16[8,4,2,2,16,1920]{5,4,3,2,1,0:T(8,128)(2,1)} %bitcast.6.left_ref.left_far_ref, bf16[1,2,2,2,16,1920]{5,4,3,2,1,0:T(8,128)(2,1)} %copy-done.2, bf16[1,2,2,2,16,1920]{5,4,3,2,1,0:T(8,128)(2,1)} %copy-done.3, bf16[1,2,2,2,16,1920]{5,4,3,2,1,0:T(8,128)(2,1)} %copy-done.4, ...), custom_call_target="tpu_custom_call" | custom-call | flops 2000000000 | bytes 8000000 | tf_op jit(solution)/shard_map/next/pallas_call | solution.py:221
  212.5 0.7 add_add_fusion
  213.2 0.7 collective-permute-start.9
  213.9 0.8 collective-permute-done.9
  214.7 0.4 collective-permute-start.10
  215.1 3.2 %collective-permute-done.10 = f32[16,128]{1,0:T(8,128)S(1)} collective-permute-done((f32[16,128]{1,0:T(8,128)S(1)}, f32[16,128]{1,0:T(8,128)S(1)}, u32[]{:S(2)}, u32[]{:S(2)}) %collective-permute-start.10) | collective-permute-done | bytes 8224 | tf_op jit(solution)/shard_map/ppermute | solution.py:270
  218.4 2.2 collective-permute-start.11
  220.6 2.9 %collective-permute-done.11 = f32[16,128]{1,0:T(8,128)S(1)} collective-permute-done((f32[16,128]{1,0:T(8,128)S(1)}, f32[16,128]{1,0:T(8,128)S(1)}, u32[]{:S(2)}, u32[]{:S(2)}) %collective-permute-start.11) | collective-permute-done | bytes 8224 | tf_op jit(solution)/shard_map/ppermute | solution.py:270
  223.5 1.9 collective-permute-start.12
  225.4 2.8 %collective-permute-done.12 = f32[16,128]{1,0:T(8,128)S(1)} collective-permute-done((f32[16,128]{1,0:T(8,128)S(1)}, f32[16,128]{1,0:T(8,128)S(1)}, u32[]{:S(2)}, u32[]{:S(2)}) %collective-permute-start.12) | collective-permute-done | bytes 8224 | tf_op jit(solution)/shard_map/ppermute | solution.py:270
  228.2 6.9 %collective-permute-start.13 = (f32[16,128]{1,0:T(8,128)S(1)}, f32[16,128]{1,0:T(8,128)S(1)}, u32[]{:S(2)}, u32[]{:S(2)}) collective-permute-start(f32[16,128]{1,0:T(8,128)S(1)} %add.120), channel_id=1, source_target_pairs={{0,2},{1,3},{2,0},{3,1},{4,6},{5,7},{6,4},{7,5},{8,10},{9,11},{10,... | collective-permute-start | bytes 24584 | tf_op jit(solution)/shard_map/ppermute | solution.py:270
  235.2 1.6 collective-permute-done.13
  236.8 3.1 %collective-permute-start.14 = (f32[16,128]{1,0:T(8,128)S(1)}, f32[16,128]{1,0:T(8,128)S(1)}, u32[]{:S(2)}, u32[]{:S(2)}) collective-permute-start(f32[16,128]{1,0:T(8,128)S(1)} %add.121), channel_id=1, source_target_pairs={{0,4},{1,5},{2,6},{3,7},{4,0},{5,1},{6,2},{7,3},{8,12},{9,13},{10,... | collective-permute-start | bytes 24584 | tf_op jit(solution)/shard_map/ppermute | solution.py:270
  239.9 0.0 all-to-all-done.2
  239.9 5.3 %z_backward.1 = bf16[2,480,1920]{2,1,0:T(8,128)(2,1)} custom-call(bf16[16,2,2,16,1920]{4,3,2,1,0:T(8,128)(2,1)} %bitcast.13.wire_ref, f32[1,1920]{1,0:T(1,128)} %reshape.67.live_ref, bf16[480,512]{1,0:T(8,128)(2,1)} %constant.129.clone.table_ref), custom_call_target="tpu_custom_call" | custom-call | flops 1800000000 | bytes 8000000 | tf_op jit(solution)/shard_map/z_backward/pallas_call | solution.py:108
  245.1 0.0 collective-permute-done.14
  245.2 0.1 collective-permute-start.15
  245.2 5.1 %collective-permute-done.15 = f32[16,128]{1,0:T(8,128)S(1)} collective-permute-done((f32[16,128]{1,0:T(8,128)S(1)}, f32[16,128]{1,0:T(8,128)S(1)}, u32[]{:S(2)}, u32[]{:S(2)}) %collective-permute-start.15) | collective-permute-done | bytes 8224 | tf_op jit(solution)/shard_map/ppermute | solution.py:270
  250.4 0.1 reshape.66
  250.5 0.6 fusion.4
  (24 shorter events, 0.1 us)
Async XLA Ops:
  9.0 11.0 %collective-permute-start = (bf16[4,2,2,2,16,1920]{5,4,3,2,1,0:T(8,128)(2,1)}, bf16[4,2,2,2,16,1920]{5,4,3,2,1,0:T(8,128)(2,1)S(1)}, u32[]{:S(2)}, u32[]{:S(2)}) collective-permute-start(bf16[4,2,2,2,16,1920]{5,4,3,2,1,0:T(8,128)(2,1)} %get-tuple-element.31), channel_id=1, source_target_pairs={{0,16},{16,0},{32,48},{48,32},{64,80},{80,64},{96,112},{112,96},{1... | collective-permute-start | bytes 5898248 | tf_op jit(solution)/shard_map/ppermute | solution.py:278
  9.0 8.4 %copy-start.1 = (s32[30720]{0:T(1024)S(1)}, s32[30720]{0:T(1024)}, u32[]{:S(2)}) copy-start(s32[30720]{0:T(1024)} %param.10) | copy-start | bytes 368644
  9.0 61.0 %all-to-all-start = ((bf16[16,64,1920]{2,1,0:T(8,128)(2,1)}), bf16[16,64,1920]{2,1,0:T(8,128)(2,1)}, u32[]{:S(2)}, u32[]{:S(2)}) async-start(bf16[16,64,1920]{2,1,0:T(8,128)(2,1)} %bitcast.20), calls=%async_computation | async-start | bytes 7864320 | tf_op jit(solution)/shard_map/all_to_all | solution.py:574
  21.5 25.1 %collective-permute-start.1 = (bf16[2,2,2,2,16,1920]{5,4,3,2,1,0:T(8,128)(2,1)S(1)}, bf16[2,2,2,2,16,1920]{5,4,3,2,1,0:T(8,128)(2,1)S(1)}, u32[]{:S(2)}, u32[]{:S(2)}) collective-permute-start(bf16[2,2,2,2,16,1920]{5,4,3,2,1,0:T(8,128)(2,1)S(1)} %get-tuple-element.34), channel_id=1, source_target_pairs={{0,32},{16,48},{32,64},{48,80},{64,96},{80,112},{96,0},{112,16},{1... | collective-permute-start | bytes 2949128 | tf_op jit(solution)/shard_map/ppermute | solution.py:278
  23.0 45.7 %collective-permute-start.2 = (bf16[2,2,2,2,16,1920]{5,4,3,2,1,0:T(8,128)(2,1)S(1)}, bf16[2,2,2,2,16,1920]{5,4,3,2,1,0:T(8,128)(2,1)}, u32[]{:S(2)}, u32[]{:S(2)}) collective-permute-start(bf16[2,2,2,2,16,1920]{5,4,3,2,1,0:T(8,128)(2,1)S(1)} %get-tuple-element.35), channel_id=1, source_target_pairs={{0,64},{16,80},{32,96},{48,112},{64,0},{80,16},{96,32},{112,48},{1... | collective-permute-start | bytes 2949128 | tf_op jit(solution)/shard_map/ppermute | solution.py:278
  25.7 43.0 %collective-permute-start.3 = (bf16[2,2,2,2,16,1920]{5,4,3,2,1,0:T(8,128)(2,1)S(1)}, bf16[2,2,2,2,16,1920]{5,4,3,2,1,0:T(8,128)(2,1)}, u32[]{:S(2)}, u32[]{:S(2)}) collective-permute-start(bf16[2,2,2,2,16,1920]{5,4,3,2,1,0:T(8,128)(2,1)S(1)} %get-tuple-element.36), channel_id=1, source_target_pairs={{0,96},{16,112},{32,0},{48,16},{64,32},{80,48},{96,64},{112,80},{1... | collective-permute-start | bytes 2949128 | tf_op jit(solution)/shard_map/ppermute | solution.py:278
  46.6 27.7 %copy-start.8 = (bf16[2,2,2,2,16,1920]{5,4,3,2,1,0:T(8,128)(2,1)}, bf16[2,2,2,2,16,1920]{5,4,3,2,1,0:T(8,128)(2,1)S(1)}, u32[]{:S(2)}) copy-start(bf16[2,2,2,2,16,1920]{5,4,3,2,1,0:T(8,128)(2,1)S(1)} %collective-permute-done.1.refs_1_) | copy-start | bytes 2949124
  74.3 93.9 %all-to-all-start.1 = ((bf16[8,256,1920]{2,1,0:T(8,128)(2,1)}), bf16[8,256,1920]{2,1,0:T(8,128)(2,1)}, u32[]{:S(2)}, u32[]{:S(2)}) async-start(bf16[8,256,1920]{2,1,0:T(8,128)(2,1)} %bitcast.19), calls=%async_computation.1 | async-start | bytes 15728640 | tf_op jit(solution)/shard_map/all_to_all | solution.py:580
  168.2 12.5 %copy-start.9 = (bf16[2,2,64,1920]{3,2,1,0:T(8,128)(2,1)S(1)}, bf16[2,2,64,1920]{3,2,1,0:T(8,128)(2,1)}, u32[]{:S(2)}) copy-start(bf16[2,2,64,1920]{3,2,1,0:T(8,128)(2,1)} %get-tuple-element.47) | copy-start | bytes 2949124
  168.2 71.7 %all-to-all-start.2 = ((bf16[16,64,1920]{2,1,0:T(8,128)(2,1)}), bf16[16,64,1920]{2,1,0:T(8,128)(2,1)}, u32[]{:S(2)}, u32[]{:S(2)}) async-start(bf16[16,64,1920]{2,1,0:T(8,128)(2,1)} %get-tuple-element.52), calls=%async_computation.2 | async-start | bytes 7864320 | tf_op jit(solution)/shard_map/all_to_all | solution.py:587
  180.7 10.7 %collective-permute-start.4 = (bf16[2,2,2,2,16,1920]{5,4,3,2,1,0:T(8,128)(2,1)S(1)}, bf16[2,2,2,2,16,1920]{5,4,3,2,1,0:T(8,128)(2,1)S(1)}, u32[]{:S(2)}, u32[]{:S(2)}) collective-permute-start(bf16[2,2,2,2,16,1920]{5,4,3,2,1,0:T(8,128)(2,1)S(1)} %bitcast.26), channel_id=1, source_target_pairs={{0,16},{16,0},{32,48},{48,32},{64,80},{80,64},{96,112},{112,96},{1... | collective-permute-start | bytes 2949128 | tf_op jit(solution)/shard_map/ppermute | solution.py:278
  180.8 17.7 %collective-permute-start.5 = (bf16[1,2,2,2,16,1920]{5,4,3,2,1,0:T(8,128)(2,1)}, bf16[1,2,2,2,16,1920]{5,4,3,2,1,0:T(8,128)(2,1)S(1)}, u32[]{:S(2)}, u32[]{:S(2)}) collective-permute-start(bf16[1,2,2,2,16,1920]{5,4,3,2,1,0:T(8,128)(2,1)} %bitcast.9), channel_id=1, source_target_pairs={{0,32},{16,48},{32,64},{48,80},{64,96},{80,112},{96,0},{112,16},{1... | collective-permute-start | bytes 1474568 | tf_op jit(solution)/shard_map/ppermute | solution.py:278
  181.5 24.5 %collective-permute-start.6 = (bf16[1,2,2,2,16,1920]{5,4,3,2,1,0:T(8,128)(2,1)}, bf16[1,2,2,2,16,1920]{5,4,3,2,1,0:T(8,128)(2,1)S(1)}, u32[]{:S(2)}, u32[]{:S(2)}) collective-permute-start(bf16[1,2,2,2,16,1920]{5,4,3,2,1,0:T(8,128)(2,1)} %bitcast.10), channel_id=1, source_target_pairs={{0,48},{16,32},{32,80},{48,64},{64,112},{80,96},{96,16},{112,0},{1... | collective-permute-start | bytes 1474568 | tf_op jit(solution)/shard_map/ppermute | solution.py:278
  181.5 24.4 %collective-permute-start.7 = (bf16[1,2,2,2,16,1920]{5,4,3,2,1,0:T(8,128)(2,1)}, bf16[1,2,2,2,16,1920]{5,4,3,2,1,0:T(8,128)(2,1)S(1)}, u32[]{:S(2)}, u32[]{:S(2)}) collective-permute-start(bf16[1,2,2,2,16,1920]{5,4,3,2,1,0:T(8,128)(2,1)} %bitcast.11), channel_id=1, source_target_pairs={{0,96},{16,112},{32,0},{48,16},{64,32},{80,48},{96,64},{112,80},{1... | collective-permute-start | bytes 1474568 | tf_op jit(solution)/shard_map/ppermute | solution.py:278
  184.5 21.8 %collective-permute-start.8 = (bf16[1,2,2,2,16,1920]{5,4,3,2,1,0:T(8,128)(2,1)}, bf16[1,2,2,2,16,1920]{5,4,3,2,1,0:T(8,128)(2,1)S(1)}, u32[]{:S(2)}, u32[]{:S(2)}) collective-permute-start(bf16[1,2,2,2,16,1920]{5,4,3,2,1,0:T(8,128)(2,1)} %bitcast.27), channel_id=1, source_target_pairs={{0,112},{16,96},{32,16},{48,0},{64,48},{80,32},{96,80},{112,64},{1... | collective-permute-start | bytes 1474568 | tf_op jit(solution)/shard_map/ppermute | solution.py:278
  191.4 1.0 copy-start
  198.5 13.9 %copy-start.6 = (f32[16,128]{1,0:T(8,128)S(1)}, f32[16,128]{1,0:T(8,128)}, u32[]{:S(2)}) copy-start(f32[16,128]{1,0:T(8,128)} %near.1) | copy-start | bytes 24580
  198.5 13.9 %copy-start.7 = (f32[16,128]{1,0:T(8,128)S(1)}, f32[16,128]{1,0:T(8,128)}, u32[]{:S(2)}) copy-start(f32[16,128]{1,0:T(8,128)} %overlap.1) | copy-start | bytes 24580
  198.6 7.7 %copy-start.2 = (bf16[1,2,2,2,16,1920]{5,4,3,2,1,0:T(8,128)(2,1)}, bf16[1,2,2,2,16,1920]{5,4,3,2,1,0:T(8,128)(2,1)S(1)}, u32[]{:S(2)}) copy-start(bf16[1,2,2,2,16,1920]{5,4,3,2,1,0:T(8,128)(2,1)S(1)} %collective-permute-done.5.before_same) | copy-start | bytes 1474564
  205.9 0.8 copy-start.3
  205.9 0.9 copy-start.4
  206.9 0.8 copy-start.5
  213.2 1.5 collective-permute-start.9
  214.7 3.7 %collective-permute-start.10 = (f32[16,128]{1,0:T(8,128)S(1)}, f32[16,128]{1,0:T(8,128)S(1)}, u32[]{:S(2)}, u32[]{:S(2)}) collective-permute-start(f32[16,128]{1,0:T(8,128)S(1)} %add.117), channel_id=1, source_target_pairs={{0,32},{16,48},{32,0},{48,16},{64,96},{80,112},{96,64},{112,80},{1... | collective-permute-start | bytes 24584 | tf_op jit(solution)/shard_map/ppermute | solution.py:270
  218.4 5.2 %collective-permute-start.11 = (f32[16,128]{1,0:T(8,128)S(1)}, f32[16,128]{1,0:T(8,128)S(1)}, u32[]{:S(2)}, u32[]{:S(2)}) collective-permute-start(f32[16,128]{1,0:T(8,128)S(1)} %add.118), channel_id=1, source_target_pairs={{0,64},{16,80},{32,96},{48,112},{64,0},{80,16},{96,32},{112,48},{1... | collective-permute-start | bytes 24584 | tf_op jit(solution)/shard_map/ppermute | solution.py:270
  223.5 4.7 %collective-permute-start.12 = (f32[16,128]{1,0:T(8,128)S(1)}, f32[16,128]{1,0:T(8,128)S(1)}, u32[]{:S(2)}, u32[]{:S(2)}) collective-permute-start(f32[16,128]{1,0:T(8,128)S(1)} %add.119), channel_id=1, source_target_pairs={{0,1},{1,0},{2,3},{3,2},{4,5},{5,4},{6,7},{7,6},{8,9},{9,8},{10,11... | collective-permute-start | bytes 24584 | tf_op jit(solution)/shard_map/ppermute | solution.py:270
  228.2 8.6 %collective-permute-start.13 = (f32[16,128]{1,0:T(8,128)S(1)}, f32[16,128]{1,0:T(8,128)S(1)}, u32[]{:S(2)}, u32[]{:S(2)}) collective-permute-start(f32[16,128]{1,0:T(8,128)S(1)} %add.120), channel_id=1, source_target_pairs={{0,2},{1,3},{2,0},{3,1},{4,6},{5,7},{6,4},{7,5},{8,10},{9,11},{10,... | collective-permute-start | bytes 24584 | tf_op jit(solution)/shard_map/ppermute | solution.py:270
  236.8 8.4 %collective-permute-start.14 = (f32[16,128]{1,0:T(8,128)S(1)}, f32[16,128]{1,0:T(8,128)S(1)}, u32[]{:S(2)}, u32[]{:S(2)}) collective-permute-start(f32[16,128]{1,0:T(8,128)S(1)} %add.121), channel_id=1, source_target_pairs={{0,4},{1,5},{2,6},{3,7},{4,0},{5,1},{6,2},{7,3},{8,12},{9,13},{10,... | collective-permute-start | bytes 24584 | tf_op jit(solution)/shard_map/ppermute | solution.py:270
  245.2 5.2 %collective-permute-start.15 = (f32[16,128]{1,0:T(8,128)S(1)}, f32[16,128]{1,0:T(8,128)S(1)}, u32[]{:S(2)}, u32[]{:S(2)}) collective-permute-start(f32[16,128]{1,0:T(8,128)S(1)} %add.122), channel_id=1, source_target_pairs={{0,8},{1,9},{2,10},{3,11},{4,12},{5,13},{6,14},{7,15},{8,0},{9,1},... | collective-permute-start | bytes 24584 | tf_op jit(solution)/shard_map/ppermute | solution.py:270
